TPU v7x, 256 devices: a whole 4x4x8 slice. The times are simulated.
256 devices in a mesh: vert: 64 (over y, x, z_lo), af: 4 (over z_hi, core).
Axes of the slice: x: 4, y: 4, z: 8 (z_hi: 2, z_lo: 4; z = z_hi * 4 + z_lo), core: 2. Of those that a mesh axis runs over, the one named last changes fastest.
Arguments:
- features: bfloat16 [256, 262144], P('af', 'vert'), may hold values from -6 to 6
- cotangent: bfloat16 [256, 262144], P('af', 'vert'), may hold values from -6 to 6
- w_self: bfloat16 [256, 256], replicated, may hold values from -0.25 to 0.25
- w_neigh: bfloat16 [256, 256], replicated, may hold values from -0.25 to 0.25
- send_index: int32 [64, 64, 64], P('vert'), may hold values from 128 to 4095
- send_count: int32 [64, 64], P('vert'), may hold values from 0 to 64
- tile_index: int32 [2048, 8], P('vert'), may hold values from 0 to 127
- tile_count: int32 [2048], P('vert'), may hold values from 1 to 8
- tile_weight: bfloat16 [2048, 8, 128, 128], P('vert'), may hold values from -0.25 to 0.25
Outputs:
- output: bfloat16 [256, 262144], P('af', 'vert')
- grad_x: float32 [256, 262144], P('af', 'vert')
- grad_w_self: float32 [256, 256], P('af')
- grad_w_neigh: float32 [256, 256], P('af')
Inputs may be any that keep to these rules, and one draw needn't show every extreme that they name: `tile_index`: tile numbers into an owner's source columns: its own vertices, then incoming boundary rows in sender order, then all hubs in owner order. `send_index`: boundary rows are never hubs.
All inputs are finite; a program needn't handle non-finite values.
Results may differ from a plain program's by a relative error of at most 0.0054.
Values may be sent and summed in bfloat16 or wider, within the bound.
No kernel may reach another device: no remote copies, remote signals or barrier semaphores. Data moves between devices by JAX's collectives and lax.ppermute only.
A program may use at most 128 MiB of HBM per device.

v0:
```python
import math

import jax
import jax.numpy as jnp
from jax import lax
from jax.sharding import PartitionSpec as P

HUB_DEV = 128


def silu_slope(pre_value):
    sig = jax.nn.sigmoid(pre_value)
    return sig * (1.0 + pre_value * (1.0 - sig))


def local(
    features,
    cotangent,
    w_self,
    w_neigh,
    send_index,
    send_count,
    tile_index,
    tile_count,
    tile_weight,
):
    row_count, local_nodes = features.shape
    width = tile_weight.shape[-1]
    peer_count = lax.axis_size("vert")
    slot_count = send_index.shape[2]
    first_feat = lax.axis_index("af") * row_count
    hub_rows = lax.all_gather(features[:, :HUB_DEV], "vert", axis=1, tiled=True)
    flat_index = send_index.reshape(peer_count * slot_count)
    slot_live = lax.broadcasted_iota(jnp.int32, (peer_count, slot_count), 1) < send_count.reshape(
        peer_count, 1
    )
    live_flat = slot_live.reshape(peer_count * slot_count)
    outgoing = jnp.take(features, flat_index, axis=1) * live_flat.astype(jnp.bfloat16)[None, :]
    incoming = lax.all_to_all(outgoing, "vert", split_axis=1, concat_axis=1, tiled=True)
    source = jnp.concatenate([features, incoming, hub_rows], axis=1)
    src_count = source.shape[1] // width
    tile_live = lax.broadcasted_iota(jnp.int32, tile_index.shape, 1) < tile_count[:, None]
    picked = jnp.take(source.reshape(row_count, src_count, width), tile_index, axis=1)
    picked = picked * tile_live.astype(jnp.bfloat16)[None, :, :, None]
    aggregate = jnp.einsum(
        "fjsa,jsab->fjb", picked, tile_weight, preferred_element_type=jnp.float32
    )
    aggregate = aggregate.reshape(row_count, local_nodes).astype(jnp.bfloat16)
    self_rows = lax.dynamic_slice_in_dim(w_self, first_feat, row_count, 0)
    neigh_rows = lax.dynamic_slice_in_dim(w_neigh, first_feat, row_count, 0)
    contract_first = (((0,), (0,)), ((), ()))
    self_part = self_rows
    neigh_part = neigh_rows
    pre_value = lax.psum_scatter(
        lax.dot_general(self_part, features, contract_first, preferred_element_type=jnp.float32)
        + lax.dot_general(
            neigh_part, aggregate, contract_first, preferred_element_type=jnp.float32
        ),
        "af",
        scatter_dimension=0,
        tiled=True,
    )
    output = jax.nn.silu(pre_value).astype(jnp.bfloat16)
    grad_pre = (cotangent.astype(jnp.float32) * silu_slope(pre_value)).astype(jnp.bfloat16)
    contract_last = (((1,), (1,)), ((), ()))
    block_rows = lax.all_gather(grad_pre, "af", axis=0, tiled=True)
    self_part = self_rows
    neigh_part = neigh_rows
    grad_direct = jnp.dot(self_part, block_rows, preferred_element_type=jnp.float32)
    grad_neigh_sum = jnp.dot(neigh_part, block_rows, preferred_element_type=jnp.float32)
    self_piece = lax.dot_general(
        features, block_rows, contract_last, preferred_element_type=jnp.float32
    )
    neigh_piece = lax.dot_general(
        aggregate, block_rows, contract_last, preferred_element_type=jnp.float32
    )
    grad_self_w = self_piece
    grad_neigh_w = neigh_piece
    grad_direct, grad_neigh_sum, grad_self_w, grad_neigh_w = (
        grad_direct,
        grad_neigh_sum,
        grad_self_w,
        grad_neigh_w,
    )
    summed_self, summed_neigh = lax.psum((grad_self_w, grad_neigh_w), "vert")
    scale = 1.0 / math.sqrt(local_nodes * peer_count)
    grad_w_self = summed_self * scale
    grad_w_neigh = summed_neigh * scale
    grad_agg = grad_neigh_sum.astype(jnp.bfloat16).reshape(row_count, tile_index.shape[0], width)
    part_grad = jnp.einsum(
        "fjb,jsab->fjsa", grad_agg, tile_weight, preferred_element_type=jnp.float32
    )
    part_grad = part_grad * tile_live.astype(jnp.float32)[None, :, :, None]
    grad_source = jnp.zeros((row_count, src_count, width), jnp.float32)
    grad_source = grad_source.at[:, tile_index.reshape(-1)].add(
        part_grad.reshape(row_count, -1, width)
    )
    grad_source = grad_source.reshape(row_count, src_count * width)
    edge = local_nodes + peer_count * slot_count
    returned = lax.all_to_all(
        grad_source[:, local_nodes:edge].astype(jnp.bfloat16),
        "vert",
        split_axis=1,
        concat_axis=1,
        tiled=True,
    ).astype(jnp.float32)
    hub_total = lax.psum_scatter(grad_source[:, edge:], "vert", scatter_dimension=1, tiled=True)
    grad_x = grad_direct + grad_source[:, :local_nodes]
    grad_x = grad_x.at[:, flat_index].add(returned * live_flat.astype(jnp.float32)[None, :])
    grad_x = grad_x.at[:, :HUB_DEV].add(hub_total)
    return (output, grad_x, grad_w_self, grad_w_neigh)


def solution(mesh):
    in_specs = (
        P("af", "vert"),
        P("af", "vert"),
        P(),
        P(),
        P("vert", None, None),
        P("vert", None),
        P("vert", None),
        P("vert"),
        P("vert", None, None, None),
    )
    out_specs = (P("af", "vert"), P("af", "vert"), P("af", None), P("af", None))
    return jax.shard_map(local, mesh=mesh, in_specs=in_specs, out_specs=out_specs, check_vma=False)
```

profile of v0, /device:TPU:0, one launch (start us, length us, event | category | flops | bytes accessed | tf_op | source)
XLA Modules:
  0.0 1438.5 jit_solution(12996689519781102152)
XLA Ops:
  11.1 12.1 gather_fusion
  26.2 10.3 all-to-all-start
  36.9 2.7 fusion.28
  39.6 16.4 %all-to-all-done = bf16[64,2,2048]{2,1,0:T(2,128)(2,1)S(1)} async-done(((bf16[64,2,2048]{2,1,0:T(2,128)(2,1)}), bf16[64,2,2048]{2,1,0:T(2,128)(2,1)S(1)}, u32[]{:S(2)}, u32[]{:S(2)}) %all-to-all-start) | async-done | bytes 524320 | tf_op jit(solution)/shard_map/all_to_all | solution.py:39
  57.0 224.6 %all-gather.3.cloned.1.call-done = bf16[64,8192]{1,0:T(8,128)(2,1)} async-done(((bf16[64,128]{1,0:T(8,128)(2,1)}), bf16[64,8192]{1,0:T(8,128)(2,1)}) %all-gather.3.cloned.1.call-update) | async-done | bytes 1048592 | tf_op jit(solution)/shard_map/all_gather | solution.py:32
  283.4 3.1 gather_fusion.1
  286.5 6.6 fusion.14
  293.9 2.7 convolution_add_fusion
  296.7 80.2 %reduce-scatter.3.cloned.1.call-done = f32[64,4096]{1,0:T(8,128)} async-done(((f32[256,4096]{1,0:T(8,128)}), f32[64,4096]{1,0:T(8,128)}) %reduce-scatter.3.cloned.1.call-update) | async-done | bytes 1048592 | tf_op jit(solution)/shard_map/reduce_scatter | solution.py:54
  376.9 2.6 multiply_convert_fusion
  379.7 39.3 %all-gather.5.cloned.1.call-done = bf16[256,4096]{1,0:T(8,128)(2,1)} async-done(((bf16[64,4096]{1,0:T(8,128)(2,1)}), bf16[256,4096]{1,0:T(8,128)(2,1)}) %all-gather.5.cloned.1.call-update) | async-done | bytes 2097168 | tf_op jit(solution)/shard_map/all_gather | solution.py:66
  419.0 2.2 fusion.13
  421.3 3.2 fusion.17
  426.1 9.6 broadcast_multiply_fusion
  435.8 2.5 broadcast_in_dim.37
  438.3 39.5 %scatter_fusion = f32[64,128,128]{2,0,1:T(8,128)} fusion(f32[64,128,128]{2,0,1:T(8,128)} %broadcast_in_dim.37, s32[256]{0:T(256)S(1)} %bitcast.84, f32[256,64,128]{2,1,0:T(8,128)} %bitcast.75), kind=kCustom, calls=%fused_computation.2 | custom fusion | flops 2097152 | bytes 25166848 | tf_op jit(solution)/shard_map/scatter-add | solution.py:95
  477.8 2.5 copy_bitcast_fusion
  489.5 3.0 reshape.244
  492.5 8.0 all-to-all-start.1
  503.5 550.7 %all-reduce.3.cloned.1.call-done = (f32[64,256]{1,0:T(8,128)}, f32[64,256]{1,0:T(8,128)}) async-done(((f32[64,256]{1,0:T(8,128)}, f32[64,256]{1,0:T(8,128)}), (f32[64,256]{1,0:T(8,128)}, f32[64,256]{1,0:T(8,128)})) %all-reduce.3.cloned.1.call-update) | async-done | bytes 131088 | tf_op jit(solution)/shard_map/psum | solution.py:85
  1057.1 2.3 reshape.245
  1064.6 3.2 copy.77
  1067.8 23.4 %scatter_fusion.1 = f32[64,4096]{0,1:T(8,128)S(1)} fusion(f32[64,4096]{0,1:T(8,128)S(1)} %copy.76, s32[4096]{0:T(1024)S(1)} %bitcast.83, f32[4096,64]{1,0:T(8,128)} %copy.77), kind=kCustom, calls=%fused_computation.3 | custom fusion | flops 262144 | bytes 3162112 | tf_op jit(solution)/shard_map/scatter-add | solution.py:109
  1091.3 337.7 %reduce-scatter.5.cloned.1.call-done = f32[64,128]{1,0:T(8,128)} async-done(((f32[64,8192]{1,0:T(8,128)}), f32[64,128]{1,0:T(8,128)}) %reduce-scatter.5.cloned.1.call-update) | async-done | bytes 32784 | tf_op jit(solution)/shard_map/reduce_scatter | solution.py:107
  (79 shorter events, 36.3 us)
Async XLA Ops:
  7.2 286.8 %copy-start = (bf16[256,256]{1,0:T(8,128)(2,1)S(1)}, bf16[256,256]{1,0:T(8,128)(2,1)}, u32[]{:S(2)}) copy-start(bf16[256,256]{1,0:T(8,128)(2,1)} %param.14) | copy-start | bytes 393220
  7.2 16.0 %copy-start.8 = (s32[1,64,64]{2,1,0:T(8,128)S(1)}, s32[1,64,64]{2,1,0:T(8,128)}, u32[]{:S(2)}) copy-start(s32[1,64,64]{2,1,0:T(8,128)} %param.15) | copy-start | bytes 49156
  7.2 16.0 %copy-start.11 = (s32[1,64]{1,0:T(1,128)S(1)}, s32[1,64]{1,0:T(1,128)}, u32[]{:S(2)}) copy-start(s32[1,64]{1,0:T(1,128)} %param.16) | copy-start | bytes 772
  7.2 274.4 %all-gather.3.cloned.1.call-start = ((), (), s32[]{:S(2)}) async-start(), calls=%async_computation.4 | async-start | bytes 1064960 | tf_op jit(solution)/shard_map/all_gather | solution.py:32
  11.0 25.5 %copy-start.9 = (s32[32,8]{0,1:T(8,128)S(1)}, s32[32,8]{0,1:T(8,128)}, u32[]{:S(2)}) copy-start(s32[32,8]{0,1:T(8,128)} %param.17) | copy-start | bytes 3076
  11.0 25.8 %copy-start.12 = (s32[32]{0:T(128)S(1)}, s32[32]{0:T(128)}, u32[]{:S(2)}) copy-start(s32[32]{0:T(128)} %param.18) | copy-start | bytes 388
  11.0 25.9 %copy-start.5 = (bf16[64,4096]{1,0:T(8,128)(2,1)S(1)}, bf16[64,4096]{1,0:T(8,128)(2,1)}, u32[]{:S(2)}) copy-start(bf16[64,4096]{1,0:T(8,128)(2,1)} %param.11) | copy-start | bytes 1572868
  11.0 25.9 %copy-start.10 = (bf16[256,256]{1,0:T(8,128)(2,1)S(1)}, bf16[256,256]{1,0:T(8,128)(2,1)}, u32[]{:S(2)}) copy-start(bf16[256,256]{1,0:T(8,128)(2,1)} %param.13) | copy-start | bytes 393220
  26.2 29.8 %all-to-all-start = ((bf16[64,2,2048]{2,1,0:T(2,128)(2,1)}), bf16[64,2,2048]{2,1,0:T(2,128)(2,1)S(1)}, u32[]{:S(2)}, u32[]{:S(2)}) async-start(bf16[64,2,2048]{2,1,0:T(2,128)(2,1)} %reshape.242), calls=%async_computation | async-start | bytes 1048576 | tf_op jit(solution)/shard_map/all_to_all | solution.py:39
  36.5 340.4 %reduce-scatter.3.cloned.1.call-start = ((), (), s32[]{:S(2)}) async-start(), calls=%async_computation.5 | async-start | bytes 5242880 | tf_op jit(solution)/shard_map/reduce_scatter | solution.py:54
  286.5 7.4 copy-start.3
  293.1 0.8 copy-start.6
  296.6 80.3 %copy-start.7 = (bf16[64,4096]{1,0:T(8,128)(2,1)S(1)}, bf16[64,4096]{1,0:T(8,128)(2,1)}, u32[]{:S(2)}) copy-start(bf16[64,4096]{1,0:T(8,128)(2,1)} %param.12) | copy-start | bytes 1572868
  296.6 122.4 %all-gather.5.cloned.1.call-start = ((), (), s32[]{:S(2)}) async-start(), calls=%async_computation.6 | async-start | bytes 2621440 | tf_op jit(solution)/shard_map/all_gather | solution.py:66
  379.5 674.7 %all-reduce.3.cloned.1.call-start = ((), (), s32[]{:S(2)}) async-start(), calls=%async_computation.8 | async-start | bytes 262144 | tf_op jit(solution)/shard_map/psum | solution.py:85
  419.0 5.5 copy-start.2
  425.9 1003.1 %reduce-scatter.5.cloned.1.call-start = ((), (), s32[]{:S(2)}) async-start(), calls=%async_computation.7 | async-start | bytes 2129920 | tf_op jit(solution)/shard_map/reduce_scatter | solution.py:107
  480.2 2.0 copy-start.4
  492.5 564.6 %all-to-all-start.1 = ((bf16[64,2,2048]{2,1,0:T(2,128)(2,1)}), bf16[64,2,2048]{2,1,0:T(2,128)(2,1)}, u32[]{:S(2)}, u32[]{:S(2)}) async-start(bf16[64,2,2048]{2,1,0:T(2,128)(2,1)} %reshape.244), calls=%async_computation.2 | async-start | bytes 1048576 | tf_op jit(solution)/shard_map/all_to_all | solution.py:100
  1067.8 364.2 %copy-start.1 = (bf16[256,256]{1,0:T(8,128)(2,1)S(1)}, bf16[256,256]{1,0:T(8,128)(2,1)}, u32[]{:S(2)}) copy-start(bf16[256,256]{1,0:T(8,128)(2,1)} %param.14) | copy-start | bytes 393220
Sparse Core Ops, SparseCore 0:
  10.3 271.2 all-gather.2
  296.8 80.0 reduce-scatter.2
  379.6 39.3 all-gather.4
  426.0 628.1 all-reduce.2
  1056.5 372.3 reduce-scatter.4
where the time goes:
time: 1440 us
  waiting for transfers between devices  1250 us (87%)
  other arithmetic  74.9 us (5%)
  local copies, waits for them, and re-layouts  52 us (4%)
  matrix products  30.1 us (2%)
  starting transfers between devices  18.6 us (1%)
    psum x1, waiting for transfers between devices, local(): summed_self, summed_neigh = lax.psum((grad_self_w, grad_neigh_w), 'vert')  551 us
    reduce_scatter x1, waiting for transfers between devices, local(): lax.psum_scatter(grad_source[:, edge:], 'vert', scatter_dimension=1, tile...  338 us
    all_gather x1, waiting for transfers between devices, local(): hub_rows = lax.all_gather(features[:, :HUB_DEV], 'vert', axis=1, tiled=True)  225 us
    reduce_scatter x1, waiting for transfers between devices, local(): lax.psum_scatter(lax.dot_general(self_part, features, contract_first, pre...  80.2 us
    scatter-add x1, other arithmetic, local(): grad_source.at[:, tile_index.reshape(-1)]  39.5 us
    all_gather x1, waiting for transfers between devices, local(): block_rows = lax.all_gather(grad_pre, 'af', axis=0, tiled=True)  39.3 us
  transfers between devices with their start and end apart: 7, of which 6 were waited for; matrix products, arithmetic and copies ran while one was open for 9% of the time, Pallas kernels for 0%

commit v1 on v0

v1 whole, which is shorter than its diff:
```python
import functools
import math

import jax
import jax.numpy as jnp
from jax import lax
from jax.experimental import pallas as pl
from jax.experimental.pallas import tpu as pltpu
from jax.sharding import PartitionSpec as P

T = 128
BF = jnp.bfloat16
F32 = jnp.float32
FIRST = (((0,), (0,)), ((), ()))
LAST = (((1,), (1,)), ((), ()))


def params(mib):
    return pltpu.CompilerParams(vmem_limit_bytes=mib * 2**20)


def low_lanes(rows):
    return lax.broadcasted_iota(jnp.int32, (rows, T), 1) < T // 2


def swap_halves(x):
    return pltpu.roll(x, T // 2, 1)


def onehot(index_row, base, nodes):
    row = lax.broadcasted_iota(jnp.int32, (nodes, index_row.shape[1]), 0)
    return jnp.where(row == index_row - base, F32(1), F32(0)).astype(BF)


def pick_kernel(feat_ref, index_ref, out_ref, *, chunk):
    rows, nodes = feat_ref.shape
    half = rows // 2
    hubs = feat_ref[:, :T]
    low = low_lanes(half)

    def body(t, carry):
        cols = pl.ds(pl.multiple_of(t * 2 * T, 2 * T), 2 * T)
        index_row = index_ref[:, cols]
        acc = jnp.zeros((rows, 2 * T), F32)
        for c in range(nodes // chunk):
            acc += jnp.dot(
                feat_ref[:, c * chunk : (c + 1) * chunk],
                onehot(index_row, c * chunk, chunk),
                preferred_element_type=F32,
            )
        for u in range(2):
            top = acc[:half, u * T : (u + 1) * T]
            bottom = acc[half:, u * T : (u + 1) * T]
            q = t * 4 + u * 2
            out_ref[q, :rows] = hubs
            out_ref[q + 1, :rows] = hubs
            out_ref[q, rows:] = jnp.where(low, top, swap_halves(bottom)).astype(BF)
            out_ref[q + 1, rows:] = jnp.where(low, swap_halves(top), bottom).astype(BF)
        return carry

    lax.fori_loop(0, index_ref.shape[1] // (2 * T), body, 0)


def forward_kernel(place_ref, feat_ref, recv_ref, weight_ref, out_ref, source):
    step = pl.program_id(0)
    rows, nodes = feat_ref.shape
    half = rows // 2
    peers = recv_ref.shape[0]
    own = nodes // T
    blocks = weight_ref.shape[0]
    slots = weight_ref.shape[1] // T

    @pl.when(step == 0)
    def _():
        low = low_lanes(half)
        for i in range(own):
            source[i] = feat_ref[:, i * T : (i + 1) * T]

        def pair(t, carry):
            a = recv_ref[2 * t, rows:].astype(F32)
            b = recv_ref[2 * t + 1, rows:].astype(F32)
            source[own + t, :half] = jnp.where(low, a, swap_halves(b)).astype(BF)
            source[own + t, half:] = jnp.where(low, swap_halves(a), b).astype(BF)
            source[own + peers // 2 + 2 * t] = recv_ref[2 * t, :rows]
            source[own + peers // 2 + 2 * t + 1] = recv_ref[2 * t + 1, :rows]
            return carry

        lax.fori_loop(0, peers // 2, pair, 0)
        source[own + peers // 2 + peers] = jnp.zeros((rows, T), BF)

    for j in range(blocks):
        at = (step * blocks + j) * slots
        picked = jnp.concatenate([source[place_ref[at + s]] for s in range(slots)], axis=1)
        total = jnp.dot(picked, weight_ref[j], preferred_element_type=F32)
        out_ref[0, :, j * T : (j + 1) * T] = total.astype(BF)


def dense_kernel(agg_ref, fc_ref, ws_ref, wn_ref, ga_ref, rest_ref, gw_ref):
    parts, rows, _ = agg_ref.shape
    agg = jnp.concatenate([agg_ref[r] for r in range(parts)], axis=0)
    feat = jnp.concatenate([fc_ref[r, :rows] for r in range(parts)], axis=0)
    ws = ws_ref[...]
    wn = wn_ref[...]
    pre = lax.dot_general(ws, feat, FIRST, preferred_element_type=F32)
    pre += lax.dot_general(wn, agg, FIRST, preferred_element_type=F32)
    cot = jnp.concatenate([fc_ref[r, rows:] for r in range(parts)], axis=0).astype(F32)
    sig = jax.nn.sigmoid(pre)
    out = (pre * sig).astype(BF)
    grad = (cot * (sig * (1.0 + pre * (1.0 - sig)))).astype(BF)
    grad_agg = jnp.dot(wn, grad, preferred_element_type=F32).astype(BF)
    direct = jnp.dot(ws, grad, preferred_element_type=F32).astype(BF)
    gself = lax.dot_general(feat, grad, LAST, preferred_element_type=F32)
    gneigh = lax.dot_general(agg, grad, LAST, preferred_element_type=F32)
    for r in range(parts):
        here = slice(r * rows, (r + 1) * rows)
        ga_ref[r] = grad_agg[here]
        rest_ref[r, :rows] = out[here]
        rest_ref[r, rows:] = direct[here]
        gw_ref[r, :, : gself.shape[1]] = gself[here]
        gw_ref[r, :, gself.shape[1] :] = gneigh[here]


def backward_kernel(place_ref, ga_ref, weight_ref, own_ref, send_ref, total, *, own, peers):
    step = pl.program_id(0)
    rows = ga_ref.shape[1]
    half = rows // 2
    blocks = weight_ref.shape[0]
    slots = weight_ref.shape[1] // T

    @pl.when(step == 0)
    def _():
        total[...] = jnp.zeros_like(total)

    for j in range(blocks):
        at = (step * blocks + j) * slots
        part = lax.dot_general(
            ga_ref[0, :, j * T : (j + 1) * T], weight_ref[j], LAST, preferred_element_type=F32
        )
        for s in range(slots):
            total[place_ref[at + s]] += part[:, s * T : (s + 1) * T]

    @pl.when(step == pl.num_programs(0) - 1)
    def _():
        low = low_lanes(half)
        for i in range(own):
            own_ref[:, i * T : (i + 1) * T] = total[i]

        def pair(t, carry):
            top = total[own + t, :half]
            bottom = total[own + t, half:]
            send_ref[2 * t, rows:] = jnp.where(low, top, swap_halves(bottom)).astype(BF)
            send_ref[2 * t + 1, rows:] = jnp.where(low, swap_halves(top), bottom).astype(BF)
            send_ref[2 * t, :rows] = total[own + peers // 2 + 2 * t].astype(BF)
            send_ref[2 * t + 1, :rows] = total[own + peers // 2 + 2 * t + 1].astype(BF)
            return carry

        lax.fori_loop(0, peers // 2, pair, 0)


def finish_kernel(recv_ref, index_ref, own_ref, direct_ref, grad_ref, out_ref, slots_ref, *, chunk):
    rows, nodes = own_ref.shape
    half = rows // 2
    peers = recv_ref.shape[0]
    parts = direct_ref.shape[0]
    span = nodes // parts
    low = low_lanes(half)
    for t in range(peers // 2):
        a = recv_ref[2 * t, rows:].astype(F32)
        b = recv_ref[2 * t + 1, rows:].astype(F32)
        slots_ref[:half, t * T : (t + 1) * T] = jnp.where(low, a, swap_halves(b)).astype(BF)
        slots_ref[half:, t * T : (t + 1) * T] = jnp.where(low, swap_halves(a), b).astype(BF)
    for r in range(parts):
        here = slice(r * span, (r + 1) * span)
        grad_ref[:, here] = own_ref[:, here] + direct_ref[r, rows:].astype(F32)
        out_ref[:, here] = direct_ref[r, :rows]
    hub = recv_ref[0, :rows].astype(F32)
    for p in range(1, peers):
        hub += recv_ref[p, :rows].astype(F32)
    grad_ref[:, :T] += hub
    slot_count = index_ref.shape[1]

    def body(t, carry):
        base = pl.multiple_of(t * 2 * T, 2 * T)
        acc = jnp.zeros((rows, 2 * T), F32)
        for c in range(slot_count // chunk):
            here = slice(c * chunk, (c + 1) * chunk)
            acc += lax.dot_general(
                slots_ref[:, here],
                onehot(index_ref[:, here], base, 2 * T),
                LAST,
                preferred_element_type=F32,
            )
        grad_ref[:, pl.ds(base, 2 * T)] += acc
        return carry

    lax.fori_loop(0, nodes // (2 * T), body, 0)


def whole(shape):
    return pl.BlockSpec(shape, lambda *_: (0,) * len(shape))


def local(
    features,
    cotangent,
    w_self,
    w_neigh,
    send_index,
    send_count,
    tile_index,
    tile_count,
    tile_weight,
):
    rows, nodes = features.shape
    peers = lax.axis_size("vert")
    parts = lax.axis_size("af")
    span = nodes // parts
    feat_out = w_self.shape[1]
    blocks, slots = tile_index.shape
    slot_count = send_index.shape[2]
    own = nodes // T
    sources = own + peers * slot_count // T + peers
    per_step = span // T
    half = rows // 2

    exchange = functools.partial(lax.all_to_all, split_axis=0, concat_axis=0, tiled=True)
    both = jnp.stack([features, cotangent]).reshape(2, rows, parts, span)
    both = jnp.transpose(both, (2, 0, 1, 3)).reshape(parts, 2 * rows, span)
    both = exchange(both, "af")

    slot_live = lax.broadcasted_iota(jnp.int32, (peers, slot_count), 1) < send_count.reshape(
        peers, 1
    )
    index_row = jnp.where(slot_live, send_index[0], -1).reshape(1, peers * slot_count)
    tile_live = lax.broadcasted_iota(jnp.int32, (blocks, slots), 1) < tile_count[:, None]
    place = jnp.where(tile_live, tile_index, sources).reshape(blocks * slots)
    weight = tile_weight.reshape(blocks, slots * T, T)

    send = pl.pallas_call(
        functools.partial(pick_kernel, chunk=512),
        out_shape=jax.ShapeDtypeStruct((peers, rows + half, T), BF),
        compiler_params=params(16),
        name="pick",
    )(features, index_row)
    recv = exchange(send, "vert")

    agg = pl.pallas_call(
        forward_kernel,
        grid_spec=pltpu.PrefetchScalarGridSpec(
            num_scalar_prefetch=1,
            grid=(parts,),
            in_specs=[
                whole((rows, nodes)),
                whole((peers, rows + half, T)),
                pl.BlockSpec((per_step, slots * T, T), lambda i, _: (i, 0, 0)),
            ],
            out_specs=pl.BlockSpec((1, rows, span), lambda i, _: (i, 0, 0)),
            scratch_shapes=[pltpu.VMEM((sources + 1, rows, T), BF)],
        ),
        out_shape=jax.ShapeDtypeStruct((parts, rows, span), BF),
        compiler_params=params(24),
        name="aggregate",
    )(place, features, recv, weight)
    agg = exchange(agg, "af")

    grad_agg, rest, gw = pl.pallas_call(
        dense_kernel,
        out_shape=(
            jax.ShapeDtypeStruct((parts, rows, span), BF),
            jax.ShapeDtypeStruct((parts, 2 * rows, span), BF),
            jax.ShapeDtypeStruct((parts, rows, 2 * feat_out), F32),
        ),
        compiler_params=params(32),
        name="dense",
    )(agg, both, w_self, w_neigh)
    grad_agg = exchange(grad_agg, "af")
    rest = exchange(rest, "af")

    gw = exchange(gw, "af").sum(axis=0)
    piece = rows * 2 * feat_out // (peers * T)
    gw = exchange(gw.reshape(peers, piece, T), "vert").sum(axis=0)
    gw = exchange(jnp.broadcast_to(gw[None], (peers, piece, T)), "vert")
    gw = gw.reshape(rows, 2 * feat_out) * (1.0 / math.sqrt(nodes * peers))

    own_grad, send = pl.pallas_call(
        functools.partial(backward_kernel, own=own, peers=peers),
        grid_spec=pltpu.PrefetchScalarGridSpec(
            num_scalar_prefetch=1,
            grid=(parts,),
            in_specs=[
                pl.BlockSpec((1, rows, span), lambda i, _: (i, 0, 0)),
                pl.BlockSpec((per_step, slots * T, T), lambda i, _: (i, 0, 0)),
            ],
            out_specs=[whole((rows, nodes)), whole((peers, rows + half, T))],
            scratch_shapes=[pltpu.VMEM((sources + 1, rows, T), F32)],
        ),
        out_shape=(
            jax.ShapeDtypeStruct((rows, nodes), F32),
            jax.ShapeDtypeStruct((peers, rows + half, T), BF),
        ),
        compiler_params=params(24),
        name="spread",
    )(place, grad_agg, weight)
    recv = exchange(send, "vert")

    grad_x, output = pl.pallas_call(
        functools.partial(finish_kernel, chunk=512),
        out_shape=(
            jax.ShapeDtypeStruct((rows, nodes), F32),
            jax.ShapeDtypeStruct((rows, nodes), BF),
        ),
        scratch_shapes=[pltpu.VMEM((rows, peers * slot_count), BF)],
        compiler_params=params(24),
        name="finish",
    )(recv, index_row, own_grad, rest)
    return output, grad_x, gw[:, :feat_out], gw[:, feat_out:]


def solution(mesh):
    in_specs = (
        P("af", "vert"),
        P("af", "vert"),
        P(),
        P(),
        P("vert", None, None),
        P("vert", None),
        P("vert", None),
        P("vert"),
        P("vert", None, None, None),
    )
    out_specs = (P("af", "vert"), P("af", "vert"), P("af", None), P("af", None))
    return jax.shard_map(local, mesh=mesh, in_specs=in_specs, out_specs=out_specs, check_vma=False)
```

time: 1440 us -> 291 us (0.20)
  waiting for transfers between devices: 1250 us -> 125 us
  blocking collectives: 0 us -> 76.1 us
  other arithmetic: 74.9 us -> 1.97 us
  Pallas kernels: 0 us -> 38 us
  local copies, waits for them, and re-layouts: 52 us -> 15.9 us
  matrix products: 30.1 us -> 0 us
    psum x1 -> x0, waiting for transfers between devices: 551 us -> none  [local(): summed_self, summed_neigh = lax.psum((grad_self_w, grad_neigh_w), 'vert')]
    reduce_scatter x2 -> x0, waiting for transfers between devices: 418 us -> none  [the longest x1 338 us: local(): lax.psum_scatter(grad_source[:, edge:], 'vert', scatter_dimension=1, tile...]
    all_gather x2 -> x0, waiting for transfers between devices: 264 us -> none  [the longest x1 225 us: local(): hub_rows = lax.all_gather(features[:, :HUB_DEV], 'vert', axis=1, tiled=True)]
    all_to_all x2 -> x5, waiting for transfers between devices: 16.4 us -> 125 us  [the longest x2 77.3 us: local(): recv = exchange(send, 'vert')]
    all_to_all x0 -> x4, blocking collectives: none -> 76.1 us  [the longest x1 22.9 us: local(): gw = exchange(gw.reshape(peers, piece, T), 'vert').sum(axis=0)]
    scatter-add x2 -> x0, other arithmetic: 62.9 us -> none  [the longest x1 39.5 us: local(): grad_source.at[:, tile_index.reshape(-1)]]
    pallas_call x0 -> x5, Pallas kernels: none -> 38 us  [the longest x1 13.6 us: local(): pl.pallas_call(functools.partial(finish_kernel, chunk=512), out_shape=(ja...]
    dot_general x8 -> x0, matrix products: 30.1 us -> none  [the longest x1 9.64 us: local(): jnp.einsum('fjb,jsab->fjsa', grad_agg, tile_weight, preferred_element_typ...]
  transfers between devices with their start and end apart: 7 -> 5, of which waited for: 6 -> 5; matrix products, arithmetic and copies ran while one was open for 9% -> 1% of each run, Pallas kernels for 0% -> 4%
where the time goes in v1:
time: 291 us; the launch traced here: 289 us
  waiting for transfers between devices  125 us (43%)
  blocking collectives  76.1 us (26%)
  Pallas kernels  38 us (13%)
  starting transfers between devices  30.4 us (10%)
  local copies, waits for them, and re-layouts  15.9 us (5%)
    all_to_all x2, waiting for transfers between devices, local(): recv = exchange(send, 'vert')  77.3 us
    all_to_all x1, blocking collectives, local(): gw = exchange(gw.reshape(peers, piece, T), 'vert').sum(axis=0)  22.9 us
    all_to_all x1, blocking collectives, local(): gw = exchange(gw, 'af').sum(axis=0)  19 us
    all_to_all x1, blocking collectives, local(): agg = exchange(agg, 'af')  17.8 us
    all_to_all x2, starting transfers between devices, local(): recv = exchange(send, 'vert')  17.7 us
    all_to_all x1, waiting for transfers between devices, local(): both = exchange(both, 'af')  17.4 us
    all_to_all x1, waiting for transfers between devices, local(): grad_agg = exchange(grad_agg, 'af')  16.5 us
    all_to_all x1, blocking collectives, local(): gw = exchange(jnp.broadcast_to(gw[None], (peers, piece, T)), 'vert')  16.4 us
  transfers between devices with their start and end apart: 5, of which 5 were waited for; matrix products, arithmetic and copies ran while one was open for 1% of the time, Pallas kernels for 4%

profile of v1, /device:TPU:0, one launch (start us, length us, event | category | flops | bytes accessed | tf_op | source)
XLA Modules:
  0.0 288.6 jit_solution(4611472849978705636)
XLA Ops:
  3.4 10.1 %pick.1 = bf16[64,96,128]{2,1,0:T(8,128)(2,1)} custom-call(bf16[64,4096]{1,0:T(8,128)(2,1)S(1)} %copy-done.2, s32[1,4096]{1,0:T(1,128)S(1)} %broadcast_select_fusion.index_ref), custom_call_target="tpu_custom_call" | custom-call | tf_op jit(solution)/shard_map/pick/pallas_call | solution.py:239
  13.5 10.4 %all-to-all-start = ((bf16[64,96,128]{2,1,0:T(8,128)(2,1)}), bf16[64,96,128]{2,1,0:T(8,128)(2,1)S(1)}, u32[]{:S(2)}, u32[]{:S(2)}) async-start(bf16[64,96,128]{2,1,0:T(8,128)(2,1)} %pick.1), calls=%async_computation | async-start | bytes 3145728 | tf_op jit(solution)/shard_map/all_to_all | solution.py:245
  24.3 1.4 stack.10
  27.2 37.4 %all-to-all-done.recv_ref = bf16[64,96,128]{2,1,0:T(8,128)(2,1)S(1)} async-done(((bf16[64,96,128]{2,1,0:T(8,128)(2,1)}), bf16[64,96,128]{2,1,0:T(8,128)(2,1)S(1)}, u32[]{:S(2)}, u32[]{:S(2)}) %all-to-all-start) | async-done | bytes 1572896 | tf_op jit(solution)/shard_map/all_to_all | solution.py:245
  64.6 5.8 %all-to-all-start.2 = ((bf16[4,128,1024]{2,1,0:T(8,128)(2,1)}), bf16[4,128,1024]{2,1,0:T(8,128)(2,1)S(1)}, u32[]{:S(2)}, u32[]{:S(2)}) async-start(bf16[4,128,1024]{2,1,0:T(8,128)(2,1)} %bitcast.11), calls=%async_computation.2 | async-start | bytes 2097152 | tf_op jit(solution)/shard_map/all_to_all | solution.py:229
  70.6 3.4 %copy-done = bf16[32,8,128,128]{3,2,1,0:T(8,128)(2,1)S(1)} copy-done((bf16[32,8,128,128]{3,2,1,0:T(8,128)(2,1)S(1)}, bf16[32,8,128,128]{3,2,1,0:T(8,128)(2,1)}, u32[]{:S(2)}) %copy-start) | copy-done | bytes 8388632
  73.9 5.3 %aggregate.1 = bf16[4,64,1024]{2,1,0:T(8,128)(2,1)S(1)} custom-call(s32[256]{0:T(256)S(1)} %reshape.65.place_ref, bf16[64,4096]{1,0:T(8,128)(2,1)S(1)} %copy-done.3, bf16[64,96,128]{2,1,0:T(8,128)(2,1)S(1)} %all-to-all-done.recv_ref, bf16[32,1024,128]{2,1,0:T(8,128)(2,1)S(1)} %bitcast.9), custom_call_target="tpu_custom_call" | custom-call | tf_op jit(solution)/shard_map/aggregate/pallas_call | solution.py:247
  80.0 17.4 %all-to-all-done.2.fc_ref = bf16[4,128,1024]{2,1,0:T(8,128)(2,1)S(1)} async-done(((bf16[4,128,1024]{2,1,0:T(8,128)(2,1)}), bf16[4,128,1024]{2,1,0:T(8,128)(2,1)S(1)}, u32[]{:S(2)}, u32[]{:S(2)}) %all-to-all-start.2) | async-done | bytes 1048608 | tf_op jit(solution)/shard_map/all_to_all | solution.py:229
  97.4 17.8 %all_to_all.45.agg_ref = bf16[4,64,1024]{2,1,0:T(8,128)(2,1)S(1)} all-to-all(bf16[4,64,1024]{2,1,0:T(8,128)(2,1)} %copy-done.4), channel_id=1, replica_groups=mesh['vert'=64,'af'=4] {'af'}, dimensions={0} | all-to-all | bytes 1048576 | tf_op jit(solution)/shard_map/all_to_all | solution.py:264
  115.3 2.1 dense.1
  117.4 19.0 %all_to_all.46 = f32[4,64,512]{2,1,0:T(8,128)S(1)} all-to-all(f32[4,64,512]{2,1,0:T(8,128)S(1)} %get-tuple-element.17), channel_id=1, replica_groups=mesh['vert'=64,'af'=4] {'af'}, dimensions={0} | all-to-all | bytes 1048576 | tf_op jit(solution)/shard_map/all_to_all | solution.py:279
  136.5 22.9 %all_to_all.47 = f32[64,4,128]{2,1,0:T(4,128)S(1)} all-to-all(f32[64,4,128]{2,1,0:T(4,128)S(1)} %reshape.68), channel_id=1, replica_groups=mesh['vert'=64,'af'=4] {'vert'}, dimensions={0} | all-to-all | bytes 262144 | tf_op jit(solution)/shard_map/all_to_all | solution.py:281
  159.4 3.5 %all-to-all-start.3 = ((bf16[4,64,1024]{2,1,0:T(8,128)(2,1)}), bf16[4,64,1024]{2,1,0:T(8,128)(2,1)S(1)}, u32[]{:S(2)}, u32[]{:S(2)}) async-start(bf16[4,64,1024]{2,1,0:T(8,128)(2,1)} %get-tuple-element.11), calls=%async_computation.3 | async-start | bytes 1048576 | tf_op jit(solution)/shard_map/all_to_all | solution.py:276
  162.9 16.5 %all-to-all-done.3.ga_ref = bf16[4,64,1024]{2,1,0:T(8,128)(2,1)S(1)} async-done(((bf16[4,64,1024]{2,1,0:T(8,128)(2,1)}), bf16[4,64,1024]{2,1,0:T(8,128)(2,1)S(1)}, u32[]{:S(2)}, u32[]{:S(2)}) %all-to-all-start.3) | async-done | bytes 524320 | tf_op jit(solution)/shard_map/all_to_all | solution.py:276
  179.4 16.4 %all_to_all.48 = f32[64,4,128]{2,1,0:T(4,128)S(1)} all-to-all(f32[64,4,128]{2,1,0:T(4,128)S(1)} %broadcast_in_dim.17), channel_id=1, replica_groups=mesh['vert'=64,'af'=4] {'vert'}, dimensions={0} | all-to-all | bytes 262144 | tf_op jit(solution)/shard_map/all_to_all | solution.py:282
  195.8 3.5 %all-to-all-start.5 = ((bf16[4,128,1024]{2,1,0:T(8,128)(2,1)}), bf16[4,128,1024]{2,1,0:T(8,128)(2,1)S(1)}, u32[]{:S(2)}, u32[]{:S(2)}) async-start(bf16[4,128,1024]{2,1,0:T(8,128)(2,1)} %get-tuple-element.14), calls=%async_computation.5 | async-start | bytes 2097152 | tf_op jit(solution)/shard_map/all_to_all | solution.py:277
  199.4 3.4 %copy-done.1 = bf16[32,8,128,128]{3,2,1,0:T(8,128)(2,1)S(1)} copy-done((bf16[32,8,128,128]{3,2,1,0:T(8,128)(2,1)S(1)}, bf16[32,8,128,128]{3,2,1,0:T(8,128)(2,1)}, u32[]{:S(2)}) %copy-start.1) | copy-done | bytes 8388632
  202.8 6.9 %spread.1 = (f32[64,4096]{1,0:T(8,128)S(1)}, bf16[64,96,128]{2,1,0:T(8,128)(2,1)S(1)}) custom-call(s32[256]{0:T(256)S(1)} %reshape.65.place_ref, bf16[4,64,1024]{2,1,0:T(8,128)(2,1)S(1)} %all-to-all-done.3.ga_ref, bf16[32,1024,128]{2,1,0:T(8,128)(2,1)S(1)} %bitcast.10), custom_call_target="tpu_custom_call" | custom-call | tf_op jit(solution)/shard_map/spread/pallas_call | solution.py:285
  209.7 1.2 copy-done.5
  211.8 14.2 %all-to-all-done.5.direct_ref = bf16[4,128,1024]{2,1,0:T(8,128)(2,1)S(1)} async-done(((bf16[4,128,1024]{2,1,0:T(8,128)(2,1)}), bf16[4,128,1024]{2,1,0:T(8,128)(2,1)S(1)}, u32[]{:S(2)}, u32[]{:S(2)}) %all-to-all-start.5) | async-done | bytes 1048608 | tf_op jit(solution)/shard_map/all_to_all | solution.py:277
  226.0 7.3 %all-to-all-start.4 = ((bf16[64,96,128]{2,1,0:T(8,128)(2,1)}), bf16[64,96,128]{2,1,0:T(8,128)(2,1)S(1)}, u32[]{:S(2)}, u32[]{:S(2)}) async-start(bf16[64,96,128]{2,1,0:T(8,128)(2,1)} %copy-done.5), calls=%async_computation.4 | async-start | bytes 3145728 | tf_op jit(solution)/shard_map/all_to_all | solution.py:304
  234.0 39.8 %all-to-all-done.4.recv_ref = bf16[64,96,128]{2,1,0:T(8,128)(2,1)S(1)} async-done(((bf16[64,96,128]{2,1,0:T(8,128)(2,1)}), bf16[64,96,128]{2,1,0:T(8,128)(2,1)S(1)}, u32[]{:S(2)}, u32[]{:S(2)}) %all-to-all-start.4) | async-done | bytes 1572896 | tf_op jit(solution)/shard_map/all_to_all | solution.py:304
  273.8 1.2 copy-done.7
  275.0 13.6 %finish.1 = (f32[64,4096]{1,0:T(8,128)}, bf16[64,4096]{1,0:T(8,128)(2,1)}) custom-call(bf16[64,96,128]{2,1,0:T(8,128)(2,1)S(1)} %all-to-all-done.4.recv_ref, s32[1,4096]{1,0:T(1,128)S(1)} %broadcast_select_fusion.index_ref, f32[64,4096]{1,0:T(8,128)S(1)} %copy-done.7, bf16[4,128,1024]{2,1,0:T(8,128)(2,1)S(1)} %all-to-all-done.5.direct_ref), custom_call_target="tpu_custom_call" | custom-call | tf_op jit(solution)/shard_map/finish/pallas_call | solution.py:306
  (38 shorter events, 7.3 us)
Async XLA Ops:
  2.3 1.0 copy-start.2
  13.5 10.4 %copy-start.3 = (bf16[64,4096]{1,0:T(8,128)(2,1)S(1)}, bf16[64,4096]{1,0:T(8,128)(2,1)}, u32[]{:S(2)}) copy-start(bf16[64,4096]{1,0:T(8,128)(2,1)} %feat_ref.3) | copy-start | bytes 1572868
  13.5 51.1 %all-to-all-start = ((bf16[64,96,128]{2,1,0:T(8,128)(2,1)}), bf16[64,96,128]{2,1,0:T(8,128)(2,1)S(1)}, u32[]{:S(2)}, u32[]{:S(2)}) async-start(bf16[64,96,128]{2,1,0:T(8,128)(2,1)} %pick.1), calls=%async_computation | async-start | bytes 3145728 | tf_op jit(solution)/shard_map/all_to_all | solution.py:245
  27.2 43.2 %copy-start.10 = (s32[32,8]{0,1:T(8,128)S(1)}, s32[32,8]{0,1:T(8,128)}, u32[]{:S(2)}) copy-start(s32[32,8]{0,1:T(8,128)} %param.15) | copy-start | bytes 3076
  27.2 43.2 %copy-start.11 = (s32[32]{0:T(128)S(1)}, s32[32]{0:T(128)}, u32[]{:S(2)}) copy-start(s32[32]{0:T(128)} %param.16) | copy-start | bytes 388
  64.6 32.8 %all-to-all-start.2 = ((bf16[4,128,1024]{2,1,0:T(8,128)(2,1)}), bf16[4,128,1024]{2,1,0:T(8,128)(2,1)S(1)}, u32[]{:S(2)}, u32[]{:S(2)}) async-start(bf16[4,128,1024]{2,1,0:T(8,128)(2,1)} %bitcast.11), calls=%async_computation.2 | async-start | bytes 2097152 | tf_op jit(solution)/shard_map/all_to_all | solution.py:229
  70.5 3.4 %copy-start = (bf16[32,8,128,128]{3,2,1,0:T(8,128)(2,1)S(1)}, bf16[32,8,128,128]{3,2,1,0:T(8,128)(2,1)}, u32[]{:S(2)}) copy-start(bf16[32,8,128,128]{3,2,1,0:T(8,128)(2,1)} %param.17) | copy-start | bytes 25165828
  73.9 41.4 %copy-start.8 = (bf16[256,256]{1,0:T(8,128)(2,1)S(1)}, bf16[256,256]{1,0:T(8,128)(2,1)}, u32[]{:S(2)}) copy-start(bf16[256,256]{1,0:T(8,128)(2,1)} %ws_ref.1) | copy-start | bytes 393220
  73.9 41.4 %copy-start.9 = (bf16[256,256]{1,0:T(8,128)(2,1)S(1)}, bf16[256,256]{1,0:T(8,128)(2,1)}, u32[]{:S(2)}) copy-start(bf16[256,256]{1,0:T(8,128)(2,1)} %wn_ref.1) | copy-start | bytes 393220
  79.2 0.8 copy-start.4
  159.4 20.0 %all-to-all-start.3 = ((bf16[4,64,1024]{2,1,0:T(8,128)(2,1)}), bf16[4,64,1024]{2,1,0:T(8,128)(2,1)S(1)}, u32[]{:S(2)}, u32[]{:S(2)}) async-start(bf16[4,64,1024]{2,1,0:T(8,128)(2,1)} %get-tuple-element.11), calls=%async_computation.3 | async-start | bytes 1048576 | tf_op jit(solution)/shard_map/all_to_all | solution.py:276
  195.8 30.2 %all-to-all-start.5 = ((bf16[4,128,1024]{2,1,0:T(8,128)(2,1)}), bf16[4,128,1024]{2,1,0:T(8,128)(2,1)S(1)}, u32[]{:S(2)}, u32[]{:S(2)}) async-start(bf16[4,128,1024]{2,1,0:T(8,128)(2,1)} %get-tuple-element.14), calls=%async_computation.5 | async-start | bytes 2097152 | tf_op jit(solution)/shard_map/all_to_all | solution.py:277
  199.4 3.4 %copy-start.1 = (bf16[32,8,128,128]{3,2,1,0:T(8,128)(2,1)S(1)}, bf16[32,8,128,128]{3,2,1,0:T(8,128)(2,1)}, u32[]{:S(2)}) copy-start(bf16[32,8,128,128]{3,2,1,0:T(8,128)(2,1)} %param.17) | copy-start | bytes 25165828
  209.7 1.2 copy-start.5
  210.9 1.0 copy-start.6
  226.0 47.8 %all-to-all-start.4 = ((bf16[64,96,128]{2,1,0:T(8,128)(2,1)}), bf16[64,96,128]{2,1,0:T(8,128)(2,1)S(1)}, u32[]{:S(2)}, u32[]{:S(2)}) async-start(bf16[64,96,128]{2,1,0:T(8,128)(2,1)} %copy-done.5), calls=%async_computation.4 | async-start | bytes 3145728 | tf_op jit(solution)/shard_map/all_to_all | solution.py:304
  273.8 1.2 copy-start.7

commit v2 on v1

v2 whole, which is shorter than its diff:
```python
import functools
import math

import jax
import jax.numpy as jnp
from jax import lax
from jax.experimental import pallas as pl
from jax.experimental.pallas import tpu as pltpu
from jax.sharding import PartitionSpec as P

T = 128
BF = jnp.bfloat16
F32 = jnp.float32
FIRST = (((0,), (0,)), ((), ()))
LAST = (((1,), (1,)), ((), ()))


def params(mib):
    return pltpu.CompilerParams(vmem_limit_bytes=mib * 2**20)


def low_lanes(rows):
    return lax.broadcasted_iota(jnp.int32, (rows, T), 1) < T // 2


def swap_halves(x):
    return pltpu.roll(x, T // 2, 1)


def onehot(index_row, width):
    row = lax.broadcasted_iota(jnp.int16, (width, index_row.shape[1]), 0)
    low = jnp.where(index_row < 0, -1, index_row & (width - 1))
    return jnp.where(row == low.astype(jnp.int16), BF(1), BF(0))


def split_kernel(me_ref, array_ref, *outs):
    span = outs[0].shape[1]
    me = me_ref[0]
    for k, out_ref in enumerate(outs, 1):
        out_ref[...] = array_ref[:, pl.ds(pl.multiple_of((me ^ k) * span, span), span)]


def pick_kernel(feat_ref, index_ref, out_ref, stacked, *, width):
    rows, nodes = feat_ref.shape
    half = rows // 2
    low = low_lanes(half)
    for h in range(nodes // width):
        stacked[h * rows : (h + 1) * rows] = feat_ref[:, h * width : (h + 1) * width]

    def body(t, carry):
        cols = pl.ds(pl.multiple_of(t * 2 * T, 2 * T), 2 * T)
        index_row = index_ref[:, cols]
        high = jnp.broadcast_to(index_row >> (width.bit_length() - 1), (rows, 2 * T))
        found = jnp.dot(stacked[...], onehot(index_row, width), preferred_element_type=F32)
        found = [found[h * rows : (h + 1) * rows] for h in range(nodes // width)]
        while len(found) > 1:
            odd = (high & 1) != 0
            high = high >> 1
            found = [jnp.where(odd, b, a) for a, b in zip(found[::2], found[1::2])]
        acc = found[0]
        for u in range(2):
            top = acc[:half, u * T : (u + 1) * T]
            bottom = acc[half:, u * T : (u + 1) * T]
            q = t * 4 + u * 2
            out_ref[q] = jnp.where(low, top, swap_halves(bottom)).astype(BF)
            out_ref[q + 1] = jnp.where(low, swap_halves(top), bottom).astype(BF)
        return carry

    lax.fori_loop(0, index_ref.shape[1] // (2 * T), body, 0, unroll=2)


def forward_kernel(me_ref, place_ref, feat_ref, recv_ref, h0, h1, h2, h3, weight_ref, *refs):
    outs, (source, result) = refs[:4], refs[4:]
    step = pl.program_id(0)
    rows, nodes = feat_ref.shape
    half = rows // 2
    peers = recv_ref.shape[0]
    own = nodes // T
    blocks = weight_ref.shape[0]
    slots = weight_ref.shape[1] // T

    @pl.when(step == 0)
    def _():
        low = low_lanes(half)
        for i in range(own):
            source[i] = feat_ref[:, i * T : (i + 1) * T]

        def pair(t, carry):
            a = recv_ref[2 * t].astype(F32)
            b = recv_ref[2 * t + 1].astype(F32)
            source[own + t, :half] = jnp.where(low, a, swap_halves(b)).astype(BF)
            source[own + t, half:] = jnp.where(low, swap_halves(a), b).astype(BF)
            return carry

        lax.fori_loop(0, peers // 2, pair, 0)
        first = own + peers // 2
        for k, hub_ref in enumerate((h0, h1, h2, h3)):
            many = hub_ref.shape[0]
            source[first + k * many : first + (k + 1) * many] = hub_ref[...]
        source[first + peers] = jnp.zeros((rows, T), BF)

    first = (me_ref[0] ^ (3 - step)) * blocks
    for j in range(blocks):
        at = (first + j) * slots
        picked = jnp.concatenate([source[place_ref[at + s]] for s in range(slots)], axis=1)
        total = jnp.dot(picked, weight_ref[j], preferred_element_type=F32)
        result[:, j * T : (j + 1) * T] = total.astype(BF)
    for k in range(4):

        @pl.when(step == 3 - k)
        def _(k=k):
            outs[k][...] = result[...]


def dense_kernel(me_ref, *refs):
    aggs, feat_ref, cot_ref, feats, cots = refs[:4], refs[4], refs[5], refs[6:9], refs[9:12]
    ws_ref, wn_ref, gas, rests = refs[12], refs[13], refs[14:18], refs[18:22]
    agg_s, feat_s, cot_s, out_s, dir_s, gw_s = refs[22:]
    rows = feat_ref.shape[0]
    me = me_ref[0]
    at = [pl.ds(pl.multiple_of((me ^ k) * rows, rows), rows) for k in range(4)]
    feat_s[at[0]] = feat_ref[...]
    cot_s[at[0]] = cot_ref[...]
    for k in range(4):
        agg_s[at[k]] = aggs[k][...]
        if k:
            feat_s[at[k]] = feats[k - 1][...]
            cot_s[at[k]] = cots[k - 1][...]
    agg = agg_s[...]
    feat = feat_s[...]
    ws = ws_ref[...]
    wn = wn_ref[...]
    pre = lax.dot_general(ws, feat, FIRST, preferred_element_type=F32)
    pre += lax.dot_general(wn, agg, FIRST, preferred_element_type=F32)
    sig = jax.nn.sigmoid(pre)
    out_s[...] = (pre * sig).astype(BF)
    grad = (cot_s[...].astype(F32) * (sig * (1.0 + pre * (1.0 - sig)))).astype(BF)
    agg_s[...] = jnp.dot(wn, grad, preferred_element_type=F32).astype(BF)
    dir_s[...] = jnp.dot(ws, grad, preferred_element_type=F32).astype(BF)
    wide = ws.shape[1]
    gw_s[:, :wide] = lax.dot_general(feat, grad, LAST, preferred_element_type=F32).astype(BF)
    gw_s[:, wide:] = lax.dot_general(agg, grad, LAST, preferred_element_type=F32).astype(BF)
    for k in range(4):
        gas[k][:rows] = agg_s[at[k]]
        mine = gw_s[at[k]]
        gas[k][rows:, : 2 * wide] = mine[: rows // 2]
        gas[k][rows:, 2 * wide :] = mine[rows // 2 :]
        rests[k][:rows] = out_s[at[k]]
        rests[k][rows:] = dir_s[at[k]]


def backward_kernel(me_ref, place_ref, g0, g1, g2, g3, weight_ref, *refs, own, peers):
    own_ref, send_ref, hub0, hub1, hub2, hub3, total, grads = refs
    step = pl.program_id(0)
    rows = own_ref.shape[0]
    half = rows // 2
    blocks = weight_ref.shape[0]
    slots = weight_ref.shape[1] // T

    @pl.when(step == 0)
    def _():
        total[...] = jnp.zeros_like(total)
        for k, grad_ref in enumerate((g0, g1, g2, g3)):
            grads[k] = grad_ref[:rows]

    first = (me_ref[0] ^ step) * blocks
    for j in range(blocks):
        at = (first + j) * slots
        part = lax.dot_general(
            grads[step, :, j * T : (j + 1) * T], weight_ref[j], LAST, preferred_element_type=F32
        )
        for s in range(slots):
            total[place_ref[at + s]] += part[:, s * T : (s + 1) * T]

    @pl.when(step == pl.num_programs(0) - 1)
    def _():
        low = low_lanes(half)
        for i in range(own):
            own_ref[:, i * T : (i + 1) * T] = total[i]

        def pair(t, carry):
            top = total[own + t, :half]
            bottom = total[own + t, half:]
            send_ref[2 * t] = jnp.where(low, top, swap_halves(bottom)).astype(BF)
            send_ref[2 * t + 1] = jnp.where(low, swap_halves(top), bottom).astype(BF)
            return carry

        lax.fori_loop(0, peers // 2, pair, 0)
        many = peers // 4
        for k, hub_ref in enumerate((hub0, hub1, hub2, hub3)):
            start = own + peers // 2 + k * many
            hub_ref[:many] = total[start : start + many].astype(hub_ref.dtype)
        wide = g0.shape[1] // 2
        for u in range(2):
            here = slice(u * wide, (u + 1) * wide)
            g = [x[rows:, here].astype(F32) for x in (g0, g1, g2, g3)]
            gw = ((g[0] + g[1]) + (g[2] + g[3])).astype(BF)
            for c in range(wide // T):
                part = gw[:, c * T : (c + 1) * T]
                for hub_ref in (hub0, hub1, hub2, hub3):
                    hub_ref[many + c, u * half : (u + 1) * half] = part.astype(hub_ref.dtype)


def finish_kernel(me_ref, recv_ref, index_ref, own_ref, *refs, width, chunk, scale):
    rests, hubs = refs[:4], refs[4:8]
    grad_ref, out_ref, gself_ref, gneigh_ref, slots_ref, acc_ref = refs[8:]
    rows, nodes = own_ref.shape
    half = rows // 2
    peers = recv_ref.shape[0]
    span = rests[0].shape[1]
    low = low_lanes(half)
    me = me_ref[0]
    for t in range(peers // 2):
        a = recv_ref[2 * t].astype(F32)
        b = recv_ref[2 * t + 1].astype(F32)
        slots_ref[:half, t * T : (t + 1) * T] = jnp.where(low, a, swap_halves(b)).astype(BF)
        slots_ref[half:, t * T : (t + 1) * T] = jnp.where(low, swap_halves(a), b).astype(BF)
    for k in range(4):
        here = pl.ds(pl.multiple_of((me ^ k) * span, span), span)
        grad_ref[:, here] = own_ref[:, here] + rests[k][rows:].astype(F32)
        out_ref[:, here] = rests[k][:rows]
    many = nodes // width
    acc_ref[...] = jnp.zeros_like(acc_ref)

    def body(t, carry):
        cols = pl.ds(pl.multiple_of(t * chunk, chunk), chunk)
        index_row = index_ref[:, cols]
        high = jnp.broadcast_to(index_row >> (width.bit_length() - 1), (rows, chunk)).astype(jnp.int16)
        values = slots_ref[:, cols]
        spread = jnp.concatenate([jnp.where(high == h, values, BF(0)) for h in range(many)], axis=0)
        acc_ref[...] += lax.dot_general(
            spread, onehot(index_row, width), LAST, preferred_element_type=F32
        )
        return carry

    lax.fori_loop(0, index_ref.shape[1] // chunk, body, 0)
    for h in range(many):
        grad_ref[:, h * width : (h + 1) * width] += acc_ref[h * rows : (h + 1) * rows]
    total = [
        (hubs[0][c] + hubs[1][c].astype(F32)) + (hubs[2][c].astype(F32) + hubs[3][c].astype(F32))
        for c in range(hubs[0].shape[0])
    ]
    grad_ref[:, :T] += total[0]
    wide = gself_ref.shape[1] // T
    for c in range(wide):
        gself_ref[:, c * T : (c + 1) * T] = total[1 + c] * scale
        gneigh_ref[:, c * T : (c + 1) * T] = total[1 + wide + c] * scale

def add_kernel(own_ref, one_ref, two_ref, three_ref, *outs):
    wide = outs[0].shape[0] * len(outs) - own_ref.shape[0]
    wide = wide // (len(outs) - 1)
    many = own_ref.shape[0] - wide
    for i in range(many + wide):
        total = (own_ref[i] + one_ref[i].astype(F32)) + (two_ref[i].astype(F32) + three_ref[i].astype(F32))
        if i < many:
            out_ref = outs[i * len(outs) // many]
            out_ref[i % (many // len(outs))] = total.astype(out_ref.dtype)
        else:
            total = total.astype(BF)
            for out_ref in outs:
                out_ref[many // len(outs) + i - many] = total.astype(out_ref.dtype)


def whole(shape):
    return pl.BlockSpec(shape, lambda *_: (0,) * len(shape))


def shape_of(*shape, dtype=BF):
    return jax.ShapeDtypeStruct(shape, dtype)


def call(kernel, name, prefetch, out_shape, operands, in_specs=None, grid=(1,), scratch=(), mib=24, micros=0):
    in_specs = in_specs or {}
    return pl.pallas_call(
        kernel,
        grid_spec=pltpu.PrefetchScalarGridSpec(
            num_scalar_prefetch=len(prefetch),
            grid=grid,
            in_specs=[in_specs.get(i) or whole(x.shape) for i, x in enumerate(operands)],
            out_specs=[whole(s.shape) for s in out_shape],
            scratch_shapes=[pltpu.VMEM(s.shape, s.dtype) for s in scratch],
        ),
        out_shape=tuple(out_shape),
        compiler_params=params(mib),
        cost_estimate=pl.CostEstimate(
            flops=int(micros * 1e9), bytes_accessed=int(micros * 3e6), transcendentals=0
        ) if micros else None,
        name=name,
    )(*prefetch, *operands)


def local(
    features,
    cotangent,
    w_self,
    w_neigh,
    send_index,
    send_count,
    tile_index,
    tile_count,
    tile_weight,
):
    rows, nodes = features.shape
    peers = lax.axis_size("vert")
    parts = lax.axis_size("af")
    span = nodes // parts
    feat_out = w_self.shape[1]
    blocks, slots = tile_index.shape
    slot_count = send_index.shape[2]
    own = nodes // T
    first_hub = own + peers * slot_count // T
    sources = first_hub + peers
    per_step = span // T
    half = rows // 2
    vert = lax.axis_index("vert")
    me = lax.axis_index("af").astype(jnp.int32).reshape(1)

    def swap(x, axis, mask):
        size = peers if axis == "vert" else parts
        return lax.ppermute(x, axis, [(i, i ^ mask) for i in range(size)])

    def swap3(x, axis, unit):
        return [swap(x, axis, k * unit) for k in (1, 2, 3)]

    plane = peers // 4
    groups = [[y * plane + i for i in range(plane)] for y in range(4)]
    hub = jnp.broadcast_to(features[None, :, :T], (plane, rows, T))
    hub = lax.all_to_all(hub, "vert", 0, 0, axis_index_groups=groups, tiled=True)

    def split(x):
        parts_out = call(split_kernel, "split", (me,), [shape_of(rows, span)] * 3, (x,))
        return [swap(part, "af", k) for k, part in enumerate(parts_out, 1)]

    feats = split(features)
    cots = split(cotangent)

    slot_live = lax.broadcasted_iota(jnp.int32, (peers, slot_count), 1) < send_count.reshape(
        peers, 1
    )
    index_row = jnp.where(slot_live, send_index[0], -1).reshape(1, peers * slot_count)
    tile_live = lax.broadcasted_iota(jnp.int32, (blocks, slots), 1) < tile_count[:, None]
    def turned(mask):
        turn = ((tile_index - first_hub) ^ mask) + first_hub
        turn = jnp.where(tile_index >= first_hub, turn, tile_index)
        return jnp.where(tile_live, turn, sources).reshape(blocks * slots)

    place = turned(vert & (3 * plane))
    place_back = turned(vert)
    weight = tile_weight.reshape(blocks, slots * T, T)

    (send,) = call(
        functools.partial(pick_kernel, width=2 * T),
        "pick",
        (),
        [shape_of(peers, half, T)],
        (features, index_row),
        micros=30,
        scratch=[shape_of(rows * nodes // (2 * T), 2 * T)],
    )
    send, hub, feats = lax.optimization_barrier((send, hub, feats))
    hubs = [hub] + swap3(hub, "vert", 16)
    recv = lax.all_to_all(send, "vert", 0, 0, tiled=True)
    recv, cots = lax.optimization_barrier((recv, cots))

    agg = call(
        forward_kernel,
        "aggregate",
        (me, place),
        [shape_of(rows, span)] * 4,
        (features, recv, *hubs, weight),
        {6: pl.BlockSpec((per_step, slots * T, T), lambda i, me, _: (me[0] ^ (3 - i), 0, 0))},
        (parts,),
        [shape_of(sources + 1, rows, T), shape_of(rows, span)],
        mib=48,
    )
    agg = [x if k == 0 else swap(x, "af", k) for k, x in enumerate(agg)]

    mine = pl.BlockSpec((rows, span), lambda i, me: (0, me[0]))
    full = shape_of(parts * rows, span)
    dense = call(
        dense_kernel,
        "dense",
        (me,),
        [shape_of(rows + half, span)] * 4 + [shape_of(2 * rows, span)] * 4,
        (*agg, features, cotangent, *feats, *cots, w_self, w_neigh),
        {4: mine, 5: mine},
        scratch=[full] * 5 + [shape_of(parts * rows, 2 * feat_out)],
        mib=32,
    )
    grad_agg, rest = (
        [x if k == 0 else swap(x, "af", k) for k, x in enumerate(dense[i : i + 4])] for i in (0, 4)
    )
    grad_agg, rest[1:3] = lax.optimization_barrier((grad_agg, rest[1:3]))
    many = peers // 4
    wide = 2 * feat_out // T
    own_grad, send, *sent = call(
        functools.partial(backward_kernel, own=own, peers=peers),
        "spread",
        (me, place_back),
        [shape_of(rows, nodes, dtype=F32), shape_of(peers, half, T)]
        + [shape_of(many + wide, rows, T, dtype=F32)]
        + [shape_of(many + wide, rows, T)] * 3,
        (*grad_agg, weight),
        {4: pl.BlockSpec((per_step, slots * T, T), lambda i, me, _: (me[0] ^ i, 0, 0))},
        (parts,),
        [shape_of(sources + 1, rows, T, dtype=F32), shape_of(parts, rows, span)],
        mib=48,
        micros=30,
    )
    recv = lax.all_to_all(send, "vert", 0, 0, tiled=True)
    sent = [x if k == 0 else swap(x, "vert", 16 * k) for k, x in enumerate(sent)]
    for unit in (4, 1):
        sent = call(
            add_kernel,
            "add",
            (),
            [shape_of(unit + wide, rows, T, dtype=F32)] + [shape_of(unit + wide, rows, T)] * 3,
            sent,
            micros=30 if unit > 1 else 0,
        )
        sent = [x if k == 0 else swap(x, "vert", unit * k) for k, x in enumerate(sent)]

    grad_x, output, gself, gneigh = call(
        functools.partial(
            finish_kernel, width=2 * T, chunk=512, scale=1.0 / math.sqrt(nodes * peers)
        ),
        "finish",
        (me,),
        [
            shape_of(rows, nodes, dtype=F32),
            shape_of(rows, nodes),
            shape_of(rows, feat_out, dtype=F32),
            shape_of(rows, feat_out, dtype=F32),
        ],
        (recv, index_row, own_grad, *rest, *sent),
        scratch=[
            shape_of(rows, peers * slot_count),
            shape_of(rows * nodes // (2 * T), 2 * T, dtype=F32),
        ],
    )
    return output, grad_x, gself, gneigh


def solution(mesh):
    in_specs = (
        P("af", "vert"),
        P("af", "vert"),
        P(),
        P(),
        P("vert", None, None),
        P("vert", None),
        P("vert", None),
        P("vert"),
        P("vert", None, None, None),
    )
    out_specs = (P("af", "vert"), P("af", "vert"), P("af", None), P("af", None))
    return jax.shard_map(local, mesh=mesh, in_specs=in_specs, out_specs=out_specs, check_vma=False)
```

time: 291 us -> 198 us (0.68)
  blocking collectives: 76.1 us -> 0 us
  waiting for transfers between devices: 125 us -> 59.2 us
  starting transfers between devices: 30.4 us -> 84.8 us
  Pallas kernels: 38 us -> 34.2 us
    all_to_all x5 -> x3, waiting for transfers between devices: 125 us -> 10.4 us  [the longest x2 10.4 us: local(): recv = lax.all_to_all(send, 'vert', 0, 0, tiled=True)]
    all_to_all x4 -> x0, blocking collectives: 76.1 us -> none  [the longest x1 22.9 us: local(): gw = exchange(gw.reshape(peers, piece, T), 'vert').sum(axis=0)]
    ppermute x0 -> x27, starting transfers between devices: none -> 51.4 us  [swap(): return lax.ppermute(x, axis, [(i, i ^ mask) for i in range(size)])]
    ppermute x0 -> x27, waiting for transfers between devices: none -> 48.8 us  [swap(): return lax.ppermute(x, axis, [(i, i ^ mask) for i in range(size)])]
    pallas_call x5 -> x9, Pallas kernels: 38 us -> 34.2 us  [call(): pl.pallas_call(kernel, grid_spec=pltpu.PrefetchScalarGridSpec(num_scalar_...]
    all_to_all x5 -> x3, starting transfers between devices: 30.4 us -> 33.4 us  [the longest x2 26.6 us: local(): recv = lax.all_to_all(send, 'vert', 0, 0, tiled=True)]
    unnamed x25 -> x32, local copies, waits for them, and re-layouts: 12 us -> 9.24 us
  transfers between devices with their start and end apart: 5 -> 30, of which waited for: 5 -> 15; matrix products, arithmetic and copies ran while one was open for 1% -> 3% of each run, Pallas kernels for 4% -> 4%
where the time goes in v2:
time: 198 us; the launch traced here: 196 us
  starting transfers between devices  84.8 us (43%)
  waiting for transfers between devices  59.2 us (30%)
  Pallas kernels  34.2 us (17%)
  local copies, waits for them, and re-layouts  15.2 us (8%)
  other arithmetic  2.05 us (1%)
    ppermute x27, starting transfers between devices, swap(): return lax.ppermute(x, axis, [(i, i ^ mask) for i in range(size)])  51.4 us
    ppermute x27, waiting for transfers between devices, swap(): return lax.ppermute(x, axis, [(i, i ^ mask) for i in range(size)])  48.8 us
    pallas_call x9, Pallas kernels, call(): pl.pallas_call(kernel, grid_spec=pltpu.PrefetchScalarGridSpec(num_scalar_...  34.2 us
    all_to_all x2, starting transfers between devices, local(): recv = lax.all_to_all(send, 'vert', 0, 0, tiled=True)  26.6 us
    all_to_all x2, waiting for transfers between devices, local(): recv = lax.all_to_all(send, 'vert', 0, 0, tiled=True)  10.4 us
    unnamed x32, local copies, waits for them, and re-layouts  9.24 us
    all_to_all x1, starting transfers between devices, local(): lax.all_to_all(hub, 'vert', 0, 0, axis_index_groups=groups, tiled=True)  6.73 us
  transfers between devices with their start and end apart: 30, of which 15 were waited for; matrix products, arithmetic and copies ran while one was open for 3% of the time, Pallas kernels for 4%

profile of v2, /device:TPU:0, one launch (start us, length us, event | category | flops | bytes accessed | tf_op | source)
XLA Modules:
  0.0 196.2 jit_solution(629917533637536054)
XLA Ops:
  2.1 6.7 %all-to-all-start = ((bf16[16,64,128]{2,1,0:T(8,128)(2,1)}), bf16[16,64,128]{2,1,0:T(8,128)(2,1)S(1)}, u32[]{:S(2)}, u32[]{:S(2)}) async-start(bf16[16,64,128]{2,1,0:T(8,128)(2,1)} %broadcast_in_dim.18), calls=%async_computation | async-start | bytes 524288 | tf_op jit(solution)/shard_map/all_to_all | solution.py:328
  10.0 4.6 %collective-permute-start.1 = (bf16[64,1024]{1,0:T(8,128)(2,1)S(1)}, bf16[64,1024]{1,0:T(8,128)(2,1)S(1)}, u32[]{:S(2)}, u32[]{:S(2)}) collective-permute-start(bf16[64,1024]{1,0:T(8,128)(2,1)S(1)} %get-tuple-element.56), channel_id=1, source_target_pairs={{0,2},{1,3},{2,0},{3,1},{4,6},{5,7},{6,4},{7,5},{8,10},{9,11},{10,... | collective-permute-start | bytes 393224 | tf_op jit(solution)/shard_map/ppermute | solution.py:320
  18.6 5.1 %pick.1 = bf16[64,32,128]{2,1,0:T(8,128)(2,1)} custom-call(bf16[64,4096]{1,0:T(8,128)(2,1)S(1)} %copy-done.1, s32[1,4096]{1,0:T(1,128)S(1)} %broadcast_select_fusion.index_ref), custom_call_target="tpu_custom_call" | custom-call | flops 30000001024 | bytes 90000000 | tf_op jit(solution)/shard_map/pick/pallas_call | solution.py:274
  24.3 15.0 %all-to-all-start.1 = ((bf16[64,32,128]{2,1,0:T(8,128)(2,1)}), bf16[64,32,128]{2,1,0:T(8,128)(2,1)S(1)}, u32[]{:S(2)}, u32[]{:S(2)}) async-start(bf16[64,32,128]{2,1,0:T(8,128)(2,1)} %pick.1), calls=%async_computation.1 | async-start | bytes 1048576 | tf_op jit(solution)/shard_map/all_to_all | solution.py:362
  40.7 3.0 %collective-permute-start.8 = (bf16[16,64,128]{2,1,0:T(8,128)(2,1)S(1)}, bf16[16,64,128]{2,1,0:T(8,128)(2,1)S(1)}, u32[]{:S(2)}, u32[]{:S(2)}) collective-permute-start(bf16[16,64,128]{2,1,0:T(8,128)(2,1)S(1)} %all-to-all-done.h0), channel_id=1, source_target_pairs={{0,192},{4,196},{8,200},{12,204},{16,208},{20,212},{24,216},{28,22... | collective-permute-start | bytes 786440 | tf_op jit(solution)/shard_map/ppermute | solution.py:320
  44.8 3.6 %collective-permute-start.4 = (bf16[64,1024]{1,0:T(8,128)(2,1)}, bf16[64,1024]{1,0:T(8,128)(2,1)S(1)}, u32[]{:S(2)}, u32[]{:S(2)}) collective-permute-start(bf16[64,1024]{1,0:T(8,128)(2,1)} %get-tuple-element.60), channel_id=1, source_target_pairs={{0,2},{1,3},{2,0},{3,1},{4,6},{5,7},{6,4},{7,5},{8,10},{9,11},{10,... | collective-permute-start | bytes 393224 | tf_op jit(solution)/shard_map/ppermute | solution.py:320
  54.6 3.8 %collective-permute-done.5.refs_11_ = bf16[64,1024]{1,0:T(8,128)(2,1)} collective-permute-done((bf16[64,1024]{1,0:T(8,128)(2,1)}, bf16[64,1024]{1,0:T(8,128)(2,1)}, u32[]{:S(2)}, u32[]{:S(2)}) %collective-permute-start.5) | collective-permute-done | bytes 131104 | tf_op jit(solution)/shard_map/ppermute | solution.py:320
  58.4 10.4 %all-to-all-done.1.recv_ref = bf16[64,32,128]{2,1,0:T(8,128)(2,1)S(1)} async-done(((bf16[64,32,128]{2,1,0:T(8,128)(2,1)}), bf16[64,32,128]{2,1,0:T(8,128)(2,1)S(1)}, u32[]{:S(2)}, u32[]{:S(2)}) %all-to-all-start.1) | async-done | bytes 524320 | tf_op jit(solution)/shard_map/all_to_all | solution.py:362
  69.4 8.2 %aggregate.1 = (bf16[64,1024]{1,0:T(8,128)(2,1)S(1)}, bf16[64,1024]{1,0:T(8,128)(2,1)S(1)}, bf16[64,1024]{1,0:T(8,128)(2,1)S(1)}, bf16[64,1024]{1,0:T(8,128)(2,1)S(1)}) custom-call(s32[1]{0:T(128)} %bitcast.me_ref, s32[256]{0:T(256)S(1)} %copy-done.6, bf16[64,4096]{1,0:T(8,128)(2,1)S(1)} %copy-done.2, bf16[64,32,128]{2,1,0:T(8,128)(2,1)S(1)} %all-to-all-done.1.recv_ref, ...), custom_call_target="tpu_custom_call" | custom-call | tf_op jit(solution)/shard_map/aggregate/pallas_call | solution.py:274
  77.7 4.2 %collective-permute-start.10 = (bf16[64,1024]{1,0:T(8,128)(2,1)S(1)}, bf16[64,1024]{1,0:T(8,128)(2,1)S(1)}, u32[]{:S(2)}, u32[]{:S(2)}) collective-permute-start(bf16[64,1024]{1,0:T(8,128)(2,1)S(1)} %get-tuple-element.66), channel_id=1, source_target_pairs={{0,2},{1,3},{2,0},{3,1},{4,6},{5,7},{6,4},{7,5},{8,10},{9,11},{10,... | collective-permute-start | bytes 393224 | tf_op jit(solution)/shard_map/ppermute | solution.py:320
  83.5 7.6 %collective-permute-done.10.refs_2_ = bf16[64,1024]{1,0:T(8,128)(2,1)S(1)} collective-permute-done((bf16[64,1024]{1,0:T(8,128)(2,1)S(1)}, bf16[64,1024]{1,0:T(8,128)(2,1)S(1)}, u32[]{:S(2)}, u32[]{:S(2)}) %collective-permute-start.10) | collective-permute-done | bytes 131104 | tf_op jit(solution)/shard_map/ppermute | solution.py:320
  93.9 3.0 %dense.1 = (bf16[96,1024]{1,0:T(8,128)(2,1)S(1)}, bf16[96,1024]{1,0:T(8,128)(2,1)}, bf16[96,1024]{1,0:T(8,128)(2,1)}, bf16[96,1024]{1,0:T(8,128)(2,1)S(1)}, bf16...) custom-call(s32[1]{0:T(128)} %bitcast.me_ref, ...), custom_call_target="tpu_custom_call" | custom-call | tf_op jit(solution)/shard_map/dense/pallas_call | solution.py:274
  98.4 3.2 %collective-permute-start.16 = (bf16[128,1024]{1,0:T(8,128)(2,1)S(1)}, bf16[128,1024]{1,0:T(8,128)(2,1)S(1)}, u32[]{:S(2)}, u32[]{:S(2)}) collective-permute-start(bf16[128,1024]{1,0:T(8,128)(2,1)S(1)} %get-tuple-element.79), channel_id=1, source_target_pairs={{0,2},{1,3},{2,0},{3,1},{4,6},{5,7},{6,4},{7,5},{8,10},{9,11},{10,... | collective-permute-start | bytes 786440 | tf_op jit(solution)/shard_map/ppermute | solution.py:320
  101.7 2.8 %collective-permute-start.13 = (bf16[96,1024]{1,0:T(8,128)(2,1)}, bf16[96,1024]{1,0:T(8,128)(2,1)S(1)}, u32[]{:S(2)}, u32[]{:S(2)}) collective-permute-start(bf16[96,1024]{1,0:T(8,128)(2,1)} %get-tuple-element.76), channel_id=1, source_target_pairs={{0,2},{1,3},{2,0},{3,1},{4,6},{5,7},{6,4},{7,5},{8,10},{9,11},{10,... | collective-permute-start | bytes 589832 | tf_op jit(solution)/shard_map/ppermute | solution.py:320
  104.5 2.9 %collective-permute-start.14 = (bf16[96,1024]{1,0:T(8,128)(2,1)S(1)}, bf16[96,1024]{1,0:T(8,128)(2,1)S(1)}, u32[]{:S(2)}, u32[]{:S(2)}) collective-permute-start(bf16[96,1024]{1,0:T(8,128)(2,1)S(1)} %get-tuple-element.77), channel_id=1, source_target_pairs={{0,3},{1,2},{2,1},{3,0},{4,7},{5,6},{6,5},{7,4},{8,11},{9,10},{10,... | collective-permute-start | bytes 589832 | tf_op jit(solution)/shard_map/ppermute | solution.py:320
  108.2 15.2 %collective-permute-done.13.g2 = bf16[96,1024]{1,0:T(8,128)(2,1)S(1)} collective-permute-done((bf16[96,1024]{1,0:T(8,128)(2,1)}, bf16[96,1024]{1,0:T(8,128)(2,1)S(1)}, u32[]{:S(2)}, u32[]{:S(2)}) %collective-permute-start.13) | collective-permute-done | bytes 196640 | tf_op jit(solution)/shard_map/ppermute | solution.py:320
  123.4 4.1 %collective-permute-done.14.g3 = bf16[96,1024]{1,0:T(8,128)(2,1)S(1)} collective-permute-done((bf16[96,1024]{1,0:T(8,128)(2,1)S(1)}, bf16[96,1024]{1,0:T(8,128)(2,1)S(1)}, u32[]{:S(2)}, u32[]{:S(2)}) %collective-permute-start.14) | collective-permute-done | bytes 196640 | tf_op jit(solution)/shard_map/ppermute | solution.py:320
  130.1 10.3 %spread.1 = (f32[64,4096]{1,0:T(8,128)S(1)}, bf16[64,32,128]{2,1,0:T(8,128)(2,1)}, f32[20,64,128]{2,1,0:T(8,128)S(1)}, bf16[20,64,128]{2,1,0:T(8,128)(2,1)}, bf1...) custom-call(s32[1]{0:T(128)} %bitcast.me_ref, s32[256]{0:T(256)S(1)} %reshape.58.place_ref, ...), custom_call_target="tpu_custom_call" | custom-call | flops 30000001024 | bytes 90000000 | tf_op jit(solution)/shard_map/spread/pallas_call | solution.py:274
  148.0 11.6 %all-to-all-start.2 = ((bf16[64,32,128]{2,1,0:T(8,128)(2,1)}), bf16[64,32,128]{2,1,0:T(8,128)(2,1)S(1)}, u32[]{:S(2)}, u32[]{:S(2)}) async-start(bf16[64,32,128]{2,1,0:T(8,128)(2,1)} %get-tuple-element.84), calls=%async_computation.2 | async-start | bytes 1048576 | tf_op jit(solution)/shard_map/all_to_all | solution.py:410
  165.8 4.6 %collective-permute-start.21 = (bf16[8,64,128]{2,1,0:T(8,128)(2,1)S(1)}, bf16[8,64,128]{2,1,0:T(8,128)(2,1)S(1)}, u32[]{:S(2)}, u32[]{:S(2)}) collective-permute-start(bf16[8,64,128]{2,1,0:T(8,128)(2,1)S(1)} %get-tuple-element.95), channel_id=1, source_target_pairs={{0,16},{4,20},{8,24},{12,28},{16,0},{20,4},{24,8},{28,12},{32,48},... | collective-permute-start | bytes 393224 | tf_op jit(solution)/shard_map/ppermute | solution.py:320
  173.9 3.5 %collective-permute-done.22.two_ref = bf16[8,64,128]{2,1,0:T(8,128)(2,1)S(1)} collective-permute-done((bf16[8,64,128]{2,1,0:T(8,128)(2,1)S(1)}, bf16[8,64,128]{2,1,0:T(8,128)(2,1)S(1)}, u32[]{:S(2)}, u32[]{:S(2)}) %collective-permute-start.22) | collective-permute-done | bytes 131104 | tf_op jit(solution)/shard_map/ppermute | solution.py:320
  179.7 4.8 %collective-permute-start.25 = (bf16[5,64,128]{2,1,0:T(8,128)(2,1)S(1)}, bf16[5,64,128]{2,1,0:T(8,128)(2,1)S(1)}, u32[]{:S(2)}, u32[]{:S(2)}) collective-permute-start(bf16[5,64,128]{2,1,0:T(8,128)(2,1)S(1)} %get-tuple-element.100), channel_id=1, source_target_pairs={{0,8},{4,12},{8,0},{12,4},{16,24},{20,28},{24,16},{28,20},{32,40},... | collective-permute-start | bytes 245768 | tf_op jit(solution)/shard_map/ppermute | solution.py:320
  187.8 3.0 %collective-permute-done.26.refs_7_ = bf16[5,64,128]{2,1,0:T(8,128)(2,1)S(1)} collective-permute-done((bf16[5,64,128]{2,1,0:T(8,128)(2,1)S(1)}, bf16[5,64,128]{2,1,0:T(8,128)(2,1)S(1)}, u32[]{:S(2)}, u32[]{:S(2)}) %collective-permute-start.26) | collective-permute-done | bytes 81952 | tf_op jit(solution)/shard_map/ppermute | solution.py:320
  190.8 5.4 %finish.1 = (f32[64,4096]{1,0:T(8,128)}, bf16[64,4096]{1,0:T(8,128)(2,1)}, f32[64,256]{1,0:T(8,128)}, f32[64,256]{1,0:T(8,128)}) custom-call(s32[1]{0:T(128)} %bitcast.me_ref, bf16[64,32,128]{2,1,0:T(8,128)(2,1)S(1)} %all-to-all-done.2.recv_ref, s32[1,4096]{1,0:T(1,128)S(1)} %broadcast_select_fusion.index_ref, f32[64,4096]{1,0:T(8,128)S(1)} %get-tuple-element.85.own_ref, ...), custom_call_target="tpu_custom_call" | custom-call | tf_op jit(solution)/shard_map/finish/pallas_call | solution.py:274
  (88 shorter events, 48.7 us)
Async XLA Ops:
  2.1 22.2 %all-to-all-start = ((bf16[16,64,128]{2,1,0:T(8,128)(2,1)}), bf16[16,64,128]{2,1,0:T(8,128)(2,1)S(1)}, u32[]{:S(2)}, u32[]{:S(2)}) async-start(bf16[16,64,128]{2,1,0:T(8,128)(2,1)} %broadcast_in_dim.18), calls=%async_computation | async-start | bytes 524288 | tf_op jit(solution)/shard_map/all_to_all | solution.py:328
  9.9 13.8 %collective-permute-start = (bf16[64,1024]{1,0:T(8,128)(2,1)S(1)}, bf16[64,1024]{1,0:T(8,128)(2,1)S(1)}, u32[]{:S(2)}, u32[]{:S(2)}) collective-permute-start(bf16[64,1024]{1,0:T(8,128)(2,1)S(1)} %get-tuple-element.55), channel_id=1, source_target_pairs={{0,1},{1,0},{2,3},{3,2},{4,5},{5,4},{6,7},{7,6},{8,9},{9,8},{10,11... | collective-permute-start | bytes 393224 | tf_op jit(solution)/shard_map/ppermute | solution.py:320
  10.0 13.7 %collective-permute-start.1 = (bf16[64,1024]{1,0:T(8,128)(2,1)S(1)}, bf16[64,1024]{1,0:T(8,128)(2,1)S(1)}, u32[]{:S(2)}, u32[]{:S(2)}) collective-permute-start(bf16[64,1024]{1,0:T(8,128)(2,1)S(1)} %get-tuple-element.56), channel_id=1, source_target_pairs={{0,2},{1,3},{2,0},{3,1},{4,6},{5,7},{6,4},{7,5},{8,10},{9,11},{10,... | collective-permute-start | bytes 393224 | tf_op jit(solution)/shard_map/ppermute | solution.py:320
  14.6 9.7 %collective-permute-start.2 = (bf16[64,1024]{1,0:T(8,128)(2,1)S(1)}, bf16[64,1024]{1,0:T(8,128)(2,1)S(1)}, u32[]{:S(2)}, u32[]{:S(2)}) collective-permute-start(bf16[64,1024]{1,0:T(8,128)(2,1)S(1)} %get-tuple-element.57), channel_id=1, source_target_pairs={{0,3},{1,2},{2,1},{3,0},{4,7},{5,6},{6,5},{7,4},{8,11},{9,10},{10,... | collective-permute-start | bytes 393224 | tf_op jit(solution)/shard_map/ppermute | solution.py:320
  24.3 44.4 %all-to-all-start.1 = ((bf16[64,32,128]{2,1,0:T(8,128)(2,1)}), bf16[64,32,128]{2,1,0:T(8,128)(2,1)S(1)}, u32[]{:S(2)}, u32[]{:S(2)}) async-start(bf16[64,32,128]{2,1,0:T(8,128)(2,1)} %pick.1), calls=%async_computation.1 | async-start | bytes 1048576 | tf_op jit(solution)/shard_map/all_to_all | solution.py:362
  40.7 28.0 %collective-permute-start.8 = (bf16[16,64,128]{2,1,0:T(8,128)(2,1)S(1)}, bf16[16,64,128]{2,1,0:T(8,128)(2,1)S(1)}, u32[]{:S(2)}, u32[]{:S(2)}) collective-permute-start(bf16[16,64,128]{2,1,0:T(8,128)(2,1)S(1)} %all-to-all-done.h0), channel_id=1, source_target_pairs={{0,192},{4,196},{8,200},{12,204},{16,208},{20,212},{24,216},{28,22... | collective-permute-start | bytes 786440 | tf_op jit(solution)/shard_map/ppermute | solution.py:320
  43.7 25.0 %collective-permute-start.7 = (bf16[16,64,128]{2,1,0:T(8,128)(2,1)S(1)}, bf16[16,64,128]{2,1,0:T(8,128)(2,1)S(1)}, u32[]{:S(2)}, u32[]{:S(2)}) collective-permute-start(bf16[16,64,128]{2,1,0:T(8,128)(2,1)S(1)} %all-to-all-done.h0), channel_id=1, source_target_pairs={{0,128},{4,132},{8,136},{12,140},{16,144},{20,148},{24,152},{28,15... | collective-permute-start | bytes 786440 | tf_op jit(solution)/shard_map/ppermute | solution.py:320
  44.4 24.4 %collective-permute-start.6 = (bf16[16,64,128]{2,1,0:T(8,128)(2,1)S(1)}, bf16[16,64,128]{2,1,0:T(8,128)(2,1)S(1)}, u32[]{:S(2)}, u32[]{:S(2)}) collective-permute-start(bf16[16,64,128]{2,1,0:T(8,128)(2,1)S(1)} %all-to-all-done.h0), channel_id=1, source_target_pairs={{0,64},{4,68},{8,72},{12,76},{16,80},{20,84},{24,88},{28,92},{32,9... | collective-permute-start | bytes 786440 | tf_op jit(solution)/shard_map/ppermute | solution.py:320
  44.8 9.8 %collective-permute-start.4 = (bf16[64,1024]{1,0:T(8,128)(2,1)}, bf16[64,1024]{1,0:T(8,128)(2,1)S(1)}, u32[]{:S(2)}, u32[]{:S(2)}) collective-permute-start(bf16[64,1024]{1,0:T(8,128)(2,1)} %get-tuple-element.60), channel_id=1, source_target_pairs={{0,2},{1,3},{2,0},{3,1},{4,6},{5,7},{6,4},{7,5},{8,10},{9,11},{10,... | collective-permute-start | bytes 393224 | tf_op jit(solution)/shard_map/ppermute | solution.py:320
  48.4 9.9 %collective-permute-start.5 = (bf16[64,1024]{1,0:T(8,128)(2,1)}, bf16[64,1024]{1,0:T(8,128)(2,1)}, u32[]{:S(2)}, u32[]{:S(2)}) collective-permute-start(bf16[64,1024]{1,0:T(8,128)(2,1)} %copy-done.13), channel_id=1, source_target_pairs={{0,3},{1,2},{2,1},{3,0},{4,7},{5,6},{6,5},{7,4},{8,11},{9,10},{10,... | collective-permute-start | bytes 393224 | tf_op jit(solution)/shard_map/ppermute | solution.py:320
  77.7 13.4 %collective-permute-start.10 = (bf16[64,1024]{1,0:T(8,128)(2,1)S(1)}, bf16[64,1024]{1,0:T(8,128)(2,1)S(1)}, u32[]{:S(2)}, u32[]{:S(2)}) collective-permute-start(bf16[64,1024]{1,0:T(8,128)(2,1)S(1)} %get-tuple-element.66), channel_id=1, source_target_pairs={{0,2},{1,3},{2,0},{3,1},{4,6},{5,7},{6,4},{7,5},{8,10},{9,11},{10,... | collective-permute-start | bytes 393224 | tf_op jit(solution)/shard_map/ppermute | solution.py:320
  81.9 11.9 %collective-permute-start.11 = (bf16[64,1024]{1,0:T(8,128)(2,1)S(1)}, bf16[64,1024]{1,0:T(8,128)(2,1)S(1)}, u32[]{:S(2)}, u32[]{:S(2)}) collective-permute-start(bf16[64,1024]{1,0:T(8,128)(2,1)S(1)} %get-tuple-element.67), channel_id=1, source_target_pairs={{0,3},{1,2},{2,1},{3,0},{4,7},{5,6},{6,5},{7,4},{8,11},{9,10},{10,... | collective-permute-start | bytes 393224 | tf_op jit(solution)/shard_map/ppermute | solution.py:320
  98.3 29.9 %collective-permute-start.15 = (bf16[128,1024]{1,0:T(8,128)(2,1)S(1)}, bf16[128,1024]{1,0:T(8,128)(2,1)S(1)}, u32[]{:S(2)}, u32[]{:S(2)}) collective-permute-start(bf16[128,1024]{1,0:T(8,128)(2,1)S(1)} %get-tuple-element.78), channel_id=1, source_target_pairs={{0,1},{1,0},{2,3},{3,2},{4,5},{5,4},{6,7},{7,6},{8,9},{9,8},{10,11... | collective-permute-start | bytes 786440 | tf_op jit(solution)/shard_map/ppermute | solution.py:320
  98.4 29.8 %collective-permute-start.16 = (bf16[128,1024]{1,0:T(8,128)(2,1)S(1)}, bf16[128,1024]{1,0:T(8,128)(2,1)S(1)}, u32[]{:S(2)}, u32[]{:S(2)}) collective-permute-start(bf16[128,1024]{1,0:T(8,128)(2,1)S(1)} %get-tuple-element.79), channel_id=1, source_target_pairs={{0,2},{1,3},{2,0},{3,1},{4,6},{5,7},{6,4},{7,5},{8,10},{9,11},{10,... | collective-permute-start | bytes 786440 | tf_op jit(solution)/shard_map/ppermute | solution.py:320
  101.7 21.8 %collective-permute-start.13 = (bf16[96,1024]{1,0:T(8,128)(2,1)}, bf16[96,1024]{1,0:T(8,128)(2,1)S(1)}, u32[]{:S(2)}, u32[]{:S(2)}) collective-permute-start(bf16[96,1024]{1,0:T(8,128)(2,1)} %get-tuple-element.76), channel_id=1, source_target_pairs={{0,2},{1,3},{2,0},{3,1},{4,6},{5,7},{6,4},{7,5},{8,10},{9,11},{10,... | collective-permute-start | bytes 589832 | tf_op jit(solution)/shard_map/ppermute | solution.py:320
  104.5 23.1 %collective-permute-start.14 = (bf16[96,1024]{1,0:T(8,128)(2,1)S(1)}, bf16[96,1024]{1,0:T(8,128)(2,1)S(1)}, u32[]{:S(2)}, u32[]{:S(2)}) collective-permute-start(bf16[96,1024]{1,0:T(8,128)(2,1)S(1)} %get-tuple-element.77), channel_id=1, source_target_pairs={{0,3},{1,2},{2,1},{3,0},{4,7},{5,6},{6,5},{7,4},{8,11},{9,10},{10,... | collective-permute-start | bytes 589832 | tf_op jit(solution)/shard_map/ppermute | solution.py:320
  141.2 18.4 %collective-permute-start.18 = (bf16[20,64,128]{2,1,0:T(8,128)(2,1)}, bf16[20,64,128]{2,1,0:T(8,128)(2,1)}, u32[]{:S(2)}, u32[]{:S(2)}) collective-permute-start(bf16[20,64,128]{2,1,0:T(8,128)(2,1)} %get-tuple-element.91), channel_id=1, source_target_pairs={{0,64},{4,68},{8,72},{12,76},{16,80},{20,84},{24,88},{28,92},{32,9... | collective-permute-start | bytes 983048 | tf_op jit(solution)/shard_map/ppermute | solution.py:320
  143.1 17.9 %collective-permute-start.19 = (bf16[20,64,128]{2,1,0:T(8,128)(2,1)S(1)}, bf16[20,64,128]{2,1,0:T(8,128)(2,1)}, u32[]{:S(2)}, u32[]{:S(2)}) collective-permute-start(bf16[20,64,128]{2,1,0:T(8,128)(2,1)S(1)} %get-tuple-element.92), channel_id=1, source_target_pairs={{0,128},{4,132},{8,136},{12,140},{16,144},{20,148},{24,152},{28,15... | collective-permute-start | bytes 983048 | tf_op jit(solution)/shard_map/ppermute | solution.py:320
  145.9 17.5 %collective-permute-start.20 = (bf16[20,64,128]{2,1,0:T(8,128)(2,1)S(1)}, bf16[20,64,128]{2,1,0:T(8,128)(2,1)}, u32[]{:S(2)}, u32[]{:S(2)}) collective-permute-start(bf16[20,64,128]{2,1,0:T(8,128)(2,1)S(1)} %get-tuple-element.93), channel_id=1, source_target_pairs={{0,192},{4,196},{8,200},{12,204},{16,208},{20,212},{24,216},{28,22... | collective-permute-start | bytes 983048 | tf_op jit(solution)/shard_map/ppermute | solution.py:320
  145.9 39.9 %collective-permute-start.17 = (bf16[128,1024]{1,0:T(8,128)(2,1)S(1)}, bf16[128,1024]{1,0:T(8,128)(2,1)S(1)}, u32[]{:S(2)}, u32[]{:S(2)}) collective-permute-start(bf16[128,1024]{1,0:T(8,128)(2,1)S(1)} %copy-done.8), channel_id=1, source_target_pairs={{0,3},{1,2},{2,1},{3,0},{4,7},{5,6},{6,5},{7,4},{8,11},{9,10},{10,... | collective-permute-start | bytes 786440 | tf_op jit(solution)/shard_map/ppermute | solution.py:320
  148.0 42.8 %all-to-all-start.2 = ((bf16[64,32,128]{2,1,0:T(8,128)(2,1)}), bf16[64,32,128]{2,1,0:T(8,128)(2,1)S(1)}, u32[]{:S(2)}, u32[]{:S(2)}) async-start(bf16[64,32,128]{2,1,0:T(8,128)(2,1)} %get-tuple-element.84), calls=%async_computation.2 | async-start | bytes 1048576 | tf_op jit(solution)/shard_map/all_to_all | solution.py:410
  165.8 8.1 %collective-permute-start.21 = (bf16[8,64,128]{2,1,0:T(8,128)(2,1)S(1)}, bf16[8,64,128]{2,1,0:T(8,128)(2,1)S(1)}, u32[]{:S(2)}, u32[]{:S(2)}) collective-permute-start(bf16[8,64,128]{2,1,0:T(8,128)(2,1)S(1)} %get-tuple-element.95), channel_id=1, source_target_pairs={{0,16},{4,20},{8,24},{12,28},{16,0},{20,4},{24,8},{28,12},{32,48},... | collective-permute-start | bytes 393224 | tf_op jit(solution)/shard_map/ppermute | solution.py:320
  170.5 8.0 %collective-permute-start.23 = (bf16[8,64,128]{2,1,0:T(8,128)(2,1)S(1)}, bf16[8,64,128]{2,1,0:T(8,128)(2,1)S(1)}, u32[]{:S(2)}, u32[]{:S(2)}) collective-permute-start(bf16[8,64,128]{2,1,0:T(8,128)(2,1)S(1)} %get-tuple-element.97), channel_id=1, source_target_pairs={{0,48},{4,52},{8,56},{12,60},{16,32},{20,36},{24,40},{28,44},{32,1... | collective-permute-start | bytes 393224 | tf_op jit(solution)/shard_map/ppermute | solution.py:320
  179.7 8.2 %collective-permute-start.25 = (bf16[5,64,128]{2,1,0:T(8,128)(2,1)S(1)}, bf16[5,64,128]{2,1,0:T(8,128)(2,1)S(1)}, u32[]{:S(2)}, u32[]{:S(2)}) collective-permute-start(bf16[5,64,128]{2,1,0:T(8,128)(2,1)S(1)} %get-tuple-element.100), channel_id=1, source_target_pairs={{0,8},{4,12},{8,0},{12,4},{16,24},{20,28},{24,16},{28,20},{32,40},... | collective-permute-start | bytes 245768 | tf_op jit(solution)/shard_map/ppermute | solution.py:320
  (22 other events, 277.3 us)

commit v3 on v2

--- a/solution.py
+++ b/solution.py
@@ -31,13 +31,6 @@
     row = lax.broadcasted_iota(jnp.int16, (width, index_row.shape[1]), 0)
     low = jnp.where(index_row < 0, -1, index_row & (width - 1))
     return jnp.where(row == low.astype(jnp.int16), BF(1), BF(0))
-
-
-def split_kernel(me_ref, array_ref, *outs):
-    span = outs[0].shape[1]
-    me = me_ref[0]
-    for k, out_ref in enumerate(outs, 1):
-        out_ref[...] = array_ref[:, pl.ds(pl.multiple_of((me ^ k) * span, span), span)]
 
 
 def pick_kernel(feat_ref, index_ref, out_ref, stacked, *, width):
@@ -69,8 +62,7 @@
     lax.fori_loop(0, index_ref.shape[1] // (2 * T), body, 0, unroll=2)
 
 
-def forward_kernel(me_ref, place_ref, feat_ref, recv_ref, h0, h1, h2, h3, weight_ref, *refs):
-    outs, (source, result) = refs[:4], refs[4:]
+def forward_kernel(place_ref, feat_ref, recv_ref, h0, h1, h2, h3, weight_ref, out_ref, source):
     step = pl.program_id(0)
     rows, nodes = feat_ref.shape
     half = rows // 2
@@ -99,58 +91,67 @@
             source[first + k * many : first + (k + 1) * many] = hub_ref[...]
         source[first + peers] = jnp.zeros((rows, T), BF)
 
-    first = (me_ref[0] ^ (3 - step)) * blocks
     for j in range(blocks):
-        at = (first + j) * slots
+        at = (step * blocks + j) * slots
         picked = jnp.concatenate([source[place_ref[at + s]] for s in range(slots)], axis=1)
         total = jnp.dot(picked, weight_ref[j], preferred_element_type=F32)
-        result[:, j * T : (j + 1) * T] = total.astype(BF)
+        out_ref[:, j * T : (j + 1) * T] = total.astype(BF)
+
+
+def partial_kernel(me_ref, feat_ref, feat2_ref, agg_ref, agg2_ref, ws_ref, wn_ref, own_ref, s0, s1, stack):
+    rows, nodes = feat_ref.shape
+    me = me_ref[0]
+    mine = pl.multiple_of((me & 1) * rows, rows)
+    other = pl.multiple_of(rows - (me & 1) * rows, rows)
+    chip = pl.ds(pl.multiple_of((me >> 1) * 2 * rows, 2 * rows), 2 * rows)
+    for base, one, two in ((0, feat_ref, feat2_ref), (2 * rows, agg_ref, agg2_ref)):
+        stack[pl.ds(base + mine, rows)] = one[...]
+        stack[pl.ds(base + other, rows)] = two[...]
+    outs = [pl.ds(pl.multiple_of((me ^ k) * rows, rows), rows) for k in (0, 2)]
+    left = jnp.concatenate(
+        [jnp.concatenate([ws_ref[o, chip], wn_ref[o, chip]], axis=1) for o in outs], axis=0
+    )
+    span = nodes // 4
+    for i in range(4):
+        here = slice(i * span, (i + 1) * span)
+        part = jnp.dot(left, stack[:, here], preferred_element_type=F32)
+        own_ref[:, here] = part[:rows]
+        (s0, s1)[i // 2][:, (i % 2) * span : (i % 2 + 1) * span] = part[rows:].astype(BF)
+
+
+def act_kernel(own_ref, recv_ref, cot_ref, out_ref, grad_ref):
+    pre = own_ref[...] + recv_ref[...].astype(F32)
+    sig = jax.nn.sigmoid(pre)
+    out_ref[...] = (pre * sig).astype(BF)
+    grad_ref[...] = (cot_ref[...].astype(F32) * (sig * (1.0 + pre * (1.0 - sig)))).astype(BF)
+
+
+def back_kernel(me_ref, *refs):
+    grads, (feat_ref, agg_ref, ws_ref, wn_ref, ga_ref, dir_ref, gw_ref, stack) = refs[:8], refs[8:]
+    rows, nodes = feat_ref.shape
+    me = me_ref[0]
+    half = nodes // 2
     for k in range(4):
-
-        @pl.when(step == 3 - k)
-        def _(k=k):
-            outs[k][...] = result[...]
-
-
-def dense_kernel(me_ref, *refs):
-    aggs, feat_ref, cot_ref, feats, cots = refs[:4], refs[4], refs[5], refs[6:9], refs[9:12]
-    ws_ref, wn_ref, gas, rests = refs[12], refs[13], refs[14:18], refs[18:22]
-    agg_s, feat_s, cot_s, out_s, dir_s, gw_s = refs[22:]
-    rows = feat_ref.shape[0]
-    me = me_ref[0]
-    at = [pl.ds(pl.multiple_of((me ^ k) * rows, rows), rows) for k in range(4)]
-    feat_s[at[0]] = feat_ref[...]
-    cot_s[at[0]] = cot_ref[...]
-    for k in range(4):
-        agg_s[at[k]] = aggs[k][...]
-        if k:
-            feat_s[at[k]] = feats[k - 1][...]
-            cot_s[at[k]] = cots[k - 1][...]
-    agg = agg_s[...]
-    feat = feat_s[...]
-    ws = ws_ref[...]
-    wn = wn_ref[...]
-    pre = lax.dot_general(ws, feat, FIRST, preferred_element_type=F32)
-    pre += lax.dot_general(wn, agg, FIRST, preferred_element_type=F32)
-    sig = jax.nn.sigmoid(pre)
-    out_s[...] = (pre * sig).astype(BF)
-    grad = (cot_s[...].astype(F32) * (sig * (1.0 + pre * (1.0 - sig)))).astype(BF)
-    agg_s[...] = jnp.dot(wn, grad, preferred_element_type=F32).astype(BF)
-    dir_s[...] = jnp.dot(ws, grad, preferred_element_type=F32).astype(BF)
-    wide = ws.shape[1]
-    gw_s[:, :wide] = lax.dot_general(feat, grad, LAST, preferred_element_type=F32).astype(BF)
-    gw_s[:, wide:] = lax.dot_general(agg, grad, LAST, preferred_element_type=F32).astype(BF)
-    for k in range(4):
-        gas[k][:rows] = agg_s[at[k]]
-        mine = gw_s[at[k]]
-        gas[k][rows:, : 2 * wide] = mine[: rows // 2]
-        gas[k][rows:, 2 * wide :] = mine[rows // 2 :]
-        rests[k][:rows] = out_s[at[k]]
-        rests[k][rows:] = dir_s[at[k]]
-
-
-def backward_kernel(me_ref, place_ref, g0, g1, g2, g3, weight_ref, *refs, own, peers):
-    own_ref, send_ref, hub0, hub1, hub2, hub3, total, grads = refs
+        at = pl.ds(pl.multiple_of((me ^ k) * rows, rows), rows)
+        for h in range(2):
+            stack[at, h * half : (h + 1) * half] = grads[2 * k + h][...]
+    mine = pl.ds(pl.multiple_of(me * rows, rows), rows)
+    span = nodes // 4
+    gself = gneigh = 0.0
+    for i in range(4):
+        here = slice(i * span, (i + 1) * span)
+        grad = stack[:, here]
+        ga_ref[:, here] = jnp.dot(wn_ref[mine], grad, preferred_element_type=F32).astype(BF)
+        dir_ref[:, here] = jnp.dot(ws_ref[mine], grad, preferred_element_type=F32)
+        gself += lax.dot_general(feat_ref[:, here], grad, LAST, preferred_element_type=F32)
+        gneigh += lax.dot_general(agg_ref[:, here], grad, LAST, preferred_element_type=F32)
+    wide = gself.shape[1]
+    gw_ref[:, :wide] = gself
+    gw_ref[:, wide:] = gneigh
+
+
+def backward_kernel(place_ref, ga_ref, dir_ref, gw_ref, weight_ref, *refs, own, peers):
+    own_ref, send_ref, hub0, hub1, hub2, hub3, total = refs
     step = pl.program_id(0)
     rows = own_ref.shape[0]
     half = rows // 2
@@ -160,14 +161,11 @@
     @pl.when(step == 0)
     def _():
         total[...] = jnp.zeros_like(total)
-        for k, grad_ref in enumerate((g0, g1, g2, g3)):
-            grads[k] = grad_ref[:rows]
-
-    first = (me_ref[0] ^ step) * blocks
+
     for j in range(blocks):
-        at = (first + j) * slots
+        at = (step * blocks + j) * slots
         part = lax.dot_general(
-            grads[step, :, j * T : (j + 1) * T], weight_ref[j], LAST, preferred_element_type=F32
+            ga_ref[:, j * T : (j + 1) * T], weight_ref[j], LAST, preferred_element_type=F32
         )
         for s in range(slots):
             total[place_ref[at + s]] += part[:, s * T : (s + 1) * T]
@@ -176,7 +174,7 @@
     def _():
         low = low_lanes(half)
         for i in range(own):
-            own_ref[:, i * T : (i + 1) * T] = total[i]
+            own_ref[:, i * T : (i + 1) * T] = total[i] + dir_ref[:, i * T : (i + 1) * T]
 
         def pair(t, carry):
             top = total[own + t, :half]
@@ -190,35 +188,27 @@
         for k, hub_ref in enumerate((hub0, hub1, hub2, hub3)):
             start = own + peers // 2 + k * many
             hub_ref[:many] = total[start : start + many].astype(hub_ref.dtype)
-        wide = g0.shape[1] // 2
-        for u in range(2):
-            here = slice(u * wide, (u + 1) * wide)
-            g = [x[rows:, here].astype(F32) for x in (g0, g1, g2, g3)]
-            gw = ((g[0] + g[1]) + (g[2] + g[3])).astype(BF)
-            for c in range(wide // T):
-                part = gw[:, c * T : (c + 1) * T]
-                for hub_ref in (hub0, hub1, hub2, hub3):
-                    hub_ref[many + c, u * half : (u + 1) * half] = part.astype(hub_ref.dtype)
-
-
-def finish_kernel(me_ref, recv_ref, index_ref, own_ref, *refs, width, chunk, scale):
-    rests, hubs = refs[:4], refs[4:8]
-    grad_ref, out_ref, gself_ref, gneigh_ref, slots_ref, acc_ref = refs[8:]
+        for c in range(gw_ref.shape[1] // T):
+            part = gw_ref[:, c * T : (c + 1) * T].astype(BF)
+            for hub_ref in (hub0, hub1, hub2, hub3):
+                hub_ref[many + c] = part.astype(hub_ref.dtype)
+
+
+def finish_kernel(recv_ref, index_ref, own_ref, out0, out1, *refs, width, chunk, scale):
+    hubs = refs[:4]
+    grad_ref, out_ref, gself_ref, gneigh_ref, slots_ref, acc_ref = refs[4:]
     rows, nodes = own_ref.shape
     half = rows // 2
     peers = recv_ref.shape[0]
-    span = rests[0].shape[1]
     low = low_lanes(half)
-    me = me_ref[0]
     for t in range(peers // 2):
         a = recv_ref[2 * t].astype(F32)
         b = recv_ref[2 * t + 1].astype(F32)
         slots_ref[:half, t * T : (t + 1) * T] = jnp.where(low, a, swap_halves(b)).astype(BF)
         slots_ref[half:, t * T : (t + 1) * T] = jnp.where(low, swap_halves(a), b).astype(BF)
-    for k in range(4):
-        here = pl.ds(pl.multiple_of((me ^ k) * span, span), span)
-        grad_ref[:, here] = own_ref[:, here] + rests[k][rows:].astype(F32)
-        out_ref[:, here] = rests[k][:rows]
+    out_ref[:, : nodes // 2] = out0[...]
+    out_ref[:, nodes // 2 :] = out1[...]
+    grad_ref[...] = own_ref[...]
     many = nodes // width
     acc_ref[...] = jnp.zeros_like(acc_ref)
 
@@ -269,7 +259,7 @@
     return jax.ShapeDtypeStruct(shape, dtype)
 
 
-def call(kernel, name, prefetch, out_shape, operands, in_specs=None, grid=(1,), scratch=(), mib=24, micros=0):
+def call(kernel, name, prefetch, out_shape, operands, in_specs=None, grid=(1,), scratch=(), mib=24, micros=0, out_specs=None):
     in_specs = in_specs or {}
     return pl.pallas_call(
         kernel,
@@ -277,7 +267,7 @@
             num_scalar_prefetch=len(prefetch),
             grid=grid,
             in_specs=[in_specs.get(i) or whole(x.shape) for i, x in enumerate(operands)],
-            out_specs=[whole(s.shape) for s in out_shape],
+            out_specs=out_specs or [whole(s.shape) for s in out_shape],
             scratch_shapes=[pltpu.VMEM(s.shape, s.dtype) for s in scratch],
         ),
         out_shape=tuple(out_shape),
@@ -327,12 +317,7 @@
     hub = jnp.broadcast_to(features[None, :, :T], (plane, rows, T))
     hub = lax.all_to_all(hub, "vert", 0, 0, axis_index_groups=groups, tiled=True)
 
-    def split(x):
-        parts_out = call(split_kernel, "split", (me,), [shape_of(rows, span)] * 3, (x,))
-        return [swap(part, "af", k) for k, part in enumerate(parts_out, 1)]
-
-    feats = split(features)
-    cots = split(cotangent)
+    features2 = swap(features, "af", 1)
 
     slot_live = lax.broadcasted_iota(jnp.int32, (peers, slot_count), 1) < send_count.reshape(
         peers, 1
@@ -357,53 +342,77 @@
         micros=30,
         scratch=[shape_of(rows * nodes // (2 * T), 2 * T)],
     )
-    send, hub, feats = lax.optimization_barrier((send, hub, feats))
+    send, hub, features2 = lax.optimization_barrier((send, hub, features2))
     hubs = [hub] + swap3(hub, "vert", 16)
     recv = lax.all_to_all(send, "vert", 0, 0, tiled=True)
-    recv, cots = lax.optimization_barrier((recv, cots))
-
-    agg = call(
+
+    blocked = pl.BlockSpec((per_step, slots * T, T), lambda i, place: (i, 0, 0))
+    (agg,) = call(
         forward_kernel,
         "aggregate",
-        (me, place),
-        [shape_of(rows, span)] * 4,
+        (place,),
+        [shape_of(rows, nodes)],
         (features, recv, *hubs, weight),
-        {6: pl.BlockSpec((per_step, slots * T, T), lambda i, me, _: (me[0] ^ (3 - i), 0, 0))},
+        {6: blocked},
         (parts,),
-        [shape_of(sources + 1, rows, T), shape_of(rows, span)],
+        [shape_of(sources + 1, rows, T)],
         mib=48,
-    )
-    agg = [x if k == 0 else swap(x, "af", k) for k, x in enumerate(agg)]
-
-    mine = pl.BlockSpec((rows, span), lambda i, me: (0, me[0]))
-    full = shape_of(parts * rows, span)
-    dense = call(
-        dense_kernel,
-        "dense",
+        out_specs=[pl.BlockSpec((rows, span), lambda i, place: (0, i))],
+    )
+    agg2 = swap(agg, "af", 1)
+
+    pre, *shares = call(
+        partial_kernel,
+        "partial",
         (me,),
-        [shape_of(rows + half, span)] * 4 + [shape_of(2 * rows, span)] * 4,
-        (*agg, features, cotangent, *feats, *cots, w_self, w_neigh),
-        {4: mine, 5: mine},
-        scratch=[full] * 5 + [shape_of(parts * rows, 2 * feat_out)],
-        mib=32,
-    )
-    grad_agg, rest = (
-        [x if k == 0 else swap(x, "af", k) for k, x in enumerate(dense[i : i + 4])] for i in (0, 4)
-    )
-    grad_agg, rest[1:3] = lax.optimization_barrier((grad_agg, rest[1:3]))
+        [shape_of(rows, nodes, dtype=F32)] + [shape_of(rows, nodes // 2)] * 2,
+        (features, features2, agg, agg2, w_self.T, w_neigh.T),
+        scratch=[shape_of(parts * rows, nodes)],
+    )
+    shares = [swap(x, "af", 2) for x in shares]
+    outs, grads = [], []
+    for h in range(2):
+        column = pl.BlockSpec((rows, nodes // 2), functools.partial(lambda h, i: (0, h), h))
+        out, grad = call(
+            act_kernel,
+            "act",
+            (),
+            [shape_of(rows, nodes // 2)] * 2,
+            (pre, shares[h], cotangent),
+            {0: column, 2: column},
+        )
+        outs.append(out)
+        grads.append(grad)
+    far = [swap(x, "af", 2) for x in grads]
+    near = [swap(x, "af", 1) for x in grads]
+    diagonal = [swap(x, "af", 1) for x in far]
+
+    grad_agg, direct, gw = call(
+        back_kernel,
+        "back",
+        (me,),
+        [
+            shape_of(rows, nodes),
+            shape_of(rows, nodes, dtype=F32),
+            shape_of(rows, 2 * feat_out, dtype=F32),
+        ],
+        (*grads, *near, *far, *diagonal, features, agg, w_self, w_neigh),
+        scratch=[shape_of(parts * rows, nodes)],
+    )
+
     many = peers // 4
     wide = 2 * feat_out // T
     own_grad, send, *sent = call(
         functools.partial(backward_kernel, own=own, peers=peers),
         "spread",
-        (me, place_back),
+        (place_back,),
         [shape_of(rows, nodes, dtype=F32), shape_of(peers, half, T)]
         + [shape_of(many + wide, rows, T, dtype=F32)]
         + [shape_of(many + wide, rows, T)] * 3,
-        (*grad_agg, weight),
-        {4: pl.BlockSpec((per_step, slots * T, T), lambda i, me, _: (me[0] ^ i, 0, 0))},
+        (grad_agg, direct, gw, weight),
+        {0: pl.BlockSpec((rows, span), lambda i, place: (0, i)), 3: blocked},
         (parts,),
-        [shape_of(sources + 1, rows, T, dtype=F32), shape_of(parts, rows, span)],
+        [shape_of(sources + 1, rows, T, dtype=F32)],
         mib=48,
         micros=30,
     )
@@ -425,14 +434,14 @@
             finish_kernel, width=2 * T, chunk=512, scale=1.0 / math.sqrt(nodes * peers)
         ),
         "finish",
-        (me,),
+        (),
         [
             shape_of(rows, nodes, dtype=F32),
             shape_of(rows, nodes),
             shape_of(rows, feat_out, dtype=F32),
             shape_of(rows, feat_out, dtype=F32),
         ],
-        (recv, index_row, own_grad, *rest, *sent),
+        (recv, index_row, own_grad, *outs, *sent),
         scratch=[
             shape_of(rows, peers * slot_count),
             shape_of(rows * nodes // (2 * T), 2 * T, dtype=F32),

time: 198 us -> 186 us (0.939)
  waiting for transfers between devices: 59.2 us -> 51.9 us
  local copies, waits for them, and re-layouts: 15.2 us -> 9.22 us
    all_to_all x2, waiting for transfers between devices: 10.4 us -> 0.01 us  [local(): recv = lax.all_to_all(send, 'vert', 0, 0, tiled=True)]
    all_to_all x2, starting transfers between devices: 26.6 us -> 35.3 us  [local(): recv = lax.all_to_all(send, 'vert', 0, 0, tiled=True)]
    ppermute x27 -> x22, starting transfers between devices: 51.4 us -> 44.4 us  [swap(): return lax.ppermute(x, axis, [(i, i ^ mask) for i in range(size)])]
    all_to_all x1, waiting for transfers between devices: 0.01 us -> 3.67 us  [local(): lax.all_to_all(hub, 'vert', 0, 0, axis_index_groups=groups, tiled=True)]
    unnamed x32 -> x28, local copies, waits for them, and re-layouts: 9.24 us -> 6.48 us
    ppermute x27 -> x22, waiting for transfers between devices: 48.8 us -> 48.2 us  [swap(): return lax.ppermute(x, axis, [(i, i ^ mask) for i in range(size)])]
    pallas_call x9 -> x10, Pallas kernels: 34.2 us -> 34.6 us  [call(): pl.pallas_call(kernel, grid_spec=pltpu.PrefetchScalarGridSpec(num_scalar_...]
  transfers between devices with their start and end apart: 30 -> 25, of which waited for: 15 -> 13; matrix products, arithmetic and copies ran while one was open for 3% -> 2% of each run, Pallas kernels for 4% -> 4%
where the time goes in v3:
time: 186 us; the launch traced here: 184 us
  starting transfers between devices  86.4 us (46%)
  waiting for transfers between devices  51.9 us (28%)
  Pallas kernels  34.6 us (19%)
  local copies, waits for them, and re-layouts  9.22 us (5%)
    ppermute x22, waiting for transfers between devices, swap(): return lax.ppermute(x, axis, [(i, i ^ mask) for i in range(size)])  48.2 us
    ppermute x22, starting transfers between devices, swap(): return lax.ppermute(x, axis, [(i, i ^ mask) for i in range(size)])  44.4 us
    all_to_all x2, starting transfers between devices, local(): recv = lax.all_to_all(send, 'vert', 0, 0, tiled=True)  35.3 us
    pallas_call x10, Pallas kernels, call(): pl.pallas_call(kernel, grid_spec=pltpu.PrefetchScalarGridSpec(num_scalar_...  34.6 us
    all_to_all x1, starting transfers between devices, local(): lax.all_to_all(hub, 'vert', 0, 0, axis_index_groups=groups, tiled=True)  6.73 us
    unnamed x28, local copies, waits for them, and re-layouts  6.48 us
  transfers between devices with their start and end apart: 25, of which 13 were waited for; matrix products, arithmetic and copies ran while one was open for 2% of the time, Pallas kernels for 4%

profile of v3, /device:TPU:0, one launch (start us, length us, event | category | flops | bytes accessed | tf_op | source)
XLA Modules:
  0.0 183.8 jit_solution(7197900245823405282)
XLA Ops:
  2.2 6.7 %all-to-all-start = ((bf16[16,64,128]{2,1,0:T(8,128)(2,1)}), bf16[16,64,128]{2,1,0:T(8,128)(2,1)S(1)}, u32[]{:S(2)}, u32[]{:S(2)}) async-start(bf16[16,64,128]{2,1,0:T(8,128)(2,1)} %broadcast_in_dim.18), calls=%async_computation | async-start | bytes 524288 | tf_op jit(solution)/shard_map/all_to_all | solution.py:318
  11.7 5.1 %pick.1 = bf16[64,32,128]{2,1,0:T(8,128)(2,1)} custom-call(bf16[64,4096]{1,0:T(8,128)(2,1)S(1)} %copy-done, s32[1,4096]{1,0:T(1,128)S(1)} %broadcast_select_fusion.index_ref), custom_call_target="tpu_custom_call" | custom-call | flops 30000001024 | bytes 90000000 | tf_op jit(solution)/shard_map/pick/pallas_call | solution.py:264
  16.8 3.7 %all-to-all-done.h0 = bf16[16,64,128]{2,1,0:T(8,128)(2,1)S(1)} async-done(((bf16[16,64,128]{2,1,0:T(8,128)(2,1)}), bf16[16,64,128]{2,1,0:T(8,128)(2,1)S(1)}, u32[]{:S(2)}, u32[]{:S(2)}) %all-to-all-start) | async-done | bytes 262176 | tf_op jit(solution)/shard_map/all_to_all | solution.py:318
  20.5 7.5 %all-to-all-start.1 = ((bf16[64,32,128]{2,1,0:T(8,128)(2,1)}), bf16[64,32,128]{2,1,0:T(8,128)(2,1)S(1)}, u32[]{:S(2)}, u32[]{:S(2)}) async-start(bf16[64,32,128]{2,1,0:T(8,128)(2,1)} %pick.1), calls=%async_computation.1 | async-start | bytes 1048576 | tf_op jit(solution)/shard_map/all_to_all | solution.py:347
  28.0 3.1 %collective-permute-start.3 = (bf16[16,64,128]{2,1,0:T(8,128)(2,1)S(1)}, bf16[16,64,128]{2,1,0:T(8,128)(2,1)S(1)}, u32[]{:S(2)}, u32[]{:S(2)}) collective-permute-start(bf16[16,64,128]{2,1,0:T(8,128)(2,1)S(1)} %all-to-all-done.h0), channel_id=1, source_target_pairs={{0,192},{4,196},{8,200},{12,204},{16,208},{20,212},{24,216},{28,22... | collective-permute-start | bytes 786440 | tf_op jit(solution)/shard_map/ppermute | solution.py:310
  32.4 15.9 %collective-permute-done.3.h3 = bf16[16,64,128]{2,1,0:T(8,128)(2,1)S(1)} collective-permute-done((bf16[16,64,128]{2,1,0:T(8,128)(2,1)S(1)}, bf16[16,64,128]{2,1,0:T(8,128)(2,1)S(1)}, u32[]{:S(2)}, u32[]{:S(2)}) %collective-permute-start.3) | collective-permute-done | bytes 262176 | tf_op jit(solution)/shard_map/ppermute | solution.py:310
  51.7 8.1 %aggregate.1.agg_ref.refs_9_ = bf16[64,4096]{1,0:T(8,128)(2,1)S(1)} custom-call(s32[256]{0:T(256)S(1)} %reshape.59.place_ref, bf16[64,4096]{1,0:T(8,128)(2,1)S(1)} %copy-done.1, bf16[64,32,128]{2,1,0:T(8,128)(2,1)S(1)} %all-to-all-done.1.recv_ref, bf16[16,64,128]{2,1,0:T(8,128)(2,1)S(1)} %all-to-all-done.h0, bf16[16,64,128]{2,1,0:T(8,128)(2,1)S(1)} %copy-done.8, ...), custom_call_target="tpu_custom_call" | custom-call | tf_op jit(solution)/shard_map/aggregate/pallas_call | solution.py:264
  62.6 4.6 %collective-permute-start.5 = (bf16[64,2048]{1,0:T(8,128)(2,1)S(1)}, bf16[64,2048]{1,0:T(8,128)(2,1)S(1)}, u32[]{:S(2)}, u32[]{:S(2)}) collective-permute-start(bf16[64,2048]{1,0:T(8,128)(2,1)S(1)} %get-tuple-element.39), channel_id=1, source_target_pairs={{0,2},{1,3},{2,0},{3,1},{4,6},{5,7},{6,4},{7,5},{8,10},{9,11},{10,... | collective-permute-start | bytes 786440 | tf_op jit(solution)/shard_map/ppermute | solution.py:310
  68.6 7.6 %collective-permute-done.5.recv_ref = bf16[64,2048]{1,0:T(8,128)(2,1)S(1)} collective-permute-done((bf16[64,2048]{1,0:T(8,128)(2,1)S(1)}, bf16[64,2048]{1,0:T(8,128)(2,1)S(1)}, u32[]{:S(2)}, u32[]{:S(2)}) %collective-permute-start.5) | collective-permute-done | bytes 262176 | tf_op jit(solution)/shard_map/ppermute | solution.py:310
  76.5 4.7 %collective-permute-start.9 = (bf16[64,2048]{1,0:T(8,128)(2,1)S(1)}, bf16[64,2048]{1,0:T(8,128)(2,1)S(1)}, u32[]{:S(2)}, u32[]{:S(2)}) collective-permute-start(bf16[64,2048]{1,0:T(8,128)(2,1)S(1)} %get-tuple-element.40.refs_0_), channel_id=1, source_target_pairs={{0,2},{1,3},{2,0},{3,1},{4,6},{5,7},{6,4},{7,5},{8,10},{9,11},{10,... | collective-permute-start | bytes 786440 | tf_op jit(solution)/shard_map/ppermute | solution.py:310
  81.7 4.8 %collective-permute-start.10 = (bf16[64,2048]{1,0:T(8,128)(2,1)S(1)}, bf16[64,2048]{1,0:T(8,128)(2,1)S(1)}, u32[]{:S(2)}, u32[]{:S(2)}) collective-permute-start(bf16[64,2048]{1,0:T(8,128)(2,1)S(1)} %get-tuple-element.42.refs_1_), channel_id=1, source_target_pairs={{0,2},{1,3},{2,0},{3,1},{4,6},{5,7},{6,4},{7,5},{8,10},{9,11},{10,... | collective-permute-start | bytes 786440 | tf_op jit(solution)/shard_map/ppermute | solution.py:310
  87.7 6.4 %collective-permute-done.10.refs_5_ = bf16[64,2048]{1,0:T(8,128)(2,1)S(1)} collective-permute-done((bf16[64,2048]{1,0:T(8,128)(2,1)S(1)}, bf16[64,2048]{1,0:T(8,128)(2,1)S(1)}, u32[]{:S(2)}, u32[]{:S(2)}) %collective-permute-start.10) | collective-permute-done | bytes 262176 | tf_op jit(solution)/shard_map/ppermute | solution.py:310
  95.8 3.3 %back.1 = (bf16[64,4096]{1,0:T(8,128)(2,1)S(1)}, f32[64,4096]{1,0:T(8,128)S(1)}, f32[64,512]{1,0:T(8,128)S(1)}) custom-call(s32[1]{0:T(128)} %bitcast.me_ref, bf16[64,2048]{1,0:T(8,128)(2,1)S(1)} %get-tuple-element.40.refs_0_, bf16[64,2048]{1,0:T(8,128)(2,1)S(1)} %get-tuple-element.42.refs_1_, bf16[64,2048]{1,0:T(8,128)(2,1)S(1)} %collective-permute-done.7.refs_2_, ...), custom_call_target="tpu_custom_call" | custom-call | tf_op jit(solution)/shard_map/back/pallas_call | solution.py:264
  99.1 10.3 %spread.1 = (f32[64,4096]{1,0:T(8,128)S(1)}, bf16[64,32,128]{2,1,0:T(8,128)(2,1)}, f32[20,64,128]{2,1,0:T(8,128)S(1)}, bf16[20,64,128]{2,1,0:T(8,128)(2,1)}, bf1...) custom-call(s32[256]{0:T(256)S(1)} %reshape.57.place_ref, bf16[64,4096]{1,0:T(8,128)(2,1)S(1)} %get-tuple-element.43.ga_ref, ...), custom_call_target="tpu_custom_call" | custom-call | flops 30000001024 | bytes 90000000 | tf_op jit(solution)/shard_map/spread/pallas_call | solution.py:264
  110.5 5.2 %collective-permute-start.14 = (bf16[20,64,128]{2,1,0:T(8,128)(2,1)S(1)}, bf16[20,64,128]{2,1,0:T(8,128)(2,1)S(1)}, u32[]{:S(2)}, u32[]{:S(2)}) collective-permute-start(bf16[20,64,128]{2,1,0:T(8,128)(2,1)S(1)} %get-tuple-element.52), channel_id=1, source_target_pairs={{0,128},{4,132},{8,136},{12,140},{16,144},{20,148},{24,152},{28,15... | collective-permute-start | bytes 983048 | tf_op jit(solution)/shard_map/ppermute | solution.py:310
  115.7 27.8 %all-to-all-start.2 = ((bf16[64,32,128]{2,1,0:T(8,128)(2,1)}), bf16[64,32,128]{2,1,0:T(8,128)(2,1)S(1)}, u32[]{:S(2)}, u32[]{:S(2)}) async-start(bf16[64,32,128]{2,1,0:T(8,128)(2,1)} %get-tuple-element.46), calls=%async_computation.2 | async-start | bytes 1048576 | tf_op jit(solution)/shard_map/all_to_all | solution.py:419
  147.4 2.7 %collective-permute-start.17 = (bf16[8,64,128]{2,1,0:T(8,128)(2,1)S(1)}, bf16[8,64,128]{2,1,0:T(8,128)(2,1)S(1)}, u32[]{:S(2)}, u32[]{:S(2)}) collective-permute-start(bf16[8,64,128]{2,1,0:T(8,128)(2,1)S(1)} %get-tuple-element.56), channel_id=1, source_target_pairs={{0,32},{4,36},{8,40},{12,44},{16,48},{20,52},{24,56},{28,60},{32,0... | collective-permute-start | bytes 393224 | tf_op jit(solution)/shard_map/ppermute | solution.py:310
  150.5 2.8 %collective-permute-done.16.one_ref = bf16[8,64,128]{2,1,0:T(8,128)(2,1)S(1)} collective-permute-done((bf16[8,64,128]{2,1,0:T(8,128)(2,1)S(1)}, bf16[8,64,128]{2,1,0:T(8,128)(2,1)S(1)}, u32[]{:S(2)}, u32[]{:S(2)}) %collective-permute-start.16) | collective-permute-done | bytes 131104 | tf_op jit(solution)/shard_map/ppermute | solution.py:310
  153.3 4.4 %collective-permute-done.17.two_ref = bf16[8,64,128]{2,1,0:T(8,128)(2,1)S(1)} collective-permute-done((bf16[8,64,128]{2,1,0:T(8,128)(2,1)S(1)}, bf16[8,64,128]{2,1,0:T(8,128)(2,1)S(1)}, u32[]{:S(2)}, u32[]{:S(2)}) %collective-permute-start.17) | collective-permute-done | bytes 131104 | tf_op jit(solution)/shard_map/ppermute | solution.py:310
  157.7 1.7 collective-permute-done.18.three_ref
  159.5 7.5 %collective-permute-start.19 = (bf16[5,64,128]{2,1,0:T(8,128)(2,1)S(1)}, bf16[5,64,128]{2,1,0:T(8,128)(2,1)S(1)}, u32[]{:S(2)}, u32[]{:S(2)}) collective-permute-start(bf16[5,64,128]{2,1,0:T(8,128)(2,1)S(1)} %get-tuple-element.59), channel_id=1, source_target_pairs={{0,4},{4,0},{8,12},{12,8},{16,20},{20,16},{24,28},{28,24},{32,36},... | collective-permute-start | bytes 245768 | tf_op jit(solution)/shard_map/ppermute | solution.py:310
  167.1 5.0 %collective-permute-start.20 = (bf16[5,64,128]{2,1,0:T(8,128)(2,1)S(1)}, bf16[5,64,128]{2,1,0:T(8,128)(2,1)S(1)}, u32[]{:S(2)}, u32[]{:S(2)}) collective-permute-start(bf16[5,64,128]{2,1,0:T(8,128)(2,1)S(1)} %get-tuple-element.60), channel_id=1, source_target_pairs={{0,8},{4,12},{8,0},{12,4},{16,24},{20,28},{24,16},{28,20},{32,40},... | collective-permute-start | bytes 245768 | tf_op jit(solution)/shard_map/ppermute | solution.py:310
  174.5 3.9 %collective-permute-done.21.refs_3_ = bf16[5,64,128]{2,1,0:T(8,128)(2,1)S(1)} collective-permute-done((bf16[5,64,128]{2,1,0:T(8,128)(2,1)S(1)}, bf16[5,64,128]{2,1,0:T(8,128)(2,1)S(1)}, u32[]{:S(2)}, u32[]{:S(2)}) %collective-permute-start.21) | collective-permute-done | bytes 81952 | tf_op jit(solution)/shard_map/ppermute | solution.py:310
  178.4 5.4 %finish.1 = (f32[64,4096]{1,0:T(8,128)}, bf16[64,4096]{1,0:T(8,128)(2,1)}, f32[64,256]{1,0:T(8,128)}, f32[64,256]{1,0:T(8,128)}) custom-call(bf16[64,32,128]{2,1,0:T(8,128)(2,1)S(1)} %all-to-all-done.2.recv_ref, s32[1,4096]{1,0:T(1,128)S(1)} %broadcast_select_fusion.index_ref, f32[64,4096]{1,0:T(8,128)S(1)} %get-tuple-element.47.own_ref, ...), custom_call_target="tpu_custom_call" | custom-call | tf_op jit(solution)/shard_map/finish/pallas_call | solution.py:264
  (75 shorter events, 24.6 us)
Async XLA Ops:
  0.6 19.9 %collective-permute-start = (bf16[64,4096]{1,0:T(8,128)(2,1)}, bf16[64,4096]{1,0:T(8,128)(2,1)S(1)}, u32[]{:S(2)}, u32[]{:S(2)}) collective-permute-start(bf16[64,4096]{1,0:T(8,128)(2,1)} %refs_8_.1), channel_id=1, source_target_pairs={{0,1},{1,0},{2,3},{3,2},{4,5},{5,4},{6,7},{7,6},{8,9},{9,8},{10,11... | collective-permute-start | bytes 1572872 | tf_op jit(solution)/shard_map/ppermute | solution.py:310
  2.2 18.3 %all-to-all-start = ((bf16[16,64,128]{2,1,0:T(8,128)(2,1)}), bf16[16,64,128]{2,1,0:T(8,128)(2,1)S(1)}, u32[]{:S(2)}, u32[]{:S(2)}) async-start(bf16[16,64,128]{2,1,0:T(8,128)(2,1)} %broadcast_in_dim.18), calls=%async_computation | async-start | bytes 524288 | tf_op jit(solution)/shard_map/all_to_all | solution.py:318
  20.5 29.3 %all-to-all-start.1 = ((bf16[64,32,128]{2,1,0:T(8,128)(2,1)}), bf16[64,32,128]{2,1,0:T(8,128)(2,1)S(1)}, u32[]{:S(2)}, u32[]{:S(2)}) async-start(bf16[64,32,128]{2,1,0:T(8,128)(2,1)} %pick.1), calls=%async_computation.1 | async-start | bytes 1048576 | tf_op jit(solution)/shard_map/all_to_all | solution.py:347
  28.0 20.3 %collective-permute-start.3 = (bf16[16,64,128]{2,1,0:T(8,128)(2,1)S(1)}, bf16[16,64,128]{2,1,0:T(8,128)(2,1)S(1)}, u32[]{:S(2)}, u32[]{:S(2)}) collective-permute-start(bf16[16,64,128]{2,1,0:T(8,128)(2,1)S(1)} %all-to-all-done.h0), channel_id=1, source_target_pairs={{0,192},{4,196},{8,200},{12,204},{16,208},{20,212},{24,216},{28,22... | collective-permute-start | bytes 786440 | tf_op jit(solution)/shard_map/ppermute | solution.py:310
  31.1 17.2 %collective-permute-start.2 = (bf16[16,64,128]{2,1,0:T(8,128)(2,1)S(1)}, bf16[16,64,128]{2,1,0:T(8,128)(2,1)S(1)}, u32[]{:S(2)}, u32[]{:S(2)}) collective-permute-start(bf16[16,64,128]{2,1,0:T(8,128)(2,1)S(1)} %all-to-all-done.h0), channel_id=1, source_target_pairs={{0,128},{4,132},{8,136},{12,140},{16,144},{20,148},{24,152},{28,15... | collective-permute-start | bytes 786440 | tf_op jit(solution)/shard_map/ppermute | solution.py:310
  31.8 17.3 %collective-permute-start.1 = (bf16[16,64,128]{2,1,0:T(8,128)(2,1)S(1)}, bf16[16,64,128]{2,1,0:T(8,128)(2,1)S(1)}, u32[]{:S(2)}, u32[]{:S(2)}) collective-permute-start(bf16[16,64,128]{2,1,0:T(8,128)(2,1)S(1)} %all-to-all-done.h0), channel_id=1, source_target_pairs={{0,64},{4,68},{8,72},{12,76},{16,80},{20,84},{24,88},{28,92},{32,9... | collective-permute-start | bytes 786440 | tf_op jit(solution)/shard_map/ppermute | solution.py:310
  59.8 2.0 %collective-permute-start.4 = (bf16[64,4096]{1,0:T(8,128)(2,1)S(1)}, bf16[64,4096]{1,0:T(8,128)(2,1)S(1)}, u32[]{:S(2)}, u32[]{:S(2)}) collective-permute-start(bf16[64,4096]{1,0:T(8,128)(2,1)S(1)} %aggregate.1.agg_ref.refs_9_), channel_id=1, source_target_pairs={{0,1},{1,0},{2,3},{3,2},{4,5},{5,4},{6,7},{7,6},{8,9},{9,8},{10,11... | collective-permute-start | bytes 1572872 | tf_op jit(solution)/shard_map/ppermute | solution.py:310
  62.6 13.6 %collective-permute-start.5 = (bf16[64,2048]{1,0:T(8,128)(2,1)S(1)}, bf16[64,2048]{1,0:T(8,128)(2,1)S(1)}, u32[]{:S(2)}, u32[]{:S(2)}) collective-permute-start(bf16[64,2048]{1,0:T(8,128)(2,1)S(1)} %get-tuple-element.39), channel_id=1, source_target_pairs={{0,2},{1,3},{2,0},{3,1},{4,6},{5,7},{6,4},{7,5},{8,10},{9,11},{10,... | collective-permute-start | bytes 786440 | tf_op jit(solution)/shard_map/ppermute | solution.py:310
  67.2 14.2 %collective-permute-start.6 = (bf16[64,2048]{1,0:T(8,128)(2,1)S(1)}, bf16[64,2048]{1,0:T(8,128)(2,1)S(1)}, u32[]{:S(2)}, u32[]{:S(2)}) collective-permute-start(bf16[64,2048]{1,0:T(8,128)(2,1)S(1)} %get-tuple-element.41), channel_id=1, source_target_pairs={{0,2},{1,3},{2,0},{3,1},{4,6},{5,7},{6,4},{7,5},{8,10},{9,11},{10,... | collective-permute-start | bytes 786440 | tf_op jit(solution)/shard_map/ppermute | solution.py:310
  76.5 11.2 %collective-permute-start.9 = (bf16[64,2048]{1,0:T(8,128)(2,1)S(1)}, bf16[64,2048]{1,0:T(8,128)(2,1)S(1)}, u32[]{:S(2)}, u32[]{:S(2)}) collective-permute-start(bf16[64,2048]{1,0:T(8,128)(2,1)S(1)} %get-tuple-element.40.refs_0_), channel_id=1, source_target_pairs={{0,2},{1,3},{2,0},{3,1},{4,6},{5,7},{6,4},{7,5},{8,10},{9,11},{10,... | collective-permute-start | bytes 786440 | tf_op jit(solution)/shard_map/ppermute | solution.py:310
  81.7 12.4 %collective-permute-start.10 = (bf16[64,2048]{1,0:T(8,128)(2,1)S(1)}, bf16[64,2048]{1,0:T(8,128)(2,1)S(1)}, u32[]{:S(2)}, u32[]{:S(2)}) collective-permute-start(bf16[64,2048]{1,0:T(8,128)(2,1)S(1)} %get-tuple-element.42.refs_1_), channel_id=1, source_target_pairs={{0,2},{1,3},{2,0},{3,1},{4,6},{5,7},{6,4},{7,5},{8,10},{9,11},{10,... | collective-permute-start | bytes 786440 | tf_op jit(solution)/shard_map/ppermute | solution.py:310
  86.5 7.9 %collective-permute-start.7 = (bf16[64,2048]{1,0:T(8,128)(2,1)S(1)}, bf16[64,2048]{1,0:T(8,128)(2,1)S(1)}, u32[]{:S(2)}, u32[]{:S(2)}) collective-permute-start(bf16[64,2048]{1,0:T(8,128)(2,1)S(1)} %get-tuple-element.40.refs_0_), channel_id=1, source_target_pairs={{0,1},{1,0},{2,3},{3,2},{4,5},{5,4},{6,7},{7,6},{8,9},{9,8},{10,11... | collective-permute-start | bytes 786440 | tf_op jit(solution)/shard_map/ppermute | solution.py:310
  86.5 7.9 %collective-permute-start.8 = (bf16[64,2048]{1,0:T(8,128)(2,1)S(1)}, bf16[64,2048]{1,0:T(8,128)(2,1)S(1)}, u32[]{:S(2)}, u32[]{:S(2)}) collective-permute-start(bf16[64,2048]{1,0:T(8,128)(2,1)S(1)} %get-tuple-element.42.refs_1_), channel_id=1, source_target_pairs={{0,1},{1,0},{2,3},{3,2},{4,5},{5,4},{6,7},{7,6},{8,9},{9,8},{10,11... | collective-permute-start | bytes 786440 | tf_op jit(solution)/shard_map/ppermute | solution.py:310
  87.7 6.6 %collective-permute-start.11 = (bf16[64,2048]{1,0:T(8,128)(2,1)S(1)}, bf16[64,2048]{1,0:T(8,128)(2,1)}, u32[]{:S(2)}, u32[]{:S(2)}) collective-permute-start(bf16[64,2048]{1,0:T(8,128)(2,1)S(1)} %collective-permute-done.9.refs_4_), channel_id=1, source_target_pairs={{0,1},{1,0},{2,3},{3,2},{4,5},{5,4},{6,7},{7,6},{8,9},{9,8},{10,11... | collective-permute-start | bytes 786440 | tf_op jit(solution)/shard_map/ppermute | solution.py:310
  110.2 33.2 %collective-permute-start.13 = (bf16[20,64,128]{2,1,0:T(8,128)(2,1)}, bf16[20,64,128]{2,1,0:T(8,128)(2,1)S(1)}, u32[]{:S(2)}, u32[]{:S(2)}) collective-permute-start(bf16[20,64,128]{2,1,0:T(8,128)(2,1)} %get-tuple-element.51), channel_id=1, source_target_pairs={{0,64},{4,68},{8,72},{12,76},{16,80},{20,84},{24,88},{28,92},{32,9... | collective-permute-start | bytes 983048 | tf_op jit(solution)/shard_map/ppermute | solution.py:310
  110.5 33.0 %collective-permute-start.14 = (bf16[20,64,128]{2,1,0:T(8,128)(2,1)S(1)}, bf16[20,64,128]{2,1,0:T(8,128)(2,1)S(1)}, u32[]{:S(2)}, u32[]{:S(2)}) collective-permute-start(bf16[20,64,128]{2,1,0:T(8,128)(2,1)S(1)} %get-tuple-element.52), channel_id=1, source_target_pairs={{0,128},{4,132},{8,136},{12,140},{16,144},{20,148},{24,152},{28,15... | collective-permute-start | bytes 983048 | tf_op jit(solution)/shard_map/ppermute | solution.py:310
  115.7 27.8 %collective-permute-start.15 = (bf16[20,64,128]{2,1,0:T(8,128)(2,1)S(1)}, bf16[20,64,128]{2,1,0:T(8,128)(2,1)}, u32[]{:S(2)}, u32[]{:S(2)}) collective-permute-start(bf16[20,64,128]{2,1,0:T(8,128)(2,1)S(1)} %get-tuple-element.53), channel_id=1, source_target_pairs={{0,192},{4,196},{8,200},{12,204},{16,208},{20,212},{24,216},{28,22... | collective-permute-start | bytes 983048 | tf_op jit(solution)/shard_map/ppermute | solution.py:310
  115.7 62.7 %all-to-all-start.2 = ((bf16[64,32,128]{2,1,0:T(8,128)(2,1)}), bf16[64,32,128]{2,1,0:T(8,128)(2,1)S(1)}, u32[]{:S(2)}, u32[]{:S(2)}) async-start(bf16[64,32,128]{2,1,0:T(8,128)(2,1)} %get-tuple-element.46), calls=%async_computation.2 | async-start | bytes 1048576 | tf_op jit(solution)/shard_map/all_to_all | solution.py:419
  145.7 7.6 %collective-permute-start.16 = (bf16[8,64,128]{2,1,0:T(8,128)(2,1)S(1)}, bf16[8,64,128]{2,1,0:T(8,128)(2,1)S(1)}, u32[]{:S(2)}, u32[]{:S(2)}) collective-permute-start(bf16[8,64,128]{2,1,0:T(8,128)(2,1)S(1)} %get-tuple-element.55), channel_id=1, source_target_pairs={{0,16},{4,20},{8,24},{12,28},{16,0},{20,4},{24,8},{28,12},{32,48},... | collective-permute-start | bytes 393224 | tf_op jit(solution)/shard_map/ppermute | solution.py:310
  147.4 10.3 %collective-permute-start.17 = (bf16[8,64,128]{2,1,0:T(8,128)(2,1)S(1)}, bf16[8,64,128]{2,1,0:T(8,128)(2,1)S(1)}, u32[]{:S(2)}, u32[]{:S(2)}) collective-permute-start(bf16[8,64,128]{2,1,0:T(8,128)(2,1)S(1)} %get-tuple-element.56), channel_id=1, source_target_pairs={{0,32},{4,36},{8,40},{12,44},{16,48},{20,52},{24,56},{28,60},{32,0... | collective-permute-start | bytes 393224 | tf_op jit(solution)/shard_map/ppermute | solution.py:310
  150.0 9.4 %collective-permute-start.18 = (bf16[8,64,128]{2,1,0:T(8,128)(2,1)S(1)}, bf16[8,64,128]{2,1,0:T(8,128)(2,1)S(1)}, u32[]{:S(2)}, u32[]{:S(2)}) collective-permute-start(bf16[8,64,128]{2,1,0:T(8,128)(2,1)S(1)} %get-tuple-element.57), channel_id=1, source_target_pairs={{0,48},{4,52},{8,56},{12,60},{16,32},{20,36},{24,40},{28,44},{32,1... | collective-permute-start | bytes 393224 | tf_op jit(solution)/shard_map/ppermute | solution.py:310
  159.5 13.8 %collective-permute-start.19 = (bf16[5,64,128]{2,1,0:T(8,128)(2,1)S(1)}, bf16[5,64,128]{2,1,0:T(8,128)(2,1)S(1)}, u32[]{:S(2)}, u32[]{:S(2)}) collective-permute-start(bf16[5,64,128]{2,1,0:T(8,128)(2,1)S(1)} %get-tuple-element.59), channel_id=1, source_target_pairs={{0,4},{4,0},{8,12},{12,8},{16,20},{20,16},{24,28},{28,24},{32,36},... | collective-permute-start | bytes 245768 | tf_op jit(solution)/shard_map/ppermute | solution.py:310
  167.1 7.4 %collective-permute-start.20 = (bf16[5,64,128]{2,1,0:T(8,128)(2,1)S(1)}, bf16[5,64,128]{2,1,0:T(8,128)(2,1)S(1)}, u32[]{:S(2)}, u32[]{:S(2)}) collective-permute-start(bf16[5,64,128]{2,1,0:T(8,128)(2,1)S(1)} %get-tuple-element.60), channel_id=1, source_target_pairs={{0,8},{4,12},{8,0},{12,4},{16,24},{20,28},{24,16},{28,20},{32,40},... | collective-permute-start | bytes 245768 | tf_op jit(solution)/shard_map/ppermute | solution.py:310
  172.1 6.3 %collective-permute-start.21 = (bf16[5,64,128]{2,1,0:T(8,128)(2,1)S(1)}, bf16[5,64,128]{2,1,0:T(8,128)(2,1)S(1)}, u32[]{:S(2)}, u32[]{:S(2)}) collective-permute-start(bf16[5,64,128]{2,1,0:T(8,128)(2,1)S(1)} %get-tuple-element.61), channel_id=1, source_target_pairs={{0,12},{4,8},{8,4},{12,0},{16,28},{20,24},{24,20},{28,16},{32,44},... | collective-permute-start | bytes 245768 | tf_op jit(solution)/shard_map/ppermute | solution.py:310
  (14 other events, 232.8 us)

commit v4 on v3

--- a/solution.py
+++ b/solution.py
@@ -164,21 +164,25 @@
 
     for j in range(blocks):
         at = (step * blocks + j) * slots
-        part = lax.dot_general(
-            ga_ref[:, j * T : (j + 1) * T], weight_ref[j], LAST, preferred_element_type=F32
-        )
+        grad = ga_ref[:, j * T : (j + 1) * T]
+        grad = jnp.concatenate([grad, jnp.zeros((T - rows, T), BF)], axis=0)
+        part = lax.dot_general(weight_ref[j], grad, LAST, preferred_element_type=F32)
         for s in range(slots):
-            total[place_ref[at + s]] += part[:, s * T : (s + 1) * T]
+            total[place_ref[at + s]] += part[s * T : (s + 1) * T]
 
     @pl.when(step == pl.num_programs(0) - 1)
     def _():
         low = low_lanes(half)
+
+        def tile(i):
+            return total[i].T[:rows]
+
         for i in range(own):
-            own_ref[:, i * T : (i + 1) * T] = total[i] + dir_ref[:, i * T : (i + 1) * T]
+            own_ref[:, i * T : (i + 1) * T] = tile(i) + dir_ref[:, i * T : (i + 1) * T]
 
         def pair(t, carry):
-            top = total[own + t, :half]
-            bottom = total[own + t, half:]
+            both = tile(own + t)
+            top, bottom = both[:half], both[half:]
             send_ref[2 * t] = jnp.where(low, top, swap_halves(bottom)).astype(BF)
             send_ref[2 * t + 1] = jnp.where(low, swap_halves(top), bottom).astype(BF)
             return carry
@@ -187,7 +191,8 @@
         many = peers // 4
         for k, hub_ref in enumerate((hub0, hub1, hub2, hub3)):
             start = own + peers // 2 + k * many
-            hub_ref[:many] = total[start : start + many].astype(hub_ref.dtype)
+            for i in range(many):
+                hub_ref[i] = tile(start + i).astype(hub_ref.dtype)
         for c in range(gw_ref.shape[1] // T):
             part = gw_ref[:, c * T : (c + 1) * T].astype(BF)
             for hub_ref in (hub0, hub1, hub2, hub3):
@@ -412,7 +417,7 @@
         (grad_agg, direct, gw, weight),
         {0: pl.BlockSpec((rows, span), lambda i, place: (0, i)), 3: blocked},
         (parts,),
-        [shape_of(sources + 1, rows, T, dtype=F32)],
+        [shape_of(sources + 1, T, T, dtype=F32)],
         mib=48,
         micros=30,
     )

time: 186 us -> 190 us (1.022)
  Pallas kernels: 34.6 us -> 38.4 us
    pallas_call x10, Pallas kernels: 34.6 us -> 38.4 us  [call(): pl.pallas_call(kernel, grid_spec=pltpu.PrefetchScalarGridSpec(num_scalar_...]
where the time goes in v4:
time: 190 us; the launch traced here: 188 us
  starting transfers between devices  86.4 us (45%)
  waiting for transfers between devices  51.9 us (27%)
  Pallas kernels  38.4 us (20%)
  local copies, waits for them, and re-layouts  9.22 us (5%)
    ppermute x22, waiting for transfers between devices, swap(): return lax.ppermute(x, axis, [(i, i ^ mask) for i in range(size)])  48.3 us
    ppermute x22, starting transfers between devices, swap(): return lax.ppermute(x, axis, [(i, i ^ mask) for i in range(size)])  44.3 us
    pallas_call x10, Pallas kernels, call(): pl.pallas_call(kernel, grid_spec=pltpu.PrefetchScalarGridSpec(num_scalar_...  38.4 us
    all_to_all x2, starting transfers between devices, local(): recv = lax.all_to_all(send, 'vert', 0, 0, tiled=True)  35.3 us
    all_to_all x1, starting transfers between devices, local(): lax.all_to_all(hub, 'vert', 0, 0, axis_index_groups=groups, tiled=True)  6.73 us
    unnamed x28, local copies, waits for them, and re-layouts  6.48 us
  transfers between devices with their start and end apart: 25, of which 13 were waited for; matrix products, arithmetic and copies ran while one was open for 2% of the time, Pallas kernels for 4%

profile of v4, /device:TPU:0, one launch (start us, length us, event | category | flops | bytes accessed | tf_op | source)
XLA Modules:
  0.0 187.6 jit_solution(2843914934544775793)
XLA Ops:
  2.2 6.7 %all-to-all-start = ((bf16[16,64,128]{2,1,0:T(8,128)(2,1)}), bf16[16,64,128]{2,1,0:T(8,128)(2,1)S(1)}, u32[]{:S(2)}, u32[]{:S(2)}) async-start(bf16[16,64,128]{2,1,0:T(8,128)(2,1)} %broadcast_in_dim.18), calls=%async_computation | async-start | bytes 524288 | tf_op jit(solution)/shard_map/all_to_all | solution.py:323
  11.7 5.1 %pick.1 = bf16[64,32,128]{2,1,0:T(8,128)(2,1)} custom-call(bf16[64,4096]{1,0:T(8,128)(2,1)S(1)} %copy-done, s32[1,4096]{1,0:T(1,128)S(1)} %broadcast_select_fusion.index_ref), custom_call_target="tpu_custom_call" | custom-call | flops 30000001024 | bytes 90000000 | tf_op jit(solution)/shard_map/pick/pallas_call | solution.py:269
  16.8 3.7 %all-to-all-done.h0 = bf16[16,64,128]{2,1,0:T(8,128)(2,1)S(1)} async-done(((bf16[16,64,128]{2,1,0:T(8,128)(2,1)}), bf16[16,64,128]{2,1,0:T(8,128)(2,1)S(1)}, u32[]{:S(2)}, u32[]{:S(2)}) %all-to-all-start) | async-done | bytes 262176 | tf_op jit(solution)/shard_map/all_to_all | solution.py:323
  20.5 7.5 %all-to-all-start.1 = ((bf16[64,32,128]{2,1,0:T(8,128)(2,1)}), bf16[64,32,128]{2,1,0:T(8,128)(2,1)S(1)}, u32[]{:S(2)}, u32[]{:S(2)}) async-start(bf16[64,32,128]{2,1,0:T(8,128)(2,1)} %pick.1), calls=%async_computation.1 | async-start | bytes 1048576 | tf_op jit(solution)/shard_map/all_to_all | solution.py:352
  28.0 3.1 %collective-permute-start.3 = (bf16[16,64,128]{2,1,0:T(8,128)(2,1)S(1)}, bf16[16,64,128]{2,1,0:T(8,128)(2,1)S(1)}, u32[]{:S(2)}, u32[]{:S(2)}) collective-permute-start(bf16[16,64,128]{2,1,0:T(8,128)(2,1)S(1)} %all-to-all-done.h0), channel_id=1, source_target_pairs={{0,192},{4,196},{8,200},{12,204},{16,208},{20,212},{24,216},{28,22... | collective-permute-start | bytes 786440 | tf_op jit(solution)/shard_map/ppermute | solution.py:315
  32.4 15.9 %collective-permute-done.3.h3 = bf16[16,64,128]{2,1,0:T(8,128)(2,1)S(1)} collective-permute-done((bf16[16,64,128]{2,1,0:T(8,128)(2,1)S(1)}, bf16[16,64,128]{2,1,0:T(8,128)(2,1)S(1)}, u32[]{:S(2)}, u32[]{:S(2)}) %collective-permute-start.3) | collective-permute-done | bytes 262176 | tf_op jit(solution)/shard_map/ppermute | solution.py:315
  51.7 8.1 %aggregate.1.agg_ref.refs_9_ = bf16[64,4096]{1,0:T(8,128)(2,1)S(1)} custom-call(s32[256]{0:T(256)S(1)} %reshape.59.place_ref, bf16[64,4096]{1,0:T(8,128)(2,1)S(1)} %copy-done.1, bf16[64,32,128]{2,1,0:T(8,128)(2,1)S(1)} %all-to-all-done.1.recv_ref, bf16[16,64,128]{2,1,0:T(8,128)(2,1)S(1)} %all-to-all-done.h0, bf16[16,64,128]{2,1,0:T(8,128)(2,1)S(1)} %copy-done.8, ...), custom_call_target="tpu_custom_call" | custom-call | tf_op jit(solution)/shard_map/aggregate/pallas_call | solution.py:269
  62.6 4.6 %collective-permute-start.5 = (bf16[64,2048]{1,0:T(8,128)(2,1)S(1)}, bf16[64,2048]{1,0:T(8,128)(2,1)S(1)}, u32[]{:S(2)}, u32[]{:S(2)}) collective-permute-start(bf16[64,2048]{1,0:T(8,128)(2,1)S(1)} %get-tuple-element.39), channel_id=1, source_target_pairs={{0,2},{1,3},{2,0},{3,1},{4,6},{5,7},{6,4},{7,5},{8,10},{9,11},{10,... | collective-permute-start | bytes 786440 | tf_op jit(solution)/shard_map/ppermute | solution.py:315
  68.6 7.6 %collective-permute-done.5.recv_ref = bf16[64,2048]{1,0:T(8,128)(2,1)S(1)} collective-permute-done((bf16[64,2048]{1,0:T(8,128)(2,1)S(1)}, bf16[64,2048]{1,0:T(8,128)(2,1)S(1)}, u32[]{:S(2)}, u32[]{:S(2)}) %collective-permute-start.5) | collective-permute-done | bytes 262176 | tf_op jit(solution)/shard_map/ppermute | solution.py:315
  76.5 4.7 %collective-permute-start.9 = (bf16[64,2048]{1,0:T(8,128)(2,1)S(1)}, bf16[64,2048]{1,0:T(8,128)(2,1)S(1)}, u32[]{:S(2)}, u32[]{:S(2)}) collective-permute-start(bf16[64,2048]{1,0:T(8,128)(2,1)S(1)} %get-tuple-element.40.refs_0_), channel_id=1, source_target_pairs={{0,2},{1,3},{2,0},{3,1},{4,6},{5,7},{6,4},{7,5},{8,10},{9,11},{10,... | collective-permute-start | bytes 786440 | tf_op jit(solution)/shard_map/ppermute | solution.py:315
  81.7 4.8 %collective-permute-start.10 = (bf16[64,2048]{1,0:T(8,128)(2,1)S(1)}, bf16[64,2048]{1,0:T(8,128)(2,1)S(1)}, u32[]{:S(2)}, u32[]{:S(2)}) collective-permute-start(bf16[64,2048]{1,0:T(8,128)(2,1)S(1)} %get-tuple-element.42.refs_1_), channel_id=1, source_target_pairs={{0,2},{1,3},{2,0},{3,1},{4,6},{5,7},{6,4},{7,5},{8,10},{9,11},{10,... | collective-permute-start | bytes 786440 | tf_op jit(solution)/shard_map/ppermute | solution.py:315
  87.8 6.4 %collective-permute-done.10.refs_5_ = bf16[64,2048]{1,0:T(8,128)(2,1)S(1)} collective-permute-done((bf16[64,2048]{1,0:T(8,128)(2,1)S(1)}, bf16[64,2048]{1,0:T(8,128)(2,1)S(1)}, u32[]{:S(2)}, u32[]{:S(2)}) %collective-permute-start.10) | collective-permute-done | bytes 262176 | tf_op jit(solution)/shard_map/ppermute | solution.py:315
  95.9 3.3 %back.1 = (bf16[64,4096]{1,0:T(8,128)(2,1)S(1)}, f32[64,4096]{1,0:T(8,128)S(1)}, f32[64,512]{1,0:T(8,128)S(1)}) custom-call(s32[1]{0:T(128)} %bitcast.me_ref, bf16[64,2048]{1,0:T(8,128)(2,1)S(1)} %get-tuple-element.40.refs_0_, bf16[64,2048]{1,0:T(8,128)(2,1)S(1)} %get-tuple-element.42.refs_1_, bf16[64,2048]{1,0:T(8,128)(2,1)S(1)} %collective-permute-done.7.refs_2_, ...), custom_call_target="tpu_custom_call" | custom-call | tf_op jit(solution)/shard_map/back/pallas_call | solution.py:269
  99.1 14.1 %spread.1 = (f32[64,4096]{1,0:T(8,128)S(1)}, bf16[64,32,128]{2,1,0:T(8,128)(2,1)}, f32[20,64,128]{2,1,0:T(8,128)S(1)}, bf16[20,64,128]{2,1,0:T(8,128)(2,1)}, bf1...) custom-call(s32[256]{0:T(256)S(1)} %reshape.57.place_ref, bf16[64,4096]{1,0:T(8,128)(2,1)S(1)} %get-tuple-element.43.ga_ref, ...), custom_call_target="tpu_custom_call" | custom-call | flops 30000001024 | bytes 90000000 | tf_op jit(solution)/shard_map/spread/pallas_call | solution.py:269
  114.3 5.2 %collective-permute-start.14 = (bf16[20,64,128]{2,1,0:T(8,128)(2,1)S(1)}, bf16[20,64,128]{2,1,0:T(8,128)(2,1)S(1)}, u32[]{:S(2)}, u32[]{:S(2)}) collective-permute-start(bf16[20,64,128]{2,1,0:T(8,128)(2,1)S(1)} %get-tuple-element.52), channel_id=1, source_target_pairs={{0,128},{4,132},{8,136},{12,140},{16,144},{20,148},{24,152},{28,15... | collective-permute-start | bytes 983048 | tf_op jit(solution)/shard_map/ppermute | solution.py:315
  119.5 27.8 %all-to-all-start.2 = ((bf16[64,32,128]{2,1,0:T(8,128)(2,1)}), bf16[64,32,128]{2,1,0:T(8,128)(2,1)S(1)}, u32[]{:S(2)}, u32[]{:S(2)}) async-start(bf16[64,32,128]{2,1,0:T(8,128)(2,1)} %get-tuple-element.46), calls=%async_computation.2 | async-start | bytes 1048576 | tf_op jit(solution)/shard_map/all_to_all | solution.py:424
  151.2 2.7 %collective-permute-start.17 = (bf16[8,64,128]{2,1,0:T(8,128)(2,1)S(1)}, bf16[8,64,128]{2,1,0:T(8,128)(2,1)S(1)}, u32[]{:S(2)}, u32[]{:S(2)}) collective-permute-start(bf16[8,64,128]{2,1,0:T(8,128)(2,1)S(1)} %get-tuple-element.56), channel_id=1, source_target_pairs={{0,32},{4,36},{8,40},{12,44},{16,48},{20,52},{24,56},{28,60},{32,0... | collective-permute-start | bytes 393224 | tf_op jit(solution)/shard_map/ppermute | solution.py:315
  154.3 2.8 %collective-permute-done.16.one_ref = bf16[8,64,128]{2,1,0:T(8,128)(2,1)S(1)} collective-permute-done((bf16[8,64,128]{2,1,0:T(8,128)(2,1)S(1)}, bf16[8,64,128]{2,1,0:T(8,128)(2,1)S(1)}, u32[]{:S(2)}, u32[]{:S(2)}) %collective-permute-start.16) | collective-permute-done | bytes 131104 | tf_op jit(solution)/shard_map/ppermute | solution.py:315
  157.1 4.4 %collective-permute-done.17.two_ref = bf16[8,64,128]{2,1,0:T(8,128)(2,1)S(1)} collective-permute-done((bf16[8,64,128]{2,1,0:T(8,128)(2,1)S(1)}, bf16[8,64,128]{2,1,0:T(8,128)(2,1)S(1)}, u32[]{:S(2)}, u32[]{:S(2)}) %collective-permute-start.17) | collective-permute-done | bytes 131104 | tf_op jit(solution)/shard_map/ppermute | solution.py:315
  161.5 1.7 collective-permute-done.18.three_ref
  163.3 7.5 %collective-permute-start.19 = (bf16[5,64,128]{2,1,0:T(8,128)(2,1)S(1)}, bf16[5,64,128]{2,1,0:T(8,128)(2,1)S(1)}, u32[]{:S(2)}, u32[]{:S(2)}) collective-permute-start(bf16[5,64,128]{2,1,0:T(8,128)(2,1)S(1)} %get-tuple-element.59), channel_id=1, source_target_pairs={{0,4},{4,0},{8,12},{12,8},{16,20},{20,16},{24,28},{28,24},{32,36},... | collective-permute-start | bytes 245768 | tf_op jit(solution)/shard_map/ppermute | solution.py:315
  170.8 5.0 %collective-permute-start.20 = (bf16[5,64,128]{2,1,0:T(8,128)(2,1)S(1)}, bf16[5,64,128]{2,1,0:T(8,128)(2,1)S(1)}, u32[]{:S(2)}, u32[]{:S(2)}) collective-permute-start(bf16[5,64,128]{2,1,0:T(8,128)(2,1)S(1)} %get-tuple-element.60), channel_id=1, source_target_pairs={{0,8},{4,12},{8,0},{12,4},{16,24},{20,28},{24,16},{28,20},{32,40},... | collective-permute-start | bytes 245768 | tf_op jit(solution)/shard_map/ppermute | solution.py:315
  178.3 3.9 %collective-permute-done.21.refs_3_ = bf16[5,64,128]{2,1,0:T(8,128)(2,1)S(1)} collective-permute-done((bf16[5,64,128]{2,1,0:T(8,128)(2,1)S(1)}, bf16[5,64,128]{2,1,0:T(8,128)(2,1)S(1)}, u32[]{:S(2)}, u32[]{:S(2)}) %collective-permute-start.21) | collective-permute-done | bytes 81952 | tf_op jit(solution)/shard_map/ppermute | solution.py:315
  182.2 5.4 %finish.1 = (f32[64,4096]{1,0:T(8,128)}, bf16[64,4096]{1,0:T(8,128)(2,1)}, f32[64,256]{1,0:T(8,128)}, f32[64,256]{1,0:T(8,128)}) custom-call(bf16[64,32,128]{2,1,0:T(8,128)(2,1)S(1)} %all-to-all-done.2.recv_ref, s32[1,4096]{1,0:T(1,128)S(1)} %broadcast_select_fusion.index_ref, f32[64,4096]{1,0:T(8,128)S(1)} %get-tuple-element.47.own_ref, ...), custom_call_target="tpu_custom_call" | custom-call | tf_op jit(solution)/shard_map/finish/pallas_call | solution.py:269
  (75 shorter events, 24.6 us)
Async XLA Ops:
  0.6 19.9 %collective-permute-start = (bf16[64,4096]{1,0:T(8,128)(2,1)}, bf16[64,4096]{1,0:T(8,128)(2,1)S(1)}, u32[]{:S(2)}, u32[]{:S(2)}) collective-permute-start(bf16[64,4096]{1,0:T(8,128)(2,1)} %refs_8_.1), channel_id=1, source_target_pairs={{0,1},{1,0},{2,3},{3,2},{4,5},{5,4},{6,7},{7,6},{8,9},{9,8},{10,11... | collective-permute-start | bytes 1572872 | tf_op jit(solution)/shard_map/ppermute | solution.py:315
  2.2 18.3 %all-to-all-start = ((bf16[16,64,128]{2,1,0:T(8,128)(2,1)}), bf16[16,64,128]{2,1,0:T(8,128)(2,1)S(1)}, u32[]{:S(2)}, u32[]{:S(2)}) async-start(bf16[16,64,128]{2,1,0:T(8,128)(2,1)} %broadcast_in_dim.18), calls=%async_computation | async-start | bytes 524288 | tf_op jit(solution)/shard_map/all_to_all | solution.py:323
  20.5 29.3 %all-to-all-start.1 = ((bf16[64,32,128]{2,1,0:T(8,128)(2,1)}), bf16[64,32,128]{2,1,0:T(8,128)(2,1)S(1)}, u32[]{:S(2)}, u32[]{:S(2)}) async-start(bf16[64,32,128]{2,1,0:T(8,128)(2,1)} %pick.1), calls=%async_computation.1 | async-start | bytes 1048576 | tf_op jit(solution)/shard_map/all_to_all | solution.py:352
  28.0 20.3 %collective-permute-start.3 = (bf16[16,64,128]{2,1,0:T(8,128)(2,1)S(1)}, bf16[16,64,128]{2,1,0:T(8,128)(2,1)S(1)}, u32[]{:S(2)}, u32[]{:S(2)}) collective-permute-start(bf16[16,64,128]{2,1,0:T(8,128)(2,1)S(1)} %all-to-all-done.h0), channel_id=1, source_target_pairs={{0,192},{4,196},{8,200},{12,204},{16,208},{20,212},{24,216},{28,22... | collective-permute-start | bytes 786440 | tf_op jit(solution)/shard_map/ppermute | solution.py:315
  31.1 17.2 %collective-permute-start.2 = (bf16[16,64,128]{2,1,0:T(8,128)(2,1)S(1)}, bf16[16,64,128]{2,1,0:T(8,128)(2,1)S(1)}, u32[]{:S(2)}, u32[]{:S(2)}) collective-permute-start(bf16[16,64,128]{2,1,0:T(8,128)(2,1)S(1)} %all-to-all-done.h0), channel_id=1, source_target_pairs={{0,128},{4,132},{8,136},{12,140},{16,144},{20,148},{24,152},{28,15... | collective-permute-start | bytes 786440 | tf_op jit(solution)/shard_map/ppermute | solution.py:315
  31.8 17.3 %collective-permute-start.1 = (bf16[16,64,128]{2,1,0:T(8,128)(2,1)S(1)}, bf16[16,64,128]{2,1,0:T(8,128)(2,1)S(1)}, u32[]{:S(2)}, u32[]{:S(2)}) collective-permute-start(bf16[16,64,128]{2,1,0:T(8,128)(2,1)S(1)} %all-to-all-done.h0), channel_id=1, source_target_pairs={{0,64},{4,68},{8,72},{12,76},{16,80},{20,84},{24,88},{28,92},{32,9... | collective-permute-start | bytes 786440 | tf_op jit(solution)/shard_map/ppermute | solution.py:315
  59.8 2.0 %collective-permute-start.4 = (bf16[64,4096]{1,0:T(8,128)(2,1)S(1)}, bf16[64,4096]{1,0:T(8,128)(2,1)S(1)}, u32[]{:S(2)}, u32[]{:S(2)}) collective-permute-start(bf16[64,4096]{1,0:T(8,128)(2,1)S(1)} %aggregate.1.agg_ref.refs_9_), channel_id=1, source_target_pairs={{0,1},{1,0},{2,3},{3,2},{4,5},{5,4},{6,7},{7,6},{8,9},{9,8},{10,11... | collective-permute-start | bytes 1572872 | tf_op jit(solution)/shard_map/ppermute | solution.py:315
  62.6 13.6 %collective-permute-start.5 = (bf16[64,2048]{1,0:T(8,128)(2,1)S(1)}, bf16[64,2048]{1,0:T(8,128)(2,1)S(1)}, u32[]{:S(2)}, u32[]{:S(2)}) collective-permute-start(bf16[64,2048]{1,0:T(8,128)(2,1)S(1)} %get-tuple-element.39), channel_id=1, source_target_pairs={{0,2},{1,3},{2,0},{3,1},{4,6},{5,7},{6,4},{7,5},{8,10},{9,11},{10,... | collective-permute-start | bytes 786440 | tf_op jit(solution)/shard_map/ppermute | solution.py:315
  67.2 14.2 %collective-permute-start.6 = (bf16[64,2048]{1,0:T(8,128)(2,1)S(1)}, bf16[64,2048]{1,0:T(8,128)(2,1)S(1)}, u32[]{:S(2)}, u32[]{:S(2)}) collective-permute-start(bf16[64,2048]{1,0:T(8,128)(2,1)S(1)} %get-tuple-element.41), channel_id=1, source_target_pairs={{0,2},{1,3},{2,0},{3,1},{4,6},{5,7},{6,4},{7,5},{8,10},{9,11},{10,... | collective-permute-start | bytes 786440 | tf_op jit(solution)/shard_map/ppermute | solution.py:315
  76.5 11.3 %collective-permute-start.9 = (bf16[64,2048]{1,0:T(8,128)(2,1)S(1)}, bf16[64,2048]{1,0:T(8,128)(2,1)S(1)}, u32[]{:S(2)}, u32[]{:S(2)}) collective-permute-start(bf16[64,2048]{1,0:T(8,128)(2,1)S(1)} %get-tuple-element.40.refs_0_), channel_id=1, source_target_pairs={{0,2},{1,3},{2,0},{3,1},{4,6},{5,7},{6,4},{7,5},{8,10},{9,11},{10,... | collective-permute-start | bytes 786440 | tf_op jit(solution)/shard_map/ppermute | solution.py:315
  81.7 12.5 %collective-permute-start.10 = (bf16[64,2048]{1,0:T(8,128)(2,1)S(1)}, bf16[64,2048]{1,0:T(8,128)(2,1)S(1)}, u32[]{:S(2)}, u32[]{:S(2)}) collective-permute-start(bf16[64,2048]{1,0:T(8,128)(2,1)S(1)} %get-tuple-element.42.refs_1_), channel_id=1, source_target_pairs={{0,2},{1,3},{2,0},{3,1},{4,6},{5,7},{6,4},{7,5},{8,10},{9,11},{10,... | collective-permute-start | bytes 786440 | tf_op jit(solution)/shard_map/ppermute | solution.py:315
  86.4 7.9 %collective-permute-start.7 = (bf16[64,2048]{1,0:T(8,128)(2,1)S(1)}, bf16[64,2048]{1,0:T(8,128)(2,1)S(1)}, u32[]{:S(2)}, u32[]{:S(2)}) collective-permute-start(bf16[64,2048]{1,0:T(8,128)(2,1)S(1)} %get-tuple-element.40.refs_0_), channel_id=1, source_target_pairs={{0,1},{1,0},{2,3},{3,2},{4,5},{5,4},{6,7},{7,6},{8,9},{9,8},{10,11... | collective-permute-start | bytes 786440 | tf_op jit(solution)/shard_map/ppermute | solution.py:315
  86.4 7.9 %collective-permute-start.8 = (bf16[64,2048]{1,0:T(8,128)(2,1)S(1)}, bf16[64,2048]{1,0:T(8,128)(2,1)S(1)}, u32[]{:S(2)}, u32[]{:S(2)}) collective-permute-start(bf16[64,2048]{1,0:T(8,128)(2,1)S(1)} %get-tuple-element.42.refs_1_), channel_id=1, source_target_pairs={{0,1},{1,0},{2,3},{3,2},{4,5},{5,4},{6,7},{7,6},{8,9},{9,8},{10,11... | collective-permute-start | bytes 786440 | tf_op jit(solution)/shard_map/ppermute | solution.py:315
  87.8 6.6 %collective-permute-start.11 = (bf16[64,2048]{1,0:T(8,128)(2,1)S(1)}, bf16[64,2048]{1,0:T(8,128)(2,1)}, u32[]{:S(2)}, u32[]{:S(2)}) collective-permute-start(bf16[64,2048]{1,0:T(8,128)(2,1)S(1)} %collective-permute-done.9.refs_4_), channel_id=1, source_target_pairs={{0,1},{1,0},{2,3},{3,2},{4,5},{5,4},{6,7},{7,6},{8,9},{9,8},{10,11... | collective-permute-start | bytes 786440 | tf_op jit(solution)/shard_map/ppermute | solution.py:315
  114.1 33.2 %collective-permute-start.13 = (bf16[20,64,128]{2,1,0:T(8,128)(2,1)}, bf16[20,64,128]{2,1,0:T(8,128)(2,1)S(1)}, u32[]{:S(2)}, u32[]{:S(2)}) collective-permute-start(bf16[20,64,128]{2,1,0:T(8,128)(2,1)} %get-tuple-element.51), channel_id=1, source_target_pairs={{0,64},{4,68},{8,72},{12,76},{16,80},{20,84},{24,88},{28,92},{32,9... | collective-permute-start | bytes 983048 | tf_op jit(solution)/shard_map/ppermute | solution.py:315
  114.3 33.0 %collective-permute-start.14 = (bf16[20,64,128]{2,1,0:T(8,128)(2,1)S(1)}, bf16[20,64,128]{2,1,0:T(8,128)(2,1)S(1)}, u32[]{:S(2)}, u32[]{:S(2)}) collective-permute-start(bf16[20,64,128]{2,1,0:T(8,128)(2,1)S(1)} %get-tuple-element.52), channel_id=1, source_target_pairs={{0,128},{4,132},{8,136},{12,140},{16,144},{20,148},{24,152},{28,15... | collective-permute-start | bytes 983048 | tf_op jit(solution)/shard_map/ppermute | solution.py:315
  119.5 27.8 %collective-permute-start.15 = (bf16[20,64,128]{2,1,0:T(8,128)(2,1)S(1)}, bf16[20,64,128]{2,1,0:T(8,128)(2,1)}, u32[]{:S(2)}, u32[]{:S(2)}) collective-permute-start(bf16[20,64,128]{2,1,0:T(8,128)(2,1)S(1)} %get-tuple-element.53), channel_id=1, source_target_pairs={{0,192},{4,196},{8,200},{12,204},{16,208},{20,212},{24,216},{28,22... | collective-permute-start | bytes 983048 | tf_op jit(solution)/shard_map/ppermute | solution.py:315
  119.5 62.8 %all-to-all-start.2 = ((bf16[64,32,128]{2,1,0:T(8,128)(2,1)}), bf16[64,32,128]{2,1,0:T(8,128)(2,1)S(1)}, u32[]{:S(2)}, u32[]{:S(2)}) async-start(bf16[64,32,128]{2,1,0:T(8,128)(2,1)} %get-tuple-element.46), calls=%async_computation.2 | async-start | bytes 1048576 | tf_op jit(solution)/shard_map/all_to_all | solution.py:424
  149.5 7.6 %collective-permute-start.16 = (bf16[8,64,128]{2,1,0:T(8,128)(2,1)S(1)}, bf16[8,64,128]{2,1,0:T(8,128)(2,1)S(1)}, u32[]{:S(2)}, u32[]{:S(2)}) collective-permute-start(bf16[8,64,128]{2,1,0:T(8,128)(2,1)S(1)} %get-tuple-element.55), channel_id=1, source_target_pairs={{0,16},{4,20},{8,24},{12,28},{16,0},{20,4},{24,8},{28,12},{32,48},... | collective-permute-start | bytes 393224 | tf_op jit(solution)/shard_map/ppermute | solution.py:315
  151.2 10.3 %collective-permute-start.17 = (bf16[8,64,128]{2,1,0:T(8,128)(2,1)S(1)}, bf16[8,64,128]{2,1,0:T(8,128)(2,1)S(1)}, u32[]{:S(2)}, u32[]{:S(2)}) collective-permute-start(bf16[8,64,128]{2,1,0:T(8,128)(2,1)S(1)} %get-tuple-element.56), channel_id=1, source_target_pairs={{0,32},{4,36},{8,40},{12,44},{16,48},{20,52},{24,56},{28,60},{32,0... | collective-permute-start | bytes 393224 | tf_op jit(solution)/shard_map/ppermute | solution.py:315
  153.9 9.4 %collective-permute-start.18 = (bf16[8,64,128]{2,1,0:T(8,128)(2,1)S(1)}, bf16[8,64,128]{2,1,0:T(8,128)(2,1)S(1)}, u32[]{:S(2)}, u32[]{:S(2)}) collective-permute-start(bf16[8,64,128]{2,1,0:T(8,128)(2,1)S(1)} %get-tuple-element.57), channel_id=1, source_target_pairs={{0,48},{4,52},{8,56},{12,60},{16,32},{20,36},{24,40},{28,44},{32,1... | collective-permute-start | bytes 393224 | tf_op jit(solution)/shard_map/ppermute | solution.py:315
  163.3 13.7 %collective-permute-start.19 = (bf16[5,64,128]{2,1,0:T(8,128)(2,1)S(1)}, bf16[5,64,128]{2,1,0:T(8,128)(2,1)S(1)}, u32[]{:S(2)}, u32[]{:S(2)}) collective-permute-start(bf16[5,64,128]{2,1,0:T(8,128)(2,1)S(1)} %get-tuple-element.59), channel_id=1, source_target_pairs={{0,4},{4,0},{8,12},{12,8},{16,20},{20,16},{24,28},{28,24},{32,36},... | collective-permute-start | bytes 245768 | tf_op jit(solution)/shard_map/ppermute | solution.py:315
  170.8 7.5 %collective-permute-start.20 = (bf16[5,64,128]{2,1,0:T(8,128)(2,1)S(1)}, bf16[5,64,128]{2,1,0:T(8,128)(2,1)S(1)}, u32[]{:S(2)}, u32[]{:S(2)}) collective-permute-start(bf16[5,64,128]{2,1,0:T(8,128)(2,1)S(1)} %get-tuple-element.60), channel_id=1, source_target_pairs={{0,8},{4,12},{8,0},{12,4},{16,24},{20,28},{24,16},{28,20},{32,40},... | collective-permute-start | bytes 245768 | tf_op jit(solution)/shard_map/ppermute | solution.py:315
  175.9 6.3 %collective-permute-start.21 = (bf16[5,64,128]{2,1,0:T(8,128)(2,1)S(1)}, bf16[5,64,128]{2,1,0:T(8,128)(2,1)S(1)}, u32[]{:S(2)}, u32[]{:S(2)}) collective-permute-start(bf16[5,64,128]{2,1,0:T(8,128)(2,1)S(1)} %get-tuple-element.61), channel_id=1, source_target_pairs={{0,12},{4,8},{8,4},{12,0},{16,28},{20,24},{24,20},{28,16},{32,44},... | collective-permute-start | bytes 245768 | tf_op jit(solution)/shard_map/ppermute | solution.py:315
  (14 other events, 232.8 us)

commit v5 on v3

--- a/solution.py
+++ b/solution.py
@@ -31,6 +31,11 @@
     row = lax.broadcasted_iota(jnp.int16, (width, index_row.shape[1]), 0)
     low = jnp.where(index_row < 0, -1, index_row & (width - 1))
     return jnp.where(row == low.astype(jnp.int16), BF(1), BF(0))
+
+
+def hub_kernel(feat_ref, out_ref):
+    for i in range(out_ref.shape[0]):
+        out_ref[i] = feat_ref[...]
 
 
 def pick_kernel(feat_ref, index_ref, out_ref, stacked, *, width):
@@ -62,7 +67,7 @@
     lax.fori_loop(0, index_ref.shape[1] // (2 * T), body, 0, unroll=2)
 
 
-def forward_kernel(place_ref, feat_ref, recv_ref, h0, h1, h2, h3, weight_ref, out_ref, source):
+def forward_kernel(place_ref, feat_ref, recv_ref, h0, h1, h2, h3, weight_ref, out_ref, source, sems):
     step = pl.program_id(0)
     rows, nodes = feat_ref.shape
     half = rows // 2
@@ -73,6 +78,14 @@
 
     @pl.when(step == 0)
     def _():
+        first = own + peers // 2
+        many = h0.shape[0]
+        copies = [
+            pltpu.make_async_copy(hub_ref, source.at[pl.ds(first + k * many, many)], sems.at[k])
+            for k, hub_ref in enumerate((h0, h1, h2, h3))
+        ]
+        for copy in copies:
+            copy.start()
         low = low_lanes(half)
         for i in range(own):
             source[i] = feat_ref[:, i * T : (i + 1) * T]
@@ -85,11 +98,9 @@
             return carry
 
         lax.fori_loop(0, peers // 2, pair, 0)
-        first = own + peers // 2
-        for k, hub_ref in enumerate((h0, h1, h2, h3)):
-            many = hub_ref.shape[0]
-            source[first + k * many : first + (k + 1) * many] = hub_ref[...]
         source[first + peers] = jnp.zeros((rows, T), BF)
+        for copy in copies:
+            copy.wait()
 
     for j in range(blocks):
         at = (step * blocks + j) * slots
@@ -268,7 +279,10 @@
             grid=grid,
             in_specs=[in_specs.get(i) or whole(x.shape) for i, x in enumerate(operands)],
             out_specs=out_specs or [whole(s.shape) for s in out_shape],
-            scratch_shapes=[pltpu.VMEM(s.shape, s.dtype) for s in scratch],
+            scratch_shapes=[
+                pltpu.VMEM(s.shape, s.dtype) if isinstance(s, jax.ShapeDtypeStruct) else s
+                for s in scratch
+            ],
         ),
         out_shape=tuple(out_shape),
         compiler_params=params(mib),
@@ -314,7 +328,15 @@
 
     plane = peers // 4
     groups = [[y * plane + i for i in range(plane)] for y in range(4)]
-    hub = jnp.broadcast_to(features[None, :, :T], (plane, rows, T))
+    (hub,) = call(
+        hub_kernel,
+        "hub",
+        (),
+        [shape_of(plane, rows, T)],
+        (features,),
+        {0: pl.BlockSpec((rows, T), lambda i: (0, 0))},
+        mib=8,
+    )
     hub = lax.all_to_all(hub, "vert", 0, 0, axis_index_groups=groups, tiled=True)
 
     features2 = swap(features, "af", 1)
@@ -346,6 +368,7 @@
     hubs = [hub] + swap3(hub, "vert", 16)
     recv = lax.all_to_all(send, "vert", 0, 0, tiled=True)
 
+    anywhere = pl.BlockSpec(memory_space=pl.ANY)
     blocked = pl.BlockSpec((per_step, slots * T, T), lambda i, place: (i, 0, 0))
     (agg,) = call(
         forward_kernel,
@@ -353,9 +376,9 @@
         (place,),
         [shape_of(rows, nodes)],
         (features, recv, *hubs, weight),
-        {6: blocked},
+        {2: anywhere, 3: anywhere, 4: anywhere, 5: anywhere, 6: blocked},
         (parts,),
-        [shape_of(sources + 1, rows, T)],
+        [shape_of(sources + 1, rows, T), pltpu.SemaphoreType.DMA((4,))],
         mib=48,
         out_specs=[pl.BlockSpec((rows, span), lambda i, place: (0, i))],
     )

time: 186 us -> 186 us (level)
    unnamed x28 -> x30, local copies, waits for them, and re-layouts: 6.48 us -> 7.51 us
    pallas_call x10 -> x11, Pallas kernels: 34.6 us -> 35.4 us  [call(): pl.pallas_call(kernel, grid_spec=pltpu.PrefetchScalarGridSpec(num_scalar_...]
  transfers between devices with their start and end apart: 25 -> 25, of which waited for: 13 -> 13; matrix products, arithmetic and copies ran while one was open for 2% -> 1% of each run, Pallas kernels for 4% -> 4%
where the time goes in v5:
time: 186 us; the launch traced here: 184 us
  starting transfers between devices  86.4 us (46%)
  waiting for transfers between devices  51.8 us (28%)
  Pallas kernels  35.4 us (19%)
  local copies, waits for them, and re-layouts  8.78 us (5%)
    ppermute x22, waiting for transfers between devices, swap(): return lax.ppermute(x, axis, [(i, i ^ mask) for i in range(size)])  48.1 us
    ppermute x22, starting transfers between devices, swap(): return lax.ppermute(x, axis, [(i, i ^ mask) for i in range(size)])  44.3 us
    pallas_call x11, Pallas kernels, call(): pl.pallas_call(kernel, grid_spec=pltpu.PrefetchScalarGridSpec(num_scalar_...  35.4 us
    all_to_all x2, starting transfers between devices, local(): recv = lax.all_to_all(send, 'vert', 0, 0, tiled=True)  35.3 us
    unnamed x30, local copies, waits for them, and re-layouts  7.51 us
    all_to_all x1, starting transfers between devices, local(): lax.all_to_all(hub, 'vert', 0, 0, axis_index_groups=groups, tiled=True)  6.73 us
  transfers between devices with their start and end apart: 25, of which 13 were waited for; matrix products, arithmetic and copies ran while one was open for 1% of the time, Pallas kernels for 4%

profile of v5, /device:TPU:0, one launch (start us, length us, event | category | flops | bytes accessed | tf_op | source)
XLA Modules:
  0.0 184.0 jit_solution(11663882518723088432)
XLA Ops:
  2.5 6.7 %all-to-all-start = ((bf16[16,64,128]{2,1,0:T(8,128)(2,1)}), bf16[16,64,128]{2,1,0:T(8,128)(2,1)S(1)}, u32[]{:S(2)}, u32[]{:S(2)}) async-start(bf16[16,64,128]{2,1,0:T(8,128)(2,1)} %hub.1), calls=%async_computation | async-start | bytes 524288 | tf_op jit(solution)/shard_map/all_to_all | solution.py:340
  12.0 5.1 %pick.1 = bf16[64,32,128]{2,1,0:T(8,128)(2,1)} custom-call(bf16[64,4096]{1,0:T(8,128)(2,1)S(1)} %copy-done.1, s32[1,4096]{1,0:T(1,128)S(1)} %broadcast_select_fusion.index_ref), custom_call_target="tpu_custom_call" | custom-call | flops 30000001024 | bytes 90000000 | tf_op jit(solution)/shard_map/pick/pallas_call | solution.py:275
  17.1 3.7 %all-to-all-done.h0 = bf16[16,64,128]{2,1,0:T(8,128)(2,1)S(1)} async-done(((bf16[16,64,128]{2,1,0:T(8,128)(2,1)}), bf16[16,64,128]{2,1,0:T(8,128)(2,1)S(1)}, u32[]{:S(2)}, u32[]{:S(2)}) %all-to-all-start) | async-done | bytes 262176 | tf_op jit(solution)/shard_map/all_to_all | solution.py:340
  20.8 7.5 %all-to-all-start.1 = ((bf16[64,32,128]{2,1,0:T(8,128)(2,1)}), bf16[64,32,128]{2,1,0:T(8,128)(2,1)S(1)}, u32[]{:S(2)}, u32[]{:S(2)}) async-start(bf16[64,32,128]{2,1,0:T(8,128)(2,1)} %pick.1), calls=%async_computation.1 | async-start | bytes 1048576 | tf_op jit(solution)/shard_map/all_to_all | solution.py:369
  28.4 3.1 %collective-permute-start.3 = (bf16[16,64,128]{2,1,0:T(8,128)(2,1)S(1)}, bf16[16,64,128]{2,1,0:T(8,128)(2,1)S(1)}, u32[]{:S(2)}, u32[]{:S(2)}) collective-permute-start(bf16[16,64,128]{2,1,0:T(8,128)(2,1)S(1)} %all-to-all-done.h0), channel_id=1, source_target_pairs={{0,192},{4,196},{8,200},{12,204},{16,208},{20,212},{24,216},{28,22... | collective-permute-start | bytes 786440 | tf_op jit(solution)/shard_map/ppermute | solution.py:324
  32.7 15.9 %collective-permute-done.3.h3 = bf16[16,64,128]{2,1,0:T(8,128)(2,1)S(1)} collective-permute-done((bf16[16,64,128]{2,1,0:T(8,128)(2,1)S(1)}, bf16[16,64,128]{2,1,0:T(8,128)(2,1)S(1)}, u32[]{:S(2)}, u32[]{:S(2)}) %collective-permute-start.3) | collective-permute-done | bytes 262176 | tf_op jit(solution)/shard_map/ppermute | solution.py:324
  52.0 8.2 %aggregate.1.agg_ref.refs_9_ = bf16[64,4096]{1,0:T(8,128)(2,1)S(1)} custom-call(s32[256]{0:T(256)S(1)} %reshape.58.place_ref, bf16[64,4096]{1,0:T(8,128)(2,1)S(1)} %copy-done.2, bf16[64,32,128]{2,1,0:T(8,128)(2,1)S(1)} %all-to-all-done.1.recv_ref, bf16[16,64,128]{2,1,0:T(8,128)(2,1)S(1)} %all-to-all-done.h0, bf16[16,64,128]{2,1,0:T(8,128)(2,1)S(1)} %copy-done.9, ...), custom_call_target="tpu_custom_call" | custom-call | tf_op jit(solution)/shard_map/aggregate/pallas_call | solution.py:275
  63.0 4.6 %collective-permute-start.5 = (bf16[64,2048]{1,0:T(8,128)(2,1)S(1)}, bf16[64,2048]{1,0:T(8,128)(2,1)S(1)}, u32[]{:S(2)}, u32[]{:S(2)}) collective-permute-start(bf16[64,2048]{1,0:T(8,128)(2,1)S(1)} %get-tuple-element.39), channel_id=1, source_target_pairs={{0,2},{1,3},{2,0},{3,1},{4,6},{5,7},{6,4},{7,5},{8,10},{9,11},{10,... | collective-permute-start | bytes 786440 | tf_op jit(solution)/shard_map/ppermute | solution.py:324
  69.0 7.6 %collective-permute-done.5.recv_ref = bf16[64,2048]{1,0:T(8,128)(2,1)S(1)} collective-permute-done((bf16[64,2048]{1,0:T(8,128)(2,1)S(1)}, bf16[64,2048]{1,0:T(8,128)(2,1)S(1)}, u32[]{:S(2)}, u32[]{:S(2)}) %collective-permute-start.5) | collective-permute-done | bytes 262176 | tf_op jit(solution)/shard_map/ppermute | solution.py:324
  76.8 4.7 %collective-permute-start.9 = (bf16[64,2048]{1,0:T(8,128)(2,1)S(1)}, bf16[64,2048]{1,0:T(8,128)(2,1)S(1)}, u32[]{:S(2)}, u32[]{:S(2)}) collective-permute-start(bf16[64,2048]{1,0:T(8,128)(2,1)S(1)} %get-tuple-element.40.refs_0_), channel_id=1, source_target_pairs={{0,2},{1,3},{2,0},{3,1},{4,6},{5,7},{6,4},{7,5},{8,10},{9,11},{10,... | collective-permute-start | bytes 786440 | tf_op jit(solution)/shard_map/ppermute | solution.py:324
  82.0 4.7 %collective-permute-start.10 = (bf16[64,2048]{1,0:T(8,128)(2,1)S(1)}, bf16[64,2048]{1,0:T(8,128)(2,1)S(1)}, u32[]{:S(2)}, u32[]{:S(2)}) collective-permute-start(bf16[64,2048]{1,0:T(8,128)(2,1)S(1)} %get-tuple-element.42.refs_1_), channel_id=1, source_target_pairs={{0,2},{1,3},{2,0},{3,1},{4,6},{5,7},{6,4},{7,5},{8,10},{9,11},{10,... | collective-permute-start | bytes 786440 | tf_op jit(solution)/shard_map/ppermute | solution.py:324
  88.1 6.4 %collective-permute-done.10.refs_5_ = bf16[64,2048]{1,0:T(8,128)(2,1)S(1)} collective-permute-done((bf16[64,2048]{1,0:T(8,128)(2,1)S(1)}, bf16[64,2048]{1,0:T(8,128)(2,1)S(1)}, u32[]{:S(2)}, u32[]{:S(2)}) %collective-permute-start.10) | collective-permute-done | bytes 262176 | tf_op jit(solution)/shard_map/ppermute | solution.py:324
  96.2 3.3 %back.1 = (bf16[64,4096]{1,0:T(8,128)(2,1)S(1)}, f32[64,4096]{1,0:T(8,128)S(1)}, f32[64,512]{1,0:T(8,128)S(1)}) custom-call(s32[1]{0:T(128)} %bitcast.me_ref, bf16[64,2048]{1,0:T(8,128)(2,1)S(1)} %get-tuple-element.40.refs_0_, bf16[64,2048]{1,0:T(8,128)(2,1)S(1)} %get-tuple-element.42.refs_1_, bf16[64,2048]{1,0:T(8,128)(2,1)S(1)} %collective-permute-done.7.refs_2_, ...), custom_call_target="tpu_custom_call" | custom-call | tf_op jit(solution)/shard_map/back/pallas_call | solution.py:275
  99.5 10.3 %spread.1 = (f32[64,4096]{1,0:T(8,128)S(1)}, bf16[64,32,128]{2,1,0:T(8,128)(2,1)}, f32[20,64,128]{2,1,0:T(8,128)S(1)}, bf16[20,64,128]{2,1,0:T(8,128)(2,1)}, bf1...) custom-call(s32[256]{0:T(256)S(1)} %reshape.56.place_ref, bf16[64,4096]{1,0:T(8,128)(2,1)S(1)} %get-tuple-element.43.ga_ref, ...), custom_call_target="tpu_custom_call" | custom-call | flops 30000001024 | bytes 90000000 | tf_op jit(solution)/shard_map/spread/pallas_call | solution.py:275
  110.7 5.4 %collective-permute-start.14 = (bf16[20,64,128]{2,1,0:T(8,128)(2,1)S(1)}, bf16[20,64,128]{2,1,0:T(8,128)(2,1)S(1)}, u32[]{:S(2)}, u32[]{:S(2)}) collective-permute-start(bf16[20,64,128]{2,1,0:T(8,128)(2,1)S(1)} %get-tuple-element.52), channel_id=1, source_target_pairs={{0,128},{4,132},{8,136},{12,140},{16,144},{20,148},{24,152},{28,15... | collective-permute-start | bytes 983048 | tf_op jit(solution)/shard_map/ppermute | solution.py:324
  116.0 27.8 %all-to-all-start.2 = ((bf16[64,32,128]{2,1,0:T(8,128)(2,1)}), bf16[64,32,128]{2,1,0:T(8,128)(2,1)S(1)}, u32[]{:S(2)}, u32[]{:S(2)}) async-start(bf16[64,32,128]{2,1,0:T(8,128)(2,1)} %get-tuple-element.46), calls=%async_computation.2 | async-start | bytes 1048576 | tf_op jit(solution)/shard_map/all_to_all | solution.py:442
  147.7 2.7 %collective-permute-start.17 = (bf16[8,64,128]{2,1,0:T(8,128)(2,1)S(1)}, bf16[8,64,128]{2,1,0:T(8,128)(2,1)S(1)}, u32[]{:S(2)}, u32[]{:S(2)}) collective-permute-start(bf16[8,64,128]{2,1,0:T(8,128)(2,1)S(1)} %get-tuple-element.56), channel_id=1, source_target_pairs={{0,32},{4,36},{8,40},{12,44},{16,48},{20,52},{24,56},{28,60},{32,0... | collective-permute-start | bytes 393224 | tf_op jit(solution)/shard_map/ppermute | solution.py:324
  150.8 2.8 %collective-permute-done.16.one_ref = bf16[8,64,128]{2,1,0:T(8,128)(2,1)S(1)} collective-permute-done((bf16[8,64,128]{2,1,0:T(8,128)(2,1)S(1)}, bf16[8,64,128]{2,1,0:T(8,128)(2,1)S(1)}, u32[]{:S(2)}, u32[]{:S(2)}) %collective-permute-start.16) | collective-permute-done | bytes 131104 | tf_op jit(solution)/shard_map/ppermute | solution.py:324
  153.7 4.4 %collective-permute-done.17.two_ref = bf16[8,64,128]{2,1,0:T(8,128)(2,1)S(1)} collective-permute-done((bf16[8,64,128]{2,1,0:T(8,128)(2,1)S(1)}, bf16[8,64,128]{2,1,0:T(8,128)(2,1)S(1)}, u32[]{:S(2)}, u32[]{:S(2)}) %collective-permute-start.17) | collective-permute-done | bytes 131104 | tf_op jit(solution)/shard_map/ppermute | solution.py:324
  158.0 1.7 collective-permute-done.18.three_ref
  159.9 7.0 %collective-permute-start.19 = (bf16[5,64,128]{2,1,0:T(8,128)(2,1)S(1)}, bf16[5,64,128]{2,1,0:T(8,128)(2,1)S(1)}, u32[]{:S(2)}, u32[]{:S(2)}) collective-permute-start(bf16[5,64,128]{2,1,0:T(8,128)(2,1)S(1)} %get-tuple-element.59), channel_id=1, source_target_pairs={{0,4},{4,0},{8,12},{12,8},{16,20},{20,16},{24,28},{28,24},{32,36},... | collective-permute-start | bytes 245768 | tf_op jit(solution)/shard_map/ppermute | solution.py:324
  166.9 5.4 %collective-permute-start.20 = (bf16[5,64,128]{2,1,0:T(8,128)(2,1)S(1)}, bf16[5,64,128]{2,1,0:T(8,128)(2,1)S(1)}, u32[]{:S(2)}, u32[]{:S(2)}) collective-permute-start(bf16[5,64,128]{2,1,0:T(8,128)(2,1)S(1)} %get-tuple-element.60), channel_id=1, source_target_pairs={{0,8},{4,12},{8,0},{12,4},{16,24},{20,28},{24,16},{28,20},{32,40},... | collective-permute-start | bytes 245768 | tf_op jit(solution)/shard_map/ppermute | solution.py:324
  174.7 3.9 %collective-permute-done.21.refs_3_ = bf16[5,64,128]{2,1,0:T(8,128)(2,1)S(1)} collective-permute-done((bf16[5,64,128]{2,1,0:T(8,128)(2,1)S(1)}, bf16[5,64,128]{2,1,0:T(8,128)(2,1)S(1)}, u32[]{:S(2)}, u32[]{:S(2)}) %collective-permute-start.21) | collective-permute-done | bytes 81952 | tf_op jit(solution)/shard_map/ppermute | solution.py:324
  178.6 5.4 %finish.1 = (f32[64,4096]{1,0:T(8,128)}, bf16[64,4096]{1,0:T(8,128)(2,1)}, f32[64,256]{1,0:T(8,128)}, f32[64,256]{1,0:T(8,128)}) custom-call(bf16[64,32,128]{2,1,0:T(8,128)(2,1)S(1)} %all-to-all-done.2.recv_ref, s32[1,4096]{1,0:T(1,128)S(1)} %broadcast_select_fusion.index_ref, f32[64,4096]{1,0:T(8,128)S(1)} %get-tuple-element.47.own_ref, ...), custom_call_target="tpu_custom_call" | custom-call | tf_op jit(solution)/shard_map/finish/pallas_call | solution.py:275
  (76 shorter events, 24.7 us)
Async XLA Ops:
  0.6 20.2 %collective-permute-start = (bf16[64,4096]{1,0:T(8,128)(2,1)}, bf16[64,4096]{1,0:T(8,128)(2,1)S(1)}, u32[]{:S(2)}, u32[]{:S(2)}) collective-permute-start(bf16[64,4096]{1,0:T(8,128)(2,1)} %refs_8_.1), channel_id=1, source_target_pairs={{0,1},{1,0},{2,3},{3,2},{4,5},{5,4},{6,7},{7,6},{8,9},{9,8},{10,11... | collective-permute-start | bytes 1572872 | tf_op jit(solution)/shard_map/ppermute | solution.py:324
  2.5 18.3 %all-to-all-start = ((bf16[16,64,128]{2,1,0:T(8,128)(2,1)}), bf16[16,64,128]{2,1,0:T(8,128)(2,1)S(1)}, u32[]{:S(2)}, u32[]{:S(2)}) async-start(bf16[16,64,128]{2,1,0:T(8,128)(2,1)} %hub.1), calls=%async_computation | async-start | bytes 524288 | tf_op jit(solution)/shard_map/all_to_all | solution.py:340
  20.8 29.3 %all-to-all-start.1 = ((bf16[64,32,128]{2,1,0:T(8,128)(2,1)}), bf16[64,32,128]{2,1,0:T(8,128)(2,1)S(1)}, u32[]{:S(2)}, u32[]{:S(2)}) async-start(bf16[64,32,128]{2,1,0:T(8,128)(2,1)} %pick.1), calls=%async_computation.1 | async-start | bytes 1048576 | tf_op jit(solution)/shard_map/all_to_all | solution.py:369
  28.4 20.3 %collective-permute-start.3 = (bf16[16,64,128]{2,1,0:T(8,128)(2,1)S(1)}, bf16[16,64,128]{2,1,0:T(8,128)(2,1)S(1)}, u32[]{:S(2)}, u32[]{:S(2)}) collective-permute-start(bf16[16,64,128]{2,1,0:T(8,128)(2,1)S(1)} %all-to-all-done.h0), channel_id=1, source_target_pairs={{0,192},{4,196},{8,200},{12,204},{16,208},{20,212},{24,216},{28,22... | collective-permute-start | bytes 786440 | tf_op jit(solution)/shard_map/ppermute | solution.py:324
  31.4 17.2 %collective-permute-start.2 = (bf16[16,64,128]{2,1,0:T(8,128)(2,1)S(1)}, bf16[16,64,128]{2,1,0:T(8,128)(2,1)S(1)}, u32[]{:S(2)}, u32[]{:S(2)}) collective-permute-start(bf16[16,64,128]{2,1,0:T(8,128)(2,1)S(1)} %all-to-all-done.h0), channel_id=1, source_target_pairs={{0,128},{4,132},{8,136},{12,140},{16,144},{20,148},{24,152},{28,15... | collective-permute-start | bytes 786440 | tf_op jit(solution)/shard_map/ppermute | solution.py:324
  32.1 17.3 %collective-permute-start.1 = (bf16[16,64,128]{2,1,0:T(8,128)(2,1)S(1)}, bf16[16,64,128]{2,1,0:T(8,128)(2,1)S(1)}, u32[]{:S(2)}, u32[]{:S(2)}) collective-permute-start(bf16[16,64,128]{2,1,0:T(8,128)(2,1)S(1)} %all-to-all-done.h0), channel_id=1, source_target_pairs={{0,64},{4,68},{8,72},{12,76},{16,80},{20,84},{24,88},{28,92},{32,9... | collective-permute-start | bytes 786440 | tf_op jit(solution)/shard_map/ppermute | solution.py:324
  60.2 2.0 %collective-permute-start.4 = (bf16[64,4096]{1,0:T(8,128)(2,1)S(1)}, bf16[64,4096]{1,0:T(8,128)(2,1)S(1)}, u32[]{:S(2)}, u32[]{:S(2)}) collective-permute-start(bf16[64,4096]{1,0:T(8,128)(2,1)S(1)} %aggregate.1.agg_ref.refs_9_), channel_id=1, source_target_pairs={{0,1},{1,0},{2,3},{3,2},{4,5},{5,4},{6,7},{7,6},{8,9},{9,8},{10,11... | collective-permute-start | bytes 1572872 | tf_op jit(solution)/shard_map/ppermute | solution.py:324
  63.0 13.6 %collective-permute-start.5 = (bf16[64,2048]{1,0:T(8,128)(2,1)S(1)}, bf16[64,2048]{1,0:T(8,128)(2,1)S(1)}, u32[]{:S(2)}, u32[]{:S(2)}) collective-permute-start(bf16[64,2048]{1,0:T(8,128)(2,1)S(1)} %get-tuple-element.39), channel_id=1, source_target_pairs={{0,2},{1,3},{2,0},{3,1},{4,6},{5,7},{6,4},{7,5},{8,10},{9,11},{10,... | collective-permute-start | bytes 786440 | tf_op jit(solution)/shard_map/ppermute | solution.py:324
  67.6 14.2 %collective-permute-start.6 = (bf16[64,2048]{1,0:T(8,128)(2,1)S(1)}, bf16[64,2048]{1,0:T(8,128)(2,1)S(1)}, u32[]{:S(2)}, u32[]{:S(2)}) collective-permute-start(bf16[64,2048]{1,0:T(8,128)(2,1)S(1)} %get-tuple-element.41), channel_id=1, source_target_pairs={{0,2},{1,3},{2,0},{3,1},{4,6},{5,7},{6,4},{7,5},{8,10},{9,11},{10,... | collective-permute-start | bytes 786440 | tf_op jit(solution)/shard_map/ppermute | solution.py:324
  76.8 11.3 %collective-permute-start.9 = (bf16[64,2048]{1,0:T(8,128)(2,1)S(1)}, bf16[64,2048]{1,0:T(8,128)(2,1)S(1)}, u32[]{:S(2)}, u32[]{:S(2)}) collective-permute-start(bf16[64,2048]{1,0:T(8,128)(2,1)S(1)} %get-tuple-element.40.refs_0_), channel_id=1, source_target_pairs={{0,2},{1,3},{2,0},{3,1},{4,6},{5,7},{6,4},{7,5},{8,10},{9,11},{10,... | collective-permute-start | bytes 786440 | tf_op jit(solution)/shard_map/ppermute | solution.py:324
  82.0 12.5 %collective-permute-start.10 = (bf16[64,2048]{1,0:T(8,128)(2,1)S(1)}, bf16[64,2048]{1,0:T(8,128)(2,1)S(1)}, u32[]{:S(2)}, u32[]{:S(2)}) collective-permute-start(bf16[64,2048]{1,0:T(8,128)(2,1)S(1)} %get-tuple-element.42.refs_1_), channel_id=1, source_target_pairs={{0,2},{1,3},{2,0},{3,1},{4,6},{5,7},{6,4},{7,5},{8,10},{9,11},{10,... | collective-permute-start | bytes 786440 | tf_op jit(solution)/shard_map/ppermute | solution.py:324
  86.8 7.9 %collective-permute-start.7 = (bf16[64,2048]{1,0:T(8,128)(2,1)S(1)}, bf16[64,2048]{1,0:T(8,128)(2,1)S(1)}, u32[]{:S(2)}, u32[]{:S(2)}) collective-permute-start(bf16[64,2048]{1,0:T(8,128)(2,1)S(1)} %get-tuple-element.40.refs_0_), channel_id=1, source_target_pairs={{0,1},{1,0},{2,3},{3,2},{4,5},{5,4},{6,7},{7,6},{8,9},{9,8},{10,11... | collective-permute-start | bytes 786440 | tf_op jit(solution)/shard_map/ppermute | solution.py:324
  86.8 8.0 %collective-permute-start.8 = (bf16[64,2048]{1,0:T(8,128)(2,1)S(1)}, bf16[64,2048]{1,0:T(8,128)(2,1)S(1)}, u32[]{:S(2)}, u32[]{:S(2)}) collective-permute-start(bf16[64,2048]{1,0:T(8,128)(2,1)S(1)} %get-tuple-element.42.refs_1_), channel_id=1, source_target_pairs={{0,1},{1,0},{2,3},{3,2},{4,5},{5,4},{6,7},{7,6},{8,9},{9,8},{10,11... | collective-permute-start | bytes 786440 | tf_op jit(solution)/shard_map/ppermute | solution.py:324
  88.1 6.6 %collective-permute-start.11 = (bf16[64,2048]{1,0:T(8,128)(2,1)S(1)}, bf16[64,2048]{1,0:T(8,128)(2,1)}, u32[]{:S(2)}, u32[]{:S(2)}) collective-permute-start(bf16[64,2048]{1,0:T(8,128)(2,1)S(1)} %collective-permute-done.9.refs_4_), channel_id=1, source_target_pairs={{0,1},{1,0},{2,3},{3,2},{4,5},{5,4},{6,7},{7,6},{8,9},{9,8},{10,11... | collective-permute-start | bytes 786440 | tf_op jit(solution)/shard_map/ppermute | solution.py:324
  110.7 33.1 %collective-permute-start.13 = (bf16[20,64,128]{2,1,0:T(8,128)(2,1)}, bf16[20,64,128]{2,1,0:T(8,128)(2,1)S(1)}, u32[]{:S(2)}, u32[]{:S(2)}) collective-permute-start(bf16[20,64,128]{2,1,0:T(8,128)(2,1)} %get-tuple-element.51), channel_id=1, source_target_pairs={{0,64},{4,68},{8,72},{12,76},{16,80},{20,84},{24,88},{28,92},{32,9... | collective-permute-start | bytes 983048 | tf_op jit(solution)/shard_map/ppermute | solution.py:324
  110.7 33.2 %collective-permute-start.14 = (bf16[20,64,128]{2,1,0:T(8,128)(2,1)S(1)}, bf16[20,64,128]{2,1,0:T(8,128)(2,1)S(1)}, u32[]{:S(2)}, u32[]{:S(2)}) collective-permute-start(bf16[20,64,128]{2,1,0:T(8,128)(2,1)S(1)} %get-tuple-element.52), channel_id=1, source_target_pairs={{0,128},{4,132},{8,136},{12,140},{16,144},{20,148},{24,152},{28,15... | collective-permute-start | bytes 983048 | tf_op jit(solution)/shard_map/ppermute | solution.py:324
  116.0 27.8 %collective-permute-start.15 = (bf16[20,64,128]{2,1,0:T(8,128)(2,1)S(1)}, bf16[20,64,128]{2,1,0:T(8,128)(2,1)}, u32[]{:S(2)}, u32[]{:S(2)}) collective-permute-start(bf16[20,64,128]{2,1,0:T(8,128)(2,1)S(1)} %get-tuple-element.53), channel_id=1, source_target_pairs={{0,192},{4,196},{8,200},{12,204},{16,208},{20,212},{24,216},{28,22... | collective-permute-start | bytes 983048 | tf_op jit(solution)/shard_map/ppermute | solution.py:324
  116.0 62.6 %all-to-all-start.2 = ((bf16[64,32,128]{2,1,0:T(8,128)(2,1)}), bf16[64,32,128]{2,1,0:T(8,128)(2,1)S(1)}, u32[]{:S(2)}, u32[]{:S(2)}) async-start(bf16[64,32,128]{2,1,0:T(8,128)(2,1)} %get-tuple-element.46), calls=%async_computation.2 | async-start | bytes 1048576 | tf_op jit(solution)/shard_map/all_to_all | solution.py:442
  146.0 7.6 %collective-permute-start.16 = (bf16[8,64,128]{2,1,0:T(8,128)(2,1)S(1)}, bf16[8,64,128]{2,1,0:T(8,128)(2,1)S(1)}, u32[]{:S(2)}, u32[]{:S(2)}) collective-permute-start(bf16[8,64,128]{2,1,0:T(8,128)(2,1)S(1)} %get-tuple-element.55), channel_id=1, source_target_pairs={{0,16},{4,20},{8,24},{12,28},{16,0},{20,4},{24,8},{28,12},{32,48},... | collective-permute-start | bytes 393224 | tf_op jit(solution)/shard_map/ppermute | solution.py:324
  147.7 10.3 %collective-permute-start.17 = (bf16[8,64,128]{2,1,0:T(8,128)(2,1)S(1)}, bf16[8,64,128]{2,1,0:T(8,128)(2,1)S(1)}, u32[]{:S(2)}, u32[]{:S(2)}) collective-permute-start(bf16[8,64,128]{2,1,0:T(8,128)(2,1)S(1)} %get-tuple-element.56), channel_id=1, source_target_pairs={{0,32},{4,36},{8,40},{12,44},{16,48},{20,52},{24,56},{28,60},{32,0... | collective-permute-start | bytes 393224 | tf_op jit(solution)/shard_map/ppermute | solution.py:324
  150.4 9.4 %collective-permute-start.18 = (bf16[8,64,128]{2,1,0:T(8,128)(2,1)S(1)}, bf16[8,64,128]{2,1,0:T(8,128)(2,1)S(1)}, u32[]{:S(2)}, u32[]{:S(2)}) collective-permute-start(bf16[8,64,128]{2,1,0:T(8,128)(2,1)S(1)} %get-tuple-element.57), channel_id=1, source_target_pairs={{0,48},{4,52},{8,56},{12,60},{16,32},{20,36},{24,40},{28,44},{32,1... | collective-permute-start | bytes 393224 | tf_op jit(solution)/shard_map/ppermute | solution.py:324
  159.9 13.8 %collective-permute-start.19 = (bf16[5,64,128]{2,1,0:T(8,128)(2,1)S(1)}, bf16[5,64,128]{2,1,0:T(8,128)(2,1)S(1)}, u32[]{:S(2)}, u32[]{:S(2)}) collective-permute-start(bf16[5,64,128]{2,1,0:T(8,128)(2,1)S(1)} %get-tuple-element.59), channel_id=1, source_target_pairs={{0,4},{4,0},{8,12},{12,8},{16,20},{20,16},{24,28},{28,24},{32,36},... | collective-permute-start | bytes 245768 | tf_op jit(solution)/shard_map/ppermute | solution.py:324
  166.9 7.8 %collective-permute-start.20 = (bf16[5,64,128]{2,1,0:T(8,128)(2,1)S(1)}, bf16[5,64,128]{2,1,0:T(8,128)(2,1)S(1)}, u32[]{:S(2)}, u32[]{:S(2)}) collective-permute-start(bf16[5,64,128]{2,1,0:T(8,128)(2,1)S(1)} %get-tuple-element.60), channel_id=1, source_target_pairs={{0,8},{4,12},{8,0},{12,4},{16,24},{20,28},{24,16},{28,20},{32,40},... | collective-permute-start | bytes 245768 | tf_op jit(solution)/shard_map/ppermute | solution.py:324
  172.3 6.3 %collective-permute-start.21 = (bf16[5,64,128]{2,1,0:T(8,128)(2,1)S(1)}, bf16[5,64,128]{2,1,0:T(8,128)(2,1)S(1)}, u32[]{:S(2)}, u32[]{:S(2)}) collective-permute-start(bf16[5,64,128]{2,1,0:T(8,128)(2,1)S(1)} %get-tuple-element.61), channel_id=1, source_target_pairs={{0,12},{4,8},{8,4},{12,0},{16,28},{20,24},{24,20},{28,16},{32,44},... | collective-permute-start | bytes 245768 | tf_op jit(solution)/shard_map/ppermute | solution.py:324
  (15 other events, 233.9 us)
